TPU v7x, 256 devices: a whole 4x4x8 slice. The times are simulated.
256 devices in a mesh: replica: 2 (over core), dp: 4 (over y), cent: 32 (over x, z).
Axes of the slice: x: 4, y: 4, z: 8, core: 2. Of those that a mesh axis runs over, the one named last changes fastest.
Arguments:
- vectors: float32 [2048, 1024], P(('replica', 'dp')), may hold values from -6 to 6
- centroids: float32 [262144, 1024], P(('dp', 'cent')), may hold values from -6 to 6
Outputs:
- new_centroids: float32 [262144, 1024], P(('dp', 'cent'), 'replica')
All inputs are finite; a program needn't handle non-finite values.
Results may differ from a plain program's by a relative error of at most 0.0022.
Values may be sent and summed in bfloat16 or wider, within the bound.
No kernel may reach another device: no remote copies, remote signals or barrier semaphores. Data moves between devices by JAX's collectives and lax.ppermute only.
A program may use at most 128 MiB of HBM per device.

v0:
```python
import jax
import jax.numpy as jnp
from jax import lax
from jax.sharding import PartitionSpec as P

VECTOR_WIDTH = 1024
ITERS = 3


SOFTMAX_HEAT = 0.05


def unit_rows(values):
    scale = lax.rsqrt(jnp.mean(values * values, axis=-1, keepdims=True) + 1e-06)
    return (values * scale).astype(jnp.bfloat16)


def balanced_weights(affinity_kernel, lists_total):
    members, slab_size, local_lists = affinity_kernel.shape
    row_scale = jnp.full((members, slab_size), 1.0 / slab_size, jnp.float32)
    for sweep in range(ITERS):
        column_totals = jnp.einsum(
            "sr,srk->sk", row_scale, affinity_kernel, precision=lax.Precision.HIGHEST
        )
        col_scale = 1.0 / lists_total / column_totals
        local_mass = jnp.einsum(
            "srk,sk->sr", affinity_kernel, col_scale, precision=lax.Precision.HIGHEST
        )
        row_totals = lax.psum(local_mass, ("dp", "cent"))
        row_scale = 1.0 / slab_size / row_totals
    scaled = (
        slab_size * lists_total * row_scale[:, :, None] * affinity_kernel * col_scale[:, None, :]
    )
    return scaled.astype(jnp.bfloat16)


def score_kernel(slab_vectors, unit_centroids):
    match_scores = lax.dot_general(
        slab_vectors, unit_centroids, (((1,), (1,)), ((), ())), preferred_element_type=jnp.float32
    )
    return jnp.exp(match_scores / VECTOR_WIDTH / SOFTMAX_HEAT)


def body(vectors, centroids):
    local_unit_rows = unit_rows(vectors)
    unit_centroids = unit_rows(centroids)
    local_lists = unit_centroids.shape[0]
    lists_total = local_lists * lax.axis_size("dp") * lax.axis_size("cent")
    slab_vectors = lax.all_gather(local_unit_rows, "dp", axis=0, tiled=True)
    affinity_kernel = score_kernel(slab_vectors, unit_centroids)[None]
    weights = balanced_weights(affinity_kernel, lists_total)[0]
    partial_numer = lax.dot_general(
        weights, slab_vectors, (((0,), (0,)), ((), ())), preferred_element_type=jnp.float32
    )
    numerators = lax.psum_scatter(partial_numer, "replica", scatter_dimension=1, tiled=True)
    squares = lax.psum(jnp.sum(numerators * numerators, axis=1), "replica")
    return numerators * lax.rsqrt(squares / VECTOR_WIDTH + 1e-06)[:, None]


def solution(mesh):
    placed = (P(("replica", "dp"), None), P(("dp", "cent"), None))
    return jax.shard_map(
        body, mesh=mesh, in_specs=placed, out_specs=P(("dp", "cent"), "replica"), check_vma=False
    )
```

profile of v0, /device:TPU:1, one launch (start us, length us, event | category | flops | bytes accessed | tf_op | source)
XLA Modules:
  0.0 1172.0 jit_solution(10423534511231442074)
XLA Ops:
  6.5 1.4 multiply_reduce_fusion.2
  7.9 2.1 multiply_convert_fusion.4
  10.1 0.0 all-gather.2.cloned.1.call-update
  10.1 0.0 reduce-scatter.2.cloned.1.call-start
  10.1 4.0 multiply_reduce_fusion
  14.2 33.3 %all-gather.2.cloned.1.call-done = bf16[1024,1024]{1,0:T(8,128)(2,1)} async-done(((bf16[256,1024]{1,0:T(8,128)(2,1)}), bf16[1024,1024]{1,0:T(8,128)(2,1)}) %all-gather.2.cloned.1.call-update) | async-done | bytes 2097168 | tf_op jit(solution)/shard_map/all_gather | solution.py:49
  47.5 7.9 multiply_exponential_fusion
  55.4 4.0 fusion.10
  59.4 0.0 copy-done
  59.4 7.2 fusion.17
  66.6 292.6 %psum.28 = f32[1,1024]{1,0:T(1,128)S(1)} all-reduce(f32[1,1024]{1,0:T(1,128)S(1)} %fusion.17), channel_id=1, replica_groups=mesh['replica'=2,'dp'=4,'cent'=32] {'dp','cent'}, use_global_device_ids=true, to_apply=%region_2.0 | all-reduce | flops 1024 | bytes 8192 | tf_op jit(solution)/shard_map/psum | solution.py:29
  359.2 7.3 fusion.6
  366.5 0.0 copy-done.1
  366.5 7.2 fusion.18
  373.7 287.3 %psum.29 = f32[1,1024]{1,0:T(1,128)S(1)} all-reduce(f32[1,1024]{1,0:T(1,128)S(1)} %fusion.18), channel_id=1, replica_groups=mesh['replica'=2,'dp'=4,'cent'=32] {'dp','cent'}, use_global_device_ids=true, to_apply=%region_3.0 | all-reduce | flops 1024 | bytes 8192 | tf_op jit(solution)/shard_map/psum | solution.py:29
  661.0 6.7 fusion.4
  667.7 9.4 fusion.19
  677.1 288.5 %psum.30 = f32[1,1024]{1,0:T(1,128)S(1)} all-reduce(f32[1,1024]{1,0:T(1,128)S(1)} %fusion.19), channel_id=1, replica_groups=mesh['replica'=2,'dp'=4,'cent'=32] {'dp','cent'}, use_global_device_ids=true, to_apply=%region_4.0 | all-reduce | flops 1024 | bytes 8192 | tf_op jit(solution)/shard_map/psum | solution.py:29
  965.6 10.5 fusion
  976.1 0.0 reduce-scatter.2.cloned.1.call-update
  976.1 179.5 %reduce-scatter.2.cloned.1.call-done = f32[2048,512]{1,0:T(8,128)} async-done(((f32[2048,1024]{1,0:T(8,128)}), f32[2048,512]{1,0:T(8,128)}) %reduce-scatter.2.cloned.1.call-update) | async-done | bytes 4194320 | tf_op jit(solution)/shard_map/reduce_scatter | solution.py:55
  1155.5 2.5 multiply_reduce_fusion.1
  1158.1 2.5 psum.31
  1160.6 4.5 broadcast_multiply_fusion
  (12 shorter events, 0.1 us)
Async XLA Ops:
  6.5 40.9 %all-gather.2.cloned.1.call-start = ((), (), s32[]{:S(2)}) async-start(), calls=%async_computation.1 | async-start | bytes 2621440 | tf_op jit(solution)/shard_map/all_gather | solution.py:49
  10.1 1145.4 %reduce-scatter.2.cloned.1.call-start = ((), (), s32[]{:S(2)}) async-start(), calls=%async_computation.2 | async-start | bytes 12582912 | tf_op jit(solution)/shard_map/reduce_scatter | solution.py:55
  55.4 4.0 copy-start
  359.2 7.3 copy-start.1
  661.0 304.6 %copy-start.2 = (bf16[1024,1024]{1,0:T(8,128)(2,1)S(1)}, bf16[1024,1024]{1,0:T(8,128)(2,1)}, u32[]{:S(2)}) copy-start(bf16[1024,1024]{1,0:T(8,128)(2,1)} %all-gather.2.cloned.1.call-done) | copy-start | bytes 6291460
Sparse Core Ops, SparseCore 0:
  10.2 37.2 all-gather.1
  976.2 179.2 reduce-scatter.1
where the time goes:
time: 1170 us
  blocking collectives  871 us (74%)
  waiting for transfers between devices  213 us (18%)
  matrix products  60.1 us (5%)
  other arithmetic  14.7 us (1%)
  between operations  13.5 us (1%)
    psum x3, blocking collectives, balanced_weights(): row_totals = lax.psum(local_mass, ('dp', 'cent'))  868 us
    reduce_scatter x1, waiting for transfers between devices, body(): lax.psum_scatter(partial_numer, 'replica', scatter_dimension=1, tiled=True)  179 us
    all_gather x1, waiting for transfers between devices, body(): slab_vectors = lax.all_gather(local_unit_rows, 'dp', axis=0, tiled=True)  33.3 us
    dot_general x3, matrix products, balanced_weights(): jnp.einsum('srk,sk->sr', affinity_kernel, col_scale, precision=lax.Precis...  23.8 us
  transfers between devices with their start and end apart: 2, of which 2 were waited for; matrix products, arithmetic and copies ran while one was open for 0% of the time, Pallas kernels for 0%

commit v1 on v0

--- a/solution.py
+++ b/solution.py
@@ -1,7 +1,7 @@
 import jax
 import jax.numpy as jnp
 from jax import lax
-from jax.sharding import PartitionSpec as P
+from jax.sharding import Mesh, PartitionSpec as P
 
 VECTOR_WIDTH = 1024
 ITERS = 3
@@ -26,12 +26,23 @@
         local_mass = jnp.einsum(
             "srk,sk->sr", affinity_kernel, col_scale, precision=lax.Precision.HIGHEST
         )
-        row_totals = lax.psum(local_mass, ("dp", "cent"))
+        row_totals = sum_over_lists(local_mass)
         row_scale = 1.0 / slab_size / row_totals
     scaled = (
         slab_size * lists_total * row_scale[:, :, None] * affinity_kernel * col_scale[:, None, :]
     )
     return scaled.astype(jnp.bfloat16)
+
+
+def sum_over(partial, axes, size):
+    copies = jnp.broadcast_to(partial[None], (size,) + partial.shape)
+    return jnp.sum(lax.all_to_all(copies, axes, 0, 0, tiled=True), axis=0)
+
+
+def sum_over_lists(local_mass):
+    partial = local_mass.reshape(8, -1)
+    partial = sum_over(partial, ("dp", "cx"), lax.axis_size("dp") * lax.axis_size("cx"))
+    return sum_over(partial, "cz", lax.axis_size("cz")).reshape(local_mass.shape)
 
 
 def score_kernel(slab_vectors, unit_centroids):
@@ -45,7 +56,7 @@
     local_unit_rows = unit_rows(vectors)
     unit_centroids = unit_rows(centroids)
     local_lists = unit_centroids.shape[0]
-    lists_total = local_lists * lax.axis_size("dp") * lax.axis_size("cent")
+    lists_total = local_lists * lax.axis_size("dp") * lax.axis_size("cx") * lax.axis_size("cz")
     slab_vectors = lax.all_gather(local_unit_rows, "dp", axis=0, tiled=True)
     affinity_kernel = score_kernel(slab_vectors, unit_centroids)[None]
     weights = balanced_weights(affinity_kernel, lists_total)[0]
@@ -58,7 +69,12 @@
 
 
 def solution(mesh):
-    placed = (P(("replica", "dp"), None), P(("dp", "cent"), None))
+    cent = mesh.shape["cent"]
+    split = Mesh(
+        mesh.devices.reshape(mesh.shape["replica"], mesh.shape["dp"], 4, cent // 4),
+        ("replica", "dp", "cx", "cz"),
+    )
+    placed = (P(("replica", "dp"), None), P(("dp", "cx", "cz"), None))
     return jax.shard_map(
-        body, mesh=mesh, in_specs=placed, out_specs=P(("dp", "cent"), "replica"), check_vma=False
+        body, mesh=split, in_specs=placed, out_specs=P(("dp", "cx", "cz"), "replica"), check_vma=False
     )

time: 1170 us -> 210 us (0.18)
  blocking collectives: 871 us -> 65 us
  waiting for transfers between devices: 213 us -> 56.6 us
    psum x3 -> x0, blocking collectives: 868 us -> none  [balanced_weights(): row_totals = lax.psum(local_mass, ('dp', 'cent'))]
    reduce_scatter x1, waiting for transfers between devices: 179 us -> 23.3 us  [body(): lax.psum_scatter(partial_numer, 'replica', scatter_dimension=1, tiled=True)]
    all_to_all x0 -> x6, blocking collectives: none -> 62.5 us  [sum_over(): return jnp.sum(lax.all_to_all(copies, axes, 0, 0, tiled=True), axis=0)]
  transfers between devices with their start and end apart: 2 -> 2, of which waited for: 2 -> 2; matrix products, arithmetic and copies ran while one was open for 0% -> 2% of each run, Pallas kernels for 0% -> 0%
where the time goes in v1:
time: 210 us
  blocking collectives  65 us (31%)
  matrix products  59.9 us (29%)
  waiting for transfers between devices  56.6 us (27%)
  other arithmetic  14.8 us (7%)
  between operations  13.5 us (6%)
    all_to_all x6, blocking collectives, sum_over(): return jnp.sum(lax.all_to_all(copies, axes, 0, 0, tiled=True), axis=0)  62.5 us
    all_gather x1, waiting for transfers between devices, body(): slab_vectors = lax.all_gather(local_unit_rows, 'dp', axis=0, tiled=True)  33.3 us
    dot_general x3, matrix products, balanced_weights(): jnp.einsum('srk,sk->sr', affinity_kernel, col_scale, precision=lax.Precis...  23.8 us
    reduce_scatter x1, waiting for transfers between devices, body(): lax.psum_scatter(partial_numer, 'replica', scatter_dimension=1, tiled=True)  23.3 us
    dot_general x3, matrix products, balanced_weights(): jnp.einsum('sr,srk->sk', row_scale, affinity_kernel, precision=lax.Precis...  17.6 us
    dot_general x1, matrix products, body(): lax.dot_general(weights, slab_vectors, (((0,), (0,)), ((), ())), preferre...  10.6 us
    dot_general x1, matrix products, score_kernel(): lax.dot_general(slab_vectors, unit_centroids, (((1,), (1,)), ((), ())), p...  7.9 us
    reduce_sum x2, other arithmetic, unit_rows(): scale = lax.rsqrt(jnp.mean(values * values, axis=-1, keepdims=True) + 1e-06)  5.37 us
  transfers between devices with their start and end apart: 2, of which 2 were waited for; matrix products, arithmetic and copies ran while one was open for 2% of the time, Pallas kernels for 0%

profile of v1, /device:TPU:1, one launch (start us, length us, event | category | flops | bytes accessed | tf_op | source)
XLA Modules:
  0.0 209.9 jit_solution(7023485402071170484)
XLA Ops:
  6.5 1.4 multiply_reduce_fusion.2
  7.9 2.1 %multiply_convert_fusion.4 = bf16[256,1024]{1,0:T(8,128)(2,1)} fusion(f32[256,1024]{1,0:T(8,128)} %param.2, f32[256]{0:T(256)S(1)} %add_rsqrt_fusion.2), kind=kLoop, calls=%fused_computation.10 | loop fusion | flops 524288 | bytes 1573888 | tf_op jit(solution)/shard_map/convert_element_type | solution.py:15
  10.1 0.0 all-gather.2.cloned.1.call-update
  10.1 0.0 reduce-scatter.2.cloned.1.call-start
  10.1 4.0 %multiply_reduce_fusion = f32[2048]{0:T(1024)S(1)} fusion(f32[2048,1024]{1,0:T(8,128)} %param.3), kind=kLoop, calls=%fused_computation.3 | loop fusion | flops 4192256 | bytes 8396800 | tf_op jit(solution)/shard_map/reduce_sum | solution.py:14
  14.2 33.3 %all-gather.2.cloned.1.call-done = bf16[1024,1024]{1,0:T(8,128)(2,1)} async-done(((bf16[256,1024]{1,0:T(8,128)(2,1)}), bf16[1024,1024]{1,0:T(8,128)(2,1)}) %all-gather.2.cloned.1.call-update) | async-done | bytes 2097168 | tf_op jit(solution)/shard_map/all_gather | solution.py:60
  47.5 7.9 %multiply_exponential_fusion = f32[1024,2048]{1,0:T(8,128)S(1)} fusion(bf16[1024,1024]{1,0:T(8,128)(2,1)} %all-gather.2.cloned.1.call-done, f32[2048,1024]{1,0:T(8,128)} %param.3, f32[2048]{0:T(1024)S(1)} %add_rsqrt_fusion.1), kind=kOutput, calls=%fused_computation.1 | convolution fusion | flops 4301258752 | bytes 18882560 | tf_op jit(solution)/shard_map/dot_general | solution.py:49
  55.4 4.0 %fusion.4 = f32[1,2048]{1,0:T(1,128)S(1)} fusion(f32[1024,2048]{1,0:T(8,128)S(1)} %multiply_exponential_fusion), kind=kOutput, calls=%fused_computation.18 | convolution fusion | flops 25165824 | bytes 8396800 | tf_op jit(solution)/shard_map/sr,srk->sk/dot_general | solution.py:22
  59.4 7.2 %fusion.7 = f32[1,8,128]{2,0,1:T(1,128)S(1)} fusion(f32[8,128,2048]{2,1,0:T(8,128)S(1)} %bitcast.34, f32[2048,1,1]{0,1,2:T(1,128)S(1)} %bitcast.38), kind=kOutput, calls=%fused_computation.24 | convolution fusion | flops 25165824 | bytes 8400896 | tf_op jit(solution)/shard_map/srk,sk->sr/dot_general | solution.py:26
  66.6 11.6 %all_to_all.30 = f32[16,8,128]{2,1,0:T(8,128)S(1)} all-to-all(f32[16,8,128]{2,1,0:T(8,128)S(1)} %broadcast_in_dim.12), channel_id=1, replica_groups=mesh['replica'=2,'dp'=4,'cx'=4,'cz'=8] {'dp','cx'}, dimensions={0} | all-to-all | bytes 131072 | tf_op jit(solution)/shard_map/all_to_all | solution.py:39
  78.2 13.4 %all_to_all.31 = f32[8,8,128]{2,1,0:T(8,128)S(1)} all-to-all(f32[8,8,128]{2,1,0:T(8,128)S(1)} %broadcast_in_dim.13), channel_id=1, replica_groups=mesh['replica'=2,'dp'=4,'cx'=4,'cz'=8] {'cz'}, dimensions={0} | all-to-all | bytes 65536 | tf_op jit(solution)/shard_map/all_to_all | solution.py:39
  91.7 7.1 %fusion.8 = f32[1,2048]{1,0:T(1,128)S(1)} fusion(f32[1024,1]{0,1:T(1,128)S(1)} %bitcast.46, f32[1024,2048]{1,0:T(8,128)} %copy-done), kind=kOutput, calls=%fused_computation.25 | convolution fusion | flops 25165824 | bytes 8400896 | tf_op jit(solution)/shard_map/sr,srk->sk/dot_general | solution.py:22
  98.8 7.2 %fusion.9 = f32[1,8,128]{2,0,1:T(1,128)S(1)} fusion(f32[8,128,2048]{2,1,0:T(8,128)S(1)} %bitcast.36, f32[2048,1,1]{0,1,2:T(1,128)S(1)} %bitcast.40), kind=kOutput, calls=%fused_computation.26 | convolution fusion | flops 25165824 | bytes 8400896 | tf_op jit(solution)/shard_map/srk,sk->sr/dot_general | solution.py:26
  106.0 9.7 %all_to_all.32 = f32[16,8,128]{2,1,0:T(8,128)S(1)} all-to-all(f32[16,8,128]{2,1,0:T(8,128)S(1)} %broadcast_in_dim.14), channel_id=1, replica_groups=mesh['replica'=2,'dp'=4,'cx'=4,'cz'=8] {'dp','cx'}, dimensions={0} | all-to-all | bytes 131072 | tf_op jit(solution)/shard_map/all_to_all | solution.py:39
  115.7 9.2 %all_to_all.33 = f32[8,8,128]{2,1,0:T(8,128)S(1)} all-to-all(f32[8,8,128]{2,1,0:T(8,128)S(1)} %broadcast_in_dim.15), channel_id=1, replica_groups=mesh['replica'=2,'dp'=4,'cx'=4,'cz'=8] {'cz'}, dimensions={0} | all-to-all | bytes 65536 | tf_op jit(solution)/shard_map/all_to_all | solution.py:39
  125.0 6.5 %fusion.10 = f32[1,2048]{1,0:T(1,128)S(1)} fusion(f32[1024,1]{0,1:T(1,128)S(1)} %bitcast.47, f32[1024,2048]{1,0:T(8,128)} %copy-done), kind=kOutput, calls=%fused_computation.27 | convolution fusion | flops 25165824 | bytes 8400896 | tf_op jit(solution)/shard_map/sr,srk->sk/dot_general | solution.py:22
  131.5 9.4 %fusion.11 = f32[1,8,128]{2,0,1:T(1,128)S(1)} fusion(f32[8,128,2048]{2,1,0:T(8,128)} %bitcast.35, f32[2048,1,1]{0,1,2:T(1,128)S(1)} %bitcast.37), kind=kOutput, calls=%fused_computation.28 | convolution fusion | flops 25165824 | bytes 8400896 | tf_op jit(solution)/shard_map/srk,sk->sr/dot_general | solution.py:26
  140.9 9.4 %all_to_all.34 = f32[16,8,128]{2,1,0:T(8,128)S(1)} all-to-all(f32[16,8,128]{2,1,0:T(8,128)S(1)} %broadcast_in_dim.16), channel_id=1, replica_groups=mesh['replica'=2,'dp'=4,'cx'=4,'cz'=8] {'dp','cx'}, dimensions={0} | all-to-all | bytes 131072 | tf_op jit(solution)/shard_map/all_to_all | solution.py:39
  150.3 9.2 %all_to_all.35 = f32[8,8,128]{2,1,0:T(8,128)S(1)} all-to-all(f32[8,8,128]{2,1,0:T(8,128)S(1)} %broadcast_in_dim.17), channel_id=1, replica_groups=mesh['replica'=2,'dp'=4,'cx'=4,'cz'=8] {'cz'}, dimensions={0} | all-to-all | bytes 65536 | tf_op jit(solution)/shard_map/all_to_all | solution.py:39
  159.6 10.6 %fusion = f32[2048,1024]{1,0:T(8,128)} fusion(bf16[1024,1024]{1,0:T(8,128)(2,1)S(1)} %copy-done.2, f32[1024,2048]{1,0:T(8,128)} %copy-done, f32[2048]{0:T(1024)S(1)} %broadcast_divide_fusion, f32[1024]{0:T(1024)S(1)} %multiply_bitcast_fusion), kind=kOutput, calls=%fused_computation.4 | convolution fusion | flops 4301258752 | bytes 18886656 | tf_op jit(solution)/shard_map/dot_general | solution.py:63
  170.2 23.3 %reduce-scatter.2.cloned.1.call-done = f32[2048,512]{1,0:T(8,128)} async-done(((f32[2048,1024]{1,0:T(8,128)}), f32[2048,512]{1,0:T(8,128)}) %reduce-scatter.2.cloned.1.call-update) | async-done | bytes 4194320 | tf_op jit(solution)/shard_map/reduce_scatter | solution.py:66
  193.4 2.5 %multiply_reduce_fusion.1 = f32[2048]{0:T(1024)S(1)} fusion(f32[2048,512]{1,0:T(8,128)} %reduce-scatter.2.cloned.1.call-done), kind=kLoop, calls=%fused_computation.5 | loop fusion | flops 2095104 | bytes 4202496 | tf_op jit(solution)/shard_map/reduce_sum | solution.py:67
  196.0 2.5 %psum.7 = f32[2048]{0:T(1024)S(1)} all-reduce(f32[2048]{0:T(1024)S(1)} %multiply_reduce_fusion.1), channel_id=1, replica_groups=mesh['replica'=2,'dp'=4,'cx'=4,'cz'=8] {'replica'}, use_global_device_ids=true, to_apply=%region_10.0 | all-reduce | flops 2048 | bytes 16384 | tf_op jit(solution)/shard_map/psum | solution.py:67
  198.5 4.5 %broadcast_multiply_fusion = f32[2048,512]{1,0:T(8,128)} fusion(f32[2048,512]{1,0:T(8,128)} %reduce-scatter.2.cloned.1.call-done, f32[2048]{0:T(1024)S(1)} %add_rsqrt_fusion), kind=kLoop, calls=%fused_computation.9 | loop fusion | flops 1048576 | bytes 8396800 | tf_op jit(solution)/shard_map/mul | solution.py:68
  (29 shorter events, 0.3 us)
Async XLA Ops:
  6.5 40.9 %all-gather.2.cloned.1.call-start = ((), (), s32[]{:S(2)}) async-start(), calls=%async_computation.7 | async-start | bytes 2621440 | tf_op jit(solution)/shard_map/all_gather | solution.py:60
  10.1 183.3 %reduce-scatter.2.cloned.1.call-start = ((), (), s32[]{:S(2)}) async-start(), calls=%async_computation.8 | async-start | bytes 12582912 | tf_op jit(solution)/shard_map/reduce_scatter | solution.py:66
  55.4 11.2 %copy-start = (f32[1024,2048]{1,0:T(8,128)}, f32[1024,2048]{1,0:T(8,128)S(1)}, u32[]{:S(2)}) copy-start(f32[1024,2048]{1,0:T(8,128)S(1)} %multiply_exponential_fusion) | copy-start | bytes 25165828
  91.6 7.1 %copy-start.1 = (f32[1024,2048]{1,0:T(8,128)S(1)}, f32[1024,2048]{1,0:T(8,128)}, u32[]{:S(2)}) copy-start(f32[1024,2048]{1,0:T(8,128)} %copy-done) | copy-start | bytes 25165828
  125.0 34.6 %copy-start.2 = (bf16[1024,1024]{1,0:T(8,128)(2,1)S(1)}, bf16[1024,1024]{1,0:T(8,128)(2,1)}, u32[]{:S(2)}) copy-start(bf16[1024,1024]{1,0:T(8,128)(2,1)} %all-gather.2.cloned.1.call-done) | copy-start | bytes 6291460
Sparse Core Ops, SparseCore 0:
  10.2 37.2 all-gather.1
  170.3 23.1 reduce-scatter.1

commit v2 on v1

v2 whole, which is shorter than its diff:
```python
import functools
import math

import jax
import jax.numpy as jnp
from jax import lax
from jax.experimental import pallas as pl
from jax.experimental.pallas import tpu as pltpu
from jax.sharding import Mesh, PartitionSpec as P

VECTOR_WIDTH = 1024
ITERS = 3
SOFTMAX_HEAT = 0.05
EXPONENT = math.log2(math.e) / SOFTMAX_HEAT / VECTOR_WIDTH

LANES = 128
GROUP_ROWS = 8
CHUNK = 256
TILE = 64
VMEM_LIMIT = 30 * 1024 * 1024
F32 = jnp.float32
BF16 = jnp.bfloat16

IN_VMEM = pl.BlockSpec(memory_space=pltpu.VMEM)


def params():
    return pltpu.CompilerParams(vmem_limit_bytes=VMEM_LIMIT)


def unit(values):
    scale = lax.rsqrt(jnp.mean(values * values, axis=-1, keepdims=True) + 1e-06)
    return (values * scale).astype(BF16)


def affinity(unit_centroids, unit_vectors):
    scores = lax.dot_general(
        unit_centroids, unit_vectors, (((1,), (1,)), ((), ())), preferred_element_type=F32
    )
    return jnp.exp2(scores * EXPONENT)


def unit_kernel(values_ref, unit_ref):
    unit_ref[...] = unit(values_ref[...])


def unit_rows(values):
    return pl.pallas_call(
        unit_kernel,
        out_shape=jax.ShapeDtypeStruct(values.shape, BF16),
        in_specs=[IN_VMEM],
        out_specs=IN_VMEM,
        compiler_params=params(),
        cost_estimate=pl.CostEstimate(flops=4 * values.size, bytes_accessed=6 * values.size, transcendentals=0),
    )(values)


def own_scores_kernel(centroids_ref, vectors_ref, unit_ref, scores_ref):
    unit_ref[...] = unit(centroids_ref[...])
    scores_ref[...] = affinity(unit_ref[...], vectors_ref[...])


def own_scores(centroids, vectors):
    lists, width = centroids.shape
    block = vectors.shape[0]
    return pl.pallas_call(
        own_scores_kernel,
        grid=(lists // CHUNK,),
        out_shape=(
            jax.ShapeDtypeStruct((lists, width), BF16),
            jax.ShapeDtypeStruct((lists, block), F32),
        ),
        in_specs=[
            pl.BlockSpec((CHUNK, width), lambda i: (i, 0)),
            pl.BlockSpec((block, width), lambda i: (0, 0)),
        ],
        out_specs=(
            pl.BlockSpec((CHUNK, width), lambda i: (i, 0)),
            pl.BlockSpec((CHUNK, block), lambda i: (i, 0)),
        ),
        compiler_params=params(),
        cost_estimate=pl.CostEstimate(
            flops=2 * lists * width * block, bytes_accessed=8 * lists * width, transcendentals=lists * block
        ),
    )(centroids, vectors)


def tile_mass(tile, row_scale, lists_total):
    totals = jnp.sum(tile * row_scale, axis=1, keepdims=True)
    col_scale = (1.0 / lists_total) / totals
    scaled = tile * col_scale
    return jnp.sum(scaled.reshape(-1, GROUP_ROWS, tile.shape[1]), axis=0)


def place_mass(mass, hops, rows_ref, copies_ref):
    row = jnp.sum(mass, axis=0, keepdims=True)
    blocks = len(hops)
    per_block = row.shape[1] // blocks // LANES
    here = lax.axis_index("dp")
    for j, hop in enumerate(hops):
        first = lax.rem(here + hop, blocks) * per_block
        for i in range(per_block):
            at = (j * per_block + i) * LANES
            rows_ref[pl.ds(first + i, 1), :] = row[:, at : at + LANES]
    copies_ref[...] = jnp.broadcast_to(rows_ref[...][None], copies_ref.shape)


def relative_row(rows_ref, hops):
    blocks = len(hops)
    per_block = rows_ref.shape[0] // blocks
    here = lax.axis_index("dp")
    parts = []
    for hop in hops:
        first = lax.rem(here + hop, blocks) * per_block
        parts += [rows_ref[pl.ds(first + i, 1), :] for i in range(per_block)]
    return jnp.concatenate(parts, axis=1)


def first_kernel(hops, lists_total, centroids_ref, own_ref, *refs):
    blocks = len(hops)
    vector_refs = refs[:blocks]
    kt_ref, slab_ref, copies_ref, mass_ref, rows_ref = refs[blocks:]
    step = pl.program_id(0)
    block = own_ref.shape[1]
    slab = block * blocks

    @pl.when(step == 0)
    def _():
        mass_ref[...] = jnp.zeros_like(mass_ref)
        for j, vector_ref in enumerate(vector_refs):
            slab_ref[pl.ds(j * block, block), :] = vector_ref[...]

    kt_ref[:, :block] = own_ref[...]
    kt_ref[:, block:] = affinity(centroids_ref[...], slab_ref[block:, :])
    row_scale = jnp.full((1, slab), 1.0 / slab, F32)
    mass = jnp.zeros(mass_ref.shape, F32)
    for t in range(CHUNK // TILE):
        mass = mass + tile_mass(kt_ref[pl.ds(t * TILE, TILE), :], row_scale, lists_total)
    mass_ref[...] += mass

    @pl.when(step == pl.num_programs(0) - 1)
    def _():
        place_mass(mass_ref[...], hops, rows_ref, copies_ref)


def first_sweep(unit_centroids, own, vectors, hops, lists_total, peers):
    lists, width = unit_centroids.shape
    block = own.shape[1]
    slab = block * len(hops)
    rows = slab // LANES
    whole = lambda shape: pl.BlockSpec(shape, lambda i: (0,) * len(shape))
    return pl.pallas_call(
        functools.partial(first_kernel, hops, lists_total),
        grid=(lists // CHUNK,),
        out_shape=(
            jax.ShapeDtypeStruct((lists, slab), F32),
            jax.ShapeDtypeStruct((slab, width), BF16),
            jax.ShapeDtypeStruct((peers, rows, LANES), F32),
        ),
        in_specs=[
            pl.BlockSpec((CHUNK, width), lambda i: (i, 0)),
            pl.BlockSpec((CHUNK, block), lambda i: (i, 0)),
        ]
        + [whole((block, width))] * len(hops),
        out_specs=(
            pl.BlockSpec((CHUNK, slab), lambda i: (i, 0)),
            whole((slab, width)),
            whole((peers, rows, LANES)),
        ),
        scratch_shapes=[pltpu.VMEM((GROUP_ROWS, slab), F32), pltpu.VMEM((rows, LANES), F32)],
        compiler_params=params(),
        cost_estimate=pl.CostEstimate(
            flops=2 * lists * width * slab, bytes_accessed=6 * lists * slab, transcendentals=lists * slab
        ),
    )(unit_centroids, own, *vectors)


def row_scale_of(received_ref, rows_ref, hops):
    totals = jnp.sum(received_ref[...], axis=0)
    rows_ref[...] = (1.0 / (totals.shape[0] * totals.shape[1])) / totals
    return relative_row(rows_ref, hops)


def sweep_kernel(hops, lists_total, received_ref, kt_ref, copies_ref, mass_ref, rows_ref, scale_ref):
    step = pl.program_id(0)

    @pl.when(step == 0)
    def _():
        mass_ref[...] = jnp.zeros_like(mass_ref)
        scale_ref[...] = row_scale_of(received_ref, rows_ref, hops)

    row_scale = scale_ref[...]
    mass = jnp.zeros(mass_ref.shape, F32)
    for t in range(CHUNK // TILE):
        mass = mass + tile_mass(kt_ref[pl.ds(t * TILE, TILE), :], row_scale, lists_total)
    mass_ref[...] += mass

    @pl.when(step == pl.num_programs(0) - 1)
    def _():
        place_mass(mass_ref[...], hops, rows_ref, copies_ref)


def next_sweep(received, kt, hops, lists_total, peers):
    lists, slab = kt.shape
    rows = slab // LANES
    return pl.pallas_call(
        functools.partial(sweep_kernel, hops, lists_total),
        grid=(lists // CHUNK,),
        out_shape=jax.ShapeDtypeStruct((peers, rows, LANES), F32),
        in_specs=[
            pl.BlockSpec(received.shape, lambda i: (0, 0, 0)),
            pl.BlockSpec((CHUNK, slab), lambda i: (i, 0)),
        ],
        out_specs=pl.BlockSpec((peers, rows, LANES), lambda i: (0, 0, 0)),
        scratch_shapes=[
            pltpu.VMEM((GROUP_ROWS, slab), F32),
            pltpu.VMEM((rows, LANES), F32),
            pltpu.VMEM((1, slab), F32),
        ],
        compiler_params=params(),
        cost_estimate=pl.CostEstimate(flops=4 * lists * slab, bytes_accessed=4 * lists * slab, transcendentals=0),
    )(received, kt)


def update_kernel(hops, lists_total, before_ref, received_ref, kt_ref, slab_ref, out_ref, rows_ref, before_scale, scale):
    @pl.when(pl.program_id(0) == 0)
    def _():
        before_scale[...] = row_scale_of(before_ref, rows_ref, hops)
        scale[...] = row_scale_of(received_ref, rows_ref, hops) * (scale.shape[1] * lists_total)

    kt = kt_ref[...]
    col_scale = (1.0 / lists_total) / jnp.sum(kt * before_scale[...], axis=1, keepdims=True)
    weights = (scale[...] * kt * col_scale).astype(BF16)
    out_ref[...] = jnp.dot(weights, slab_ref[...], preferred_element_type=F32)


def update(before, received, kt, slab_vectors, hops, lists_total):
    lists, slab = kt.shape
    width = slab_vectors.shape[1]
    rows = slab // LANES
    return pl.pallas_call(
        functools.partial(update_kernel, hops, lists_total),
        grid=(lists // CHUNK,),
        out_shape=jax.ShapeDtypeStruct((lists, width), F32),
        in_specs=[
            pl.BlockSpec(before.shape, lambda i: (0, 0, 0)),
            pl.BlockSpec(received.shape, lambda i: (0, 0, 0)),
            pl.BlockSpec((CHUNK, slab), lambda i: (i, 0)),
            pl.BlockSpec((slab, width), lambda i: (0, 0)),
        ],
        out_specs=pl.BlockSpec((CHUNK, width), lambda i: (i, 0)),
        scratch_shapes=[
            pltpu.VMEM((rows, LANES), F32),
            pltpu.VMEM((1, slab), F32),
            pltpu.VMEM((1, slab), F32),
        ],
        compiler_params=params(),
        cost_estimate=pl.CostEstimate(
            flops=2 * lists * width * slab, bytes_accessed=8 * lists * slab, transcendentals=0
        ),
    )(before, received, kt, slab_vectors)


def exchange(copies, axes):
    return lax.all_to_all(copies, axes, 0, 0, tiled=True)


def sum_over_lists(copies):
    partial = jnp.sum(exchange(copies, ("dp", "cx")), axis=0)
    size = lax.axis_size("cz")
    return exchange(jnp.broadcast_to(partial[None], (size,) + partial.shape), "cz")


def body(vectors, centroids):
    dp = lax.axis_size("dp")
    peers = dp * lax.axis_size("cx")
    lists_total = centroids.shape[0] * peers * lax.axis_size("cz")
    hops = tuple(range(dp))
    mine = unit_rows(vectors)
    others = [lax.ppermute(mine, "dp", [((i + hop) % dp, i) for i in range(dp)]) for hop in hops[1:]]
    unit_centroids, own = own_scores(centroids, mine)
    kt, slab_vectors, copies = first_sweep(
        unit_centroids, own, [mine] + others, hops, lists_total, peers
    )
    received = sum_over_lists(copies)
    for sweep in range(1, ITERS):
        before = received
        received = sum_over_lists(next_sweep(before, kt, hops, lists_total, peers))
    partial_numer = update(before, received, kt, slab_vectors, hops, lists_total)
    numerators = lax.psum_scatter(partial_numer, "replica", scatter_dimension=1, tiled=True)
    squares = lax.psum(jnp.sum(numerators * numerators, axis=1), "replica")
    return numerators * lax.rsqrt(squares / VECTOR_WIDTH + 1e-06)[:, None]


def solution(mesh):
    cent = mesh.shape["cent"]
    split = Mesh(
        mesh.devices.reshape(mesh.shape["replica"], mesh.shape["dp"], 4, cent // 4),
        ("replica", "dp", "cx", "cz"),
    )
    placed = (P(("replica", "dp"), None), P(("dp", "cx", "cz"), None))
    return jax.shard_map(
        body, mesh=split, in_specs=placed, out_specs=P(("dp", "cx", "cz"), "replica"), check_vma=False
    )
```

time: 210 us -> 174 us (0.83)
  matrix products: 59.9 us -> 0 us
  local copies, waits for them, and re-layouts: 0.08 us -> 21.2 us
  Pallas kernels: 0 us -> 19 us
  waiting for transfers between devices: 56.6 us -> 38.3 us
  other arithmetic: 14.8 us -> 7.14 us
  starting transfers between devices: 0.04 us -> 5.89 us
  blocking collectives: 65 us -> 68 us
    dot_general x8 -> x0, matrix products: 59.9 us -> none  [the longest x3 23.8 us: balanced_weights(): jnp.einsum('srk,sk->sr', affinity_kernel, col_scale, precision=lax.Precis...]
    all_gather x1 -> x0, waiting for transfers between devices: 33.3 us -> none  [body(): slab_vectors = lax.all_gather(local_unit_rows, 'dp', axis=0, tiled=True)]
    unnamed x6 -> x14, local copies, waits for them, and re-layouts: 0.01 us -> 21.2 us
    pallas_call x0 -> x6, Pallas kernels: none -> 19 us  [the longest x1 6.68 us: update(): pl.pallas_call(functools.partial(update_kernel, hops, lists_total), grid=...]
    ppermute x0 -> x3, waiting for transfers between devices: none -> 14.9 us  [body(): lax.ppermute(mine, 'dp', [((i + hop) % dp, i) for i in range(dp)])]
    ppermute x0 -> x3, starting transfers between devices: none -> 5.89 us  [body(): lax.ppermute(mine, 'dp', [((i + hop) % dp, i) for i in range(dp)])]
    reduce_sum x8 -> x3, other arithmetic: 5.46 us -> 0.06 us  [sum_over_lists(): partial = jnp.sum(exchange(copies, ('dp', 'cx')), axis=0)]
    all_to_all x6, blocking collectives: 62.5 us -> 65.5 us  [exchange(): return lax.all_to_all(copies, axes, 0, 0, tiled=True)]
  transfers between devices with their start and end apart: 2 -> 4, of which waited for: 2 -> 3; matrix products, arithmetic and copies ran while one was open for 2% -> 0% of each run, Pallas kernels for 0% -> 2%
where the time goes in v2:
time: 174 us; the launch traced here: 173 us
  blocking collectives  68 us (39%)
  waiting for transfers between devices  38.3 us (22%)
  local copies, waits for them, and re-layouts  21.2 us (12%)
  Pallas kernels  19 us (11%)
  between operations  13.5 us (8%)
  other arithmetic  7.14 us (4%)
  starting transfers between devices  5.89 us (3%)
    all_to_all x6, blocking collectives, exchange(): return lax.all_to_all(copies, axes, 0, 0, tiled=True)  65.5 us
    reduce_scatter x1, waiting for transfers between devices, body(): lax.psum_scatter(partial_numer, 'replica', scatter_dimension=1, tiled=True)  23.5 us
    unnamed x14, local copies, waits for them, and re-layouts  21.2 us
    ppermute x3, waiting for transfers between devices, body(): lax.ppermute(mine, 'dp', [((i + hop) % dp, i) for i in range(dp)])  14.9 us
    pallas_call x1, Pallas kernels, update(): pl.pallas_call(functools.partial(update_kernel, hops, lists_total), grid=...  6.68 us
    pallas_call x1, Pallas kernels, first_sweep(): pl.pallas_call(functools.partial(first_kernel, hops, lists_total), grid=(...  5.96 us
    ppermute x3, starting transfers between devices, body(): lax.ppermute(mine, 'dp', [((i + hop) % dp, i) for i in range(dp)])  5.89 us
    mul x1, other arithmetic, body(): return numerators * lax.rsqrt(squares / VECTOR_WIDTH + 1e-06)[:, None]  4.54 us
  transfers between devices with their start and end apart: 4, of which 3 were waited for; matrix products, arithmetic and copies ran while one was open for 0% of the time, Pallas kernels for 2%

profile of v2, /device:TPU:1, one launch (start us, length us, event | category | flops | bytes accessed | tf_op | source)
XLA Modules:
  0.0 173.1 jit_solution(17895408102211696125)
XLA Ops:
  7.9 2.2 %collective-permute-start.2 = (bf16[256,1024]{1,0:T(8,128)(2,1)S(1)}, bf16[256,1024]{1,0:T(8,128)(2,1)S(1)}, u32[]{:S(2)}, u32[]{:S(2)}) collective-permute-start(bf16[256,1024]{1,0:T(8,128)(2,1)S(1)} %shard_map.28.vectors_ref.refs_0_), channel_id=1, source_target_pairs={{96,0},{0,32},{32,64},{64,96},{97,1},{1,33},{33,65},{65,97},{98,2}... | collective-permute-start | bytes 1572872 | tf_op jit(solution)/shard_map/ppermute | solution.py:280
  10.1 2.6 %collective-permute-start.1 = (bf16[256,1024]{1,0:T(8,128)(2,1)S(1)}, bf16[256,1024]{1,0:T(8,128)(2,1)S(1)}, u32[]{:S(2)}, u32[]{:S(2)}) collective-permute-start(bf16[256,1024]{1,0:T(8,128)(2,1)S(1)} %shard_map.28.vectors_ref.refs_0_), channel_id=1, source_target_pairs={{64,0},{96,32},{0,64},{32,96},{65,1},{97,33},{1,65},{33,97},{66,2}... | collective-permute-start | bytes 1572872 | tf_op jit(solution)/shard_map/ppermute | solution.py:280
  13.8 3.4 %copy-done.5 = f32[2048,1024]{1,0:T(8,128)S(1)} copy-done((f32[2048,1024]{1,0:T(8,128)S(1)}, f32[2048,1024]{1,0:T(8,128)}, u32[]{:S(2)}) %copy-start.5) | copy-done | bytes 8388632
  17.2 3.2 %shard_map.29 = (bf16[2048,1024]{1,0:T(8,128)(2,1)S(1)}, f32[2048,256]{1,0:T(8,128)S(1)}) custom-call(f32[2048,1024]{1,0:T(8,128)S(1)} %copy-done.5, bf16[256,1024]{1,0:T(8,128)(2,1)S(1)} %shard_map.28.vectors_ref.refs_0_), custom_call_target="tpu_custom_call" | custom-call | flops 1073741824 | bytes 16777216 | tf_op jit(solution)/shard_map/pallas_call | solution.py:66
  21.2 14.1 %collective-permute-done.1.refs_2_ = bf16[256,1024]{1,0:T(8,128)(2,1)S(1)} collective-permute-done((bf16[256,1024]{1,0:T(8,128)(2,1)S(1)}, bf16[256,1024]{1,0:T(8,128)(2,1)S(1)}, u32[]{:S(2)}, u32[]{:S(2)}) %collective-permute-start.1) | collective-permute-done | bytes 524320 | tf_op jit(solution)/shard_map/ppermute | solution.py:280
  35.3 6.0 %shard_map.30 = (f32[2048,1024]{1,0:T(8,128)S(1)}, bf16[1024,1024]{1,0:T(8,128)(2,1)S(1)}, f32[16,8,128]{2,1,0:T(8,128)S(1)}) custom-call(bf16[2048,1024]{1,0:T(8,128)(2,1)S(1)} %get-tuple-element.10.centroids_ref, f32[2048,256]{1,0:T(8,128)S(1)} %get-tuple-element.11.own_ref, bf16[256,1024]{1,0:T(8,128)(2,1)S(1)} %shard_map.28.vectors_ref.refs_0_, ...), custom_call_target="tpu_custom_call" | custom-call | flops 4294967296 | bytes 12582912 | tf_op jit(solution)/shard_map/pallas_call | solution.py:152
  41.3 3.2 %copy-done = f32[2048,1024]{1,0:T(8,128)} copy-done((f32[2048,1024]{1,0:T(8,128)}, f32[2048,1024]{1,0:T(8,128)S(1)}, u32[]{:S(2)}) %copy-start) | copy-done | bytes 8388632
  44.5 13.1 %all_to_all.30 = f32[16,8,128]{2,1,0:T(8,128)S(1)} all-to-all(f32[16,8,128]{2,1,0:T(8,128)S(1)} %get-tuple-element.12), channel_id=1, replica_groups=mesh['replica'=2,'dp'=4,'cx'=4,'cz'=8] {'dp','cx'}, dimensions={0} | all-to-all | bytes 131072 | tf_op jit(solution)/shard_map/all_to_all | solution.py:265
  57.6 14.9 %all_to_all.31.received_ref = f32[8,8,128]{2,1,0:T(8,128)S(1)} all-to-all(f32[8,8,128]{2,1,0:T(8,128)S(1)} %broadcast_in_dim.6), channel_id=1, replica_groups=mesh['replica'=2,'dp'=4,'cx'=4,'cz'=8] {'cz'}, dimensions={0} | all-to-all | bytes 65536 | tf_op jit(solution)/shard_map/all_to_all | solution.py:265
  72.5 3.4 %copy-done.1 = f32[2048,1024]{1,0:T(8,128)S(1)} copy-done((f32[2048,1024]{1,0:T(8,128)S(1)}, f32[2048,1024]{1,0:T(8,128)}, u32[]{:S(2)}) %copy-start.1) | copy-done | bytes 8388632
  75.9 1.5 shard_map.31
  77.4 9.7 %all_to_all.32 = f32[16,8,128]{2,1,0:T(8,128)S(1)} all-to-all(f32[16,8,128]{2,1,0:T(8,128)S(1)} %shard_map.31), channel_id=1, replica_groups=mesh['replica'=2,'dp'=4,'cx'=4,'cz'=8] {'dp','cx'}, dimensions={0} | all-to-all | bytes 131072 | tf_op jit(solution)/shard_map/all_to_all | solution.py:265
  87.1 9.2 %all_to_all.33.received_ref.before_ref = f32[8,8,128]{2,1,0:T(8,128)S(1)} all-to-all(f32[8,8,128]{2,1,0:T(8,128)S(1)} %broadcast_in_dim.7), channel_id=1, replica_groups=mesh['replica'=2,'dp'=4,'cx'=4,'cz'=8] {'cz'}, dimensions={0} | all-to-all | bytes 65536 | tf_op jit(solution)/shard_map/all_to_all | solution.py:265
  96.3 3.4 %copy-done.2 = f32[2048,1024]{1,0:T(8,128)S(1)} copy-done((f32[2048,1024]{1,0:T(8,128)S(1)}, f32[2048,1024]{1,0:T(8,128)}, u32[]{:S(2)}) %copy-start.2) | copy-done | bytes 8388632
  99.7 1.5 shard_map.32
  101.2 9.4 %all_to_all.34 = f32[16,8,128]{2,1,0:T(8,128)S(1)} all-to-all(f32[16,8,128]{2,1,0:T(8,128)S(1)} %shard_map.32), channel_id=1, replica_groups=mesh['replica'=2,'dp'=4,'cx'=4,'cz'=8] {'dp','cx'}, dimensions={0} | all-to-all | bytes 131072 | tf_op jit(solution)/shard_map/all_to_all | solution.py:265
  110.6 9.2 %all_to_all.35.received_ref = f32[8,8,128]{2,1,0:T(8,128)S(1)} all-to-all(f32[8,8,128]{2,1,0:T(8,128)S(1)} %broadcast_in_dim.8), channel_id=1, replica_groups=mesh['replica'=2,'dp'=4,'cx'=4,'cz'=8] {'cz'}, dimensions={0} | all-to-all | bytes 65536 | tf_op jit(solution)/shard_map/all_to_all | solution.py:265
  119.8 3.4 %copy-done.3 = f32[2048,1024]{1,0:T(8,128)S(1)} copy-done((f32[2048,1024]{1,0:T(8,128)S(1)}, f32[2048,1024]{1,0:T(8,128)}, u32[]{:S(2)}) %copy-start.3) | copy-done | bytes 8388632
  123.2 6.7 %shard_map.33 = f32[2048,1024]{1,0:T(8,128)S(1)} custom-call(f32[8,8,128]{2,1,0:T(8,128)S(1)} %all_to_all.33.received_ref.before_ref, f32[8,8,128]{2,1,0:T(8,128)S(1)} %all_to_all.35.received_ref, f32[2048,1024]{1,0:T(8,128)S(1)} %copy-done.3, bf16[1024,1024]{1,0:T(8,128)(2,1)S(1)} %get-tuple-element.14.slab_ref), custom_call_target="tpu_custom_call" | custom-call | flops 4294967296 | bytes 16777216 | tf_op jit(solution)/shard_map/pallas_call | solution.py:241
  129.9 3.2 %copy-done.4 = f32[2048,1024]{1,0:T(8,128)} copy-done((f32[2048,1024]{1,0:T(8,128)}, f32[2048,1024]{1,0:T(8,128)S(1)}, u32[]{:S(2)}) %copy-start.4) | copy-done | bytes 8388632
  133.1 23.5 %reduce-scatter.2.cloned.1.call-done = f32[2048,512]{1,0:T(8,128)} async-done(((f32[2048,1024]{1,0:T(8,128)}), f32[2048,512]{1,0:T(8,128)}) %reduce-scatter.2.cloned.1.call-update) | async-done | bytes 4194320 | tf_op jit(solution)/shard_map/reduce_scatter | solution.py:290
  156.6 2.5 %multiply_reduce_fusion = f32[2048]{0:T(1024)S(1)} fusion(f32[2048,512]{1,0:T(8,128)} %reduce-scatter.2.cloned.1.call-done), kind=kLoop, calls=%fused_computation | loop fusion | flops 2095104 | bytes 4202496 | tf_op jit(solution)/shard_map/reduce_sum | solution.py:291
  159.1 2.5 %psum.7 = f32[2048]{0:T(1024)S(1)} all-reduce(f32[2048]{0:T(1024)S(1)} %multiply_reduce_fusion), channel_id=1, replica_groups=mesh['replica'=2,'dp'=4,'cx'=4,'cz'=8] {'replica'}, use_global_device_ids=true, to_apply=%region_5.0 | all-reduce | flops 2048 | bytes 16384 | tf_op jit(solution)/shard_map/psum | solution.py:291
  161.7 4.5 %broadcast_multiply_fusion = f32[2048,512]{1,0:T(8,128)} fusion(f32[2048,512]{1,0:T(8,128)} %reduce-scatter.2.cloned.1.call-done, f32[2048]{0:T(1024)S(1)} %add_rsqrt_fusion), kind=kLoop, calls=%fused_computation.1 | loop fusion | flops 1048576 | bytes 8396800 | tf_op jit(solution)/shard_map/mul | solution.py:292
  (21 shorter events, 3.3 us)
Async XLA Ops:
  6.5 150.1 %reduce-scatter.2.cloned.1.call-start = ((), (), s32[]{:S(2)}) async-start(), calls=%async_computation.7 | async-start | bytes 12582912 | tf_op jit(solution)/shard_map/reduce_scatter | solution.py:290
  6.5 1.2 copy-start.6
  7.9 13.3 %collective-permute-start.2 = (bf16[256,1024]{1,0:T(8,128)(2,1)S(1)}, bf16[256,1024]{1,0:T(8,128)(2,1)S(1)}, u32[]{:S(2)}, u32[]{:S(2)}) collective-permute-start(bf16[256,1024]{1,0:T(8,128)(2,1)S(1)} %shard_map.28.vectors_ref.refs_0_), channel_id=1, source_target_pairs={{96,0},{0,32},{32,64},{64,96},{97,1},{1,33},{33,65},{65,97},{98,2}... | collective-permute-start | bytes 1572872 | tf_op jit(solution)/shard_map/ppermute | solution.py:280
  10.1 25.2 %collective-permute-start.1 = (bf16[256,1024]{1,0:T(8,128)(2,1)S(1)}, bf16[256,1024]{1,0:T(8,128)(2,1)S(1)}, u32[]{:S(2)}, u32[]{:S(2)}) collective-permute-start(bf16[256,1024]{1,0:T(8,128)(2,1)S(1)} %shard_map.28.vectors_ref.refs_0_), channel_id=1, source_target_pairs={{64,0},{96,32},{0,64},{32,96},{65,1},{97,33},{1,65},{33,97},{66,2}... | collective-permute-start | bytes 1572872 | tf_op jit(solution)/shard_map/ppermute | solution.py:280
  12.8 22.6 %collective-permute-start = (bf16[256,1024]{1,0:T(8,128)(2,1)S(1)}, bf16[256,1024]{1,0:T(8,128)(2,1)S(1)}, u32[]{:S(2)}, u32[]{:S(2)}) collective-permute-start(bf16[256,1024]{1,0:T(8,128)(2,1)S(1)} %shard_map.28.vectors_ref.refs_0_), channel_id=1, source_target_pairs={{32,0},{64,32},{96,64},{0,96},{33,1},{65,33},{97,65},{1,97},{34,2}... | collective-permute-start | bytes 1572872 | tf_op jit(solution)/shard_map/ppermute | solution.py:280
  13.8 3.4 %copy-start.5 = (f32[2048,1024]{1,0:T(8,128)S(1)}, f32[2048,1024]{1,0:T(8,128)}, u32[]{:S(2)}) copy-start(f32[2048,1024]{1,0:T(8,128)} %centroids_ref.1) | copy-start | bytes 25165828
  41.3 3.2 %copy-start = (f32[2048,1024]{1,0:T(8,128)}, f32[2048,1024]{1,0:T(8,128)S(1)}, u32[]{:S(2)}) copy-start(f32[2048,1024]{1,0:T(8,128)S(1)} %get-tuple-element.13.kt_ref) | copy-start | bytes 25165828
  72.5 3.4 %copy-start.1 = (f32[2048,1024]{1,0:T(8,128)S(1)}, f32[2048,1024]{1,0:T(8,128)}, u32[]{:S(2)}) copy-start(f32[2048,1024]{1,0:T(8,128)} %copy-done) | copy-start | bytes 25165828
  96.3 3.4 %copy-start.2 = (f32[2048,1024]{1,0:T(8,128)S(1)}, f32[2048,1024]{1,0:T(8,128)}, u32[]{:S(2)}) copy-start(f32[2048,1024]{1,0:T(8,128)} %copy-done) | copy-start | bytes 25165828
  119.8 3.4 %copy-start.3 = (f32[2048,1024]{1,0:T(8,128)S(1)}, f32[2048,1024]{1,0:T(8,128)}, u32[]{:S(2)}) copy-start(f32[2048,1024]{1,0:T(8,128)} %copy-done) | copy-start | bytes 25165828
  129.9 3.2 %copy-start.4 = (f32[2048,1024]{1,0:T(8,128)}, f32[2048,1024]{1,0:T(8,128)S(1)}, u32[]{:S(2)}) copy-start(f32[2048,1024]{1,0:T(8,128)S(1)} %shard_map.33) | copy-start | bytes 25165828
Sparse Core Ops, SparseCore 0:
  133.3 23.2 reduce-scatter.1

commit v3 on v2

--- a/solution.py
+++ b/solution.py
@@ -17,7 +17,8 @@
 GROUP_ROWS = 8
 CHUNK = 256
 TILE = 64
-VMEM_LIMIT = 30 * 1024 * 1024
+KT_PARTS = 4
+VMEM_LIMIT = 20 * 1024 * 1024
 F32 = jnp.float32
 BF16 = jnp.bfloat16
 
@@ -119,7 +120,7 @@
 def first_kernel(hops, lists_total, centroids_ref, own_ref, *refs):
     blocks = len(hops)
     vector_refs = refs[:blocks]
-    kt_ref, slab_ref, copies_ref, mass_ref, rows_ref = refs[blocks:]
+    kt_ref, kt_send_ref, keep_ref, send_ref, copies_ref, slab_ref, mass_ref, rows_ref = refs[blocks:]
     step = pl.program_id(0)
     block = own_ref.shape[1]
     slab = block * blocks
@@ -129,9 +130,14 @@
         mass_ref[...] = jnp.zeros_like(mass_ref)
         for j, vector_ref in enumerate(vector_refs):
             slab_ref[pl.ds(j * block, block), :] = vector_ref[...]
+        half = keep_ref.shape[1]
+        here = lax.axis_index("replica")
+        keep_ref[...] = slab_ref[:, pl.ds(pl.multiple_of(here * half, half), half)]
+        send_ref[...] = slab_ref[:, pl.ds(pl.multiple_of((1 - here) * half, half), half)]
 
     kt_ref[:, :block] = own_ref[...]
     kt_ref[:, block:] = affinity(centroids_ref[...], slab_ref[block:, :])
+    kt_send_ref[...] = kt_ref[...]
     row_scale = jnp.full((1, slab), 1.0 / slab, F32)
     mass = jnp.zeros(mass_ref.shape, F32)
     for t in range(CHUNK // TILE):
@@ -154,7 +160,8 @@
         grid=(lists // CHUNK,),
         out_shape=(
             jax.ShapeDtypeStruct((lists, slab), F32),
-            jax.ShapeDtypeStruct((slab, width), BF16),
+            pltpu.HBM((lists, slab), F32),
+            *[jax.ShapeDtypeStruct((slab, width // 2), BF16)] * 2,
             jax.ShapeDtypeStruct((peers, rows, LANES), F32),
         ),
         in_specs=[
@@ -163,11 +170,15 @@
         ]
         + [whole((block, width))] * len(hops),
         out_specs=(
-            pl.BlockSpec((CHUNK, slab), lambda i: (i, 0)),
-            whole((slab, width)),
+            *[pl.BlockSpec((CHUNK, slab), lambda i: (i, 0))] * 2,
+            *[whole((slab, width // 2))] * 2,
             whole((peers, rows, LANES)),
         ),
-        scratch_shapes=[pltpu.VMEM((GROUP_ROWS, slab), F32), pltpu.VMEM((rows, LANES), F32)],
+        scratch_shapes=[
+            pltpu.VMEM((slab, width), BF16),
+            pltpu.VMEM((GROUP_ROWS, slab), F32),
+            pltpu.VMEM((rows, LANES), F32),
+        ],
         compiler_params=params(),
         cost_estimate=pl.CostEstimate(
             flops=2 * lists * width * slab, bytes_accessed=6 * lists * slab, transcendentals=lists * slab
@@ -222,33 +233,64 @@
     )(received, kt)
 
 
-def update_kernel(hops, lists_total, before_ref, received_ref, kt_ref, slab_ref, out_ref, rows_ref, before_scale, scale):
-    @pl.when(pl.program_id(0) == 0)
+def to_row(column):
+    return jnp.broadcast_to(column, (LANES, LANES)).T[:1, :]
+
+
+def to_lanes(row):
+    return jnp.broadcast_to(row, (LANES, LANES)).T
+
+
+def update_kernel(hops, lists_total, before_ref, received_ref, slab_ref, *refs):
+    kt_refs, refs = refs[:KT_PARTS], refs[KT_PARTS:]
+    *earlier_refs, out_ref, rows_ref, before_scale, scale = refs
+    step = pl.program_id(0)
+
+    @pl.when(step == 0)
     def _():
         before_scale[...] = row_scale_of(before_ref, rows_ref, hops)
         scale[...] = row_scale_of(received_ref, rows_ref, hops) * (scale.shape[1] * lists_total)
 
-    kt = kt_ref[...]
+    kt = jnp.concatenate([kt_ref[...] for kt_ref in kt_refs], axis=0)
     col_scale = (1.0 / lists_total) / jnp.sum(kt * before_scale[...], axis=1, keepdims=True)
     weights = (scale[...] * kt * col_scale).astype(BF16)
-    out_ref[...] = jnp.dot(weights, slab_ref[...], preferred_element_type=F32)
-
-
-def update(before, received, kt, slab_vectors, hops, lists_total):
+    numerators = jnp.dot(weights, slab_ref[...], preferred_element_type=F32)
+    if not earlier_refs:
+        out_ref[...] = numerators
+        return
+    earlier_ref, total_ref, squares_ref = earlier_refs[0], earlier_refs[1], out_ref
+    total = earlier_ref[...] + numerators
+    total_ref[...] = total
+    squares = jnp.sum(total * total, axis=1, keepdims=True)
+    per_chunk = CHUNK // LANES
+    for k in range(per_chunk):
+        squares_ref[pl.ds(step * per_chunk + k, 1), :] = to_row(squares[k * LANES : (k + 1) * LANES])
+
+
+def update(before, received, kt, slab_vectors, hops, lists_total, earlier=None):
     lists, slab = kt.shape
     width = slab_vectors.shape[1]
     rows = slab // LANES
+    numerators = jax.ShapeDtypeStruct((lists, width), F32)
+    numerators_spec = pl.BlockSpec((CHUNK, width), lambda i: (i, 0))
+    squares = jax.ShapeDtypeStruct((lists // LANES, LANES), F32)
+    squares_spec = pl.BlockSpec(squares.shape, lambda i: (0, 0))
+    first = earlier is None
     return pl.pallas_call(
         functools.partial(update_kernel, hops, lists_total),
         grid=(lists // CHUNK,),
-        out_shape=jax.ShapeDtypeStruct((lists, width), F32),
+        out_shape=numerators if first else (numerators, squares),
         in_specs=[
             pl.BlockSpec(before.shape, lambda i: (0, 0, 0)),
             pl.BlockSpec(received.shape, lambda i: (0, 0, 0)),
-            pl.BlockSpec((CHUNK, slab), lambda i: (i, 0)),
             pl.BlockSpec((slab, width), lambda i: (0, 0)),
-        ],
-        out_specs=pl.BlockSpec((CHUNK, width), lambda i: (i, 0)),
+        ]
+        + [
+            pl.BlockSpec((CHUNK // KT_PARTS, slab), lambda i, j=j: (KT_PARTS * i + j, 0))
+            for j in range(KT_PARTS)
+        ]
+        + [numerators_spec] * (not first),
+        out_specs=numerators_spec if first else (numerators_spec, squares_spec),
         scratch_shapes=[
             pltpu.VMEM((rows, LANES), F32),
             pltpu.VMEM((1, slab), F32),
@@ -258,17 +300,56 @@
         cost_estimate=pl.CostEstimate(
             flops=2 * lists * width * slab, bytes_accessed=8 * lists * slab, transcendentals=0
         ),
-    )(before, received, kt, slab_vectors)
+    )(before, received, slab_vectors, *[kt] * KT_PARTS, *(() if first else (earlier,)))
+
+
+def finish_kernel(numerators_ref, mine_ref, theirs_ref, out_ref):
+    step = pl.program_id(0)
+    per_chunk = CHUNK // LANES
+    for k in range(per_chunk):
+        at = pl.ds(step * per_chunk + k, 1)
+        squares = mine_ref[at, :] + theirs_ref[at, :]
+        scale = to_lanes(lax.rsqrt(squares / VECTOR_WIDTH + 1e-06))
+        lists = pl.ds(k * LANES, LANES)
+        for f in range(0, out_ref.shape[1], LANES):
+            out_ref[lists, f : f + LANES] = numerators_ref[lists, f : f + LANES] * scale
+
+
+def finish(numerators, mine, theirs):
+    lists, width = numerators.shape
+    chunk = pl.BlockSpec((CHUNK, width), lambda i: (i, 0))
+    whole = pl.BlockSpec(mine.shape, lambda i: (0, 0))
+    return pl.pallas_call(
+        finish_kernel,
+        grid=(lists // CHUNK,),
+        out_shape=jax.ShapeDtypeStruct((lists, width), F32),
+        in_specs=[chunk, whole, whole],
+        out_specs=chunk,
+        compiler_params=params(),
+        cost_estimate=pl.CostEstimate(flops=lists * width, bytes_accessed=8 * lists * width, transcendentals=0),
+    )(numerators, mine, theirs)
 
 
 def exchange(copies, axes):
     return lax.all_to_all(copies, axes, 0, 0, tiled=True)
 
 
+def join_kernel(received_ref, copies_ref):
+    copies_ref[...] = jnp.broadcast_to(jnp.sum(received_ref[...], axis=0)[None], copies_ref.shape)
+
+
+def join(received, peers):
+    return pl.pallas_call(
+        join_kernel,
+        out_shape=jax.ShapeDtypeStruct((peers,) + received.shape[1:], F32),
+        in_specs=[IN_VMEM],
+        out_specs=IN_VMEM,
+        compiler_params=pltpu.CompilerParams(vmem_limit_bytes=1024 * 1024),
+    )(received)
+
+
 def sum_over_lists(copies):
-    partial = jnp.sum(exchange(copies, ("dp", "cx")), axis=0)
-    size = lax.axis_size("cz")
-    return exchange(jnp.broadcast_to(partial[None], (size,) + partial.shape), "cz")
+    return exchange(join(exchange(copies, ("dp", "cx")), lax.axis_size("cz")), "cz")
 
 
 def body(vectors, centroids):
@@ -279,17 +360,22 @@
     mine = unit_rows(vectors)
     others = [lax.ppermute(mine, "dp", [((i + hop) % dp, i) for i in range(dp)]) for hop in hops[1:]]
     unit_centroids, own = own_scores(centroids, mine)
-    kt, slab_vectors, copies = first_sweep(
+    kt, kt_sent, kept, sent, copies = first_sweep(
         unit_centroids, own, [mine] + others, hops, lists_total, peers
     )
+    swapped = lambda x: lax.ppermute(x, "replica", [(0, 1), (1, 0)])
+    other_kt, other_vectors = swapped(kt_sent), swapped(sent)
     received = sum_over_lists(copies)
     for sweep in range(1, ITERS):
         before = received
         received = sum_over_lists(next_sweep(before, kt, hops, lists_total, peers))
-    partial_numer = update(before, received, kt, slab_vectors, hops, lists_total)
-    numerators = lax.psum_scatter(partial_numer, "replica", scatter_dimension=1, tiled=True)
-    squares = lax.psum(jnp.sum(numerators * numerators, axis=1), "replica")
-    return numerators * lax.rsqrt(squares / VECTOR_WIDTH + 1e-06)[:, None]
+    before, received = lax.optimization_barrier((before, received))
+    other_before, other_received = swapped(before), swapped(received)
+    numerators = update(before, received, kt, kept, hops, lists_total)
+    numerators, squares = update(
+        other_before, other_received, other_kt, other_vectors, hops, lists_total, numerators
+    )
+    return finish(numerators, squares, swapped(squares))
 
 
 def solution(mesh):

time: 174 us -> 130 us (0.75)
  waiting for transfers between devices: 38.3 us -> 15.7 us
  local copies, waits for them, and re-layouts: 21.2 us -> 4.61 us
  between operations: 13.5 us -> 0.08 us
  starting transfers between devices: 5.89 us -> 16.3 us
  Pallas kernels: 19 us -> 28.5 us
  other arithmetic: 7.14 us -> 0 us
  blocking collectives: 68 us -> 64.8 us
    reduce_scatter x1 -> x0, waiting for transfers between devices: 23.5 us -> none  [body(): lax.psum_scatter(partial_numer, 'replica', scatter_dimension=1, tiled=True)]
    unnamed x14 -> x4, local copies, waits for them, and re-layouts: 21.2 us -> 4.61 us
    ppermute x0 -> x5, starting transfers between devices: none -> 10.4 us  [body(): swapped = lambda x: lax.ppermute(x, 'replica', [(0, 1), (1, 0)])]
    mul x1 -> x0, other arithmetic: 4.54 us -> none  [body(): return numerators * lax.rsqrt(squares / VECTOR_WIDTH + 1e-06)[:, None]]
    pallas_call x0 -> x4, Pallas kernels: none -> 3.85 us  [the longest x1 3.79 us: finish(): pl.pallas_call(finish_kernel, grid=(lists // CHUNK,), out_shape=jax.Shape...]
    pallas_call x1 -> x2, Pallas kernels: 6.68 us -> 10.4 us  [update(): pl.pallas_call(functools.partial(update_kernel, hops, lists_total), grid=...]
    reduce_sum x4 -> x0, other arithmetic: 2.59 us -> none  [the longest x1 2.54 us: body(): squares = lax.psum(jnp.sum(numerators * numerators, axis=1), 'replica')]
    psum x1 -> x0, blocking collectives: 2.51 us -> none  [body(): squares = lax.psum(jnp.sum(numerators * numerators, axis=1), 'replica')]
  transfers between devices with their start and end apart: 4 -> 8, of which waited for: 3 -> 3; matrix products, arithmetic and copies ran while one was open for 0% -> 0% of each run, Pallas kernels for 2% -> 8%
where the time goes in v3:
time: 130 us
  blocking collectives  64.8 us (50%)
  Pallas kernels  28.5 us (22%)
  starting transfers between devices  16.3 us (13%)
  waiting for transfers between devices  15.7 us (12%)
  local copies, waits for them, and re-layouts  4.61 us (4%)
    all_to_all x6, blocking collectives, exchange(): return lax.all_to_all(copies, axes, 0, 0, tiled=True)  64.8 us
    ppermute x3, waiting for transfers between devices, body(): lax.ppermute(mine, 'dp', [((i + hop) % dp, i) for i in range(dp)])  14.9 us
    ppermute x5, starting transfers between devices, body(): swapped = lambda x: lax.ppermute(x, 'replica', [(0, 1), (1, 0)])  10.4 us
    pallas_call x2, Pallas kernels, update(): pl.pallas_call(functools.partial(update_kernel, hops, lists_total), grid=...  10.4 us
    pallas_call x1, Pallas kernels, first_sweep(): pl.pallas_call(functools.partial(first_kernel, hops, lists_total), grid=(...  7.9 us
    ppermute x3, starting transfers between devices, body(): lax.ppermute(mine, 'dp', [((i + hop) % dp, i) for i in range(dp)])  5.89 us
    unnamed x4, local copies, waits for them, and re-layouts  4.61 us
    pallas_call x1, Pallas kernels, finish(): pl.pallas_call(finish_kernel, grid=(lists // CHUNK,), out_shape=jax.Shape...  3.79 us
  transfers between devices with their start and end apart: 8, of which 3 were waited for; matrix products, arithmetic and copies ran while one was open for 0% of the time, Pallas kernels for 8%

profile of v3, /device:TPU:1, one launch (start us, length us, event | category | flops | bytes accessed | tf_op | source)
XLA Modules:
  0.0 130.0 jit_solution(4500787291676959955)
XLA Ops:
  0.0 1.2 copy-done.1
  1.4 2.2 %collective-permute-start.2 = (bf16[256,1024]{1,0:T(8,128)(2,1)S(1)}, bf16[256,1024]{1,0:T(8,128)(2,1)S(1)}, u32[]{:S(2)}, u32[]{:S(2)}) collective-permute-start(bf16[256,1024]{1,0:T(8,128)(2,1)S(1)} %shard_map.28.vectors_ref.refs_0_), channel_id=1, source_target_pairs={{96,0},{0,32},{32,64},{64,96},{97,1},{1,33},{33,65},{65,97},{98,2}... | collective-permute-start | bytes 1572872 | tf_op jit(solution)/shard_map/ppermute | solution.py:361
  3.6 2.6 %collective-permute-start.1 = (bf16[256,1024]{1,0:T(8,128)(2,1)S(1)}, bf16[256,1024]{1,0:T(8,128)(2,1)S(1)}, u32[]{:S(2)}, u32[]{:S(2)}) collective-permute-start(bf16[256,1024]{1,0:T(8,128)(2,1)S(1)} %shard_map.28.vectors_ref.refs_0_), channel_id=1, source_target_pairs={{64,0},{96,32},{0,64},{32,96},{65,1},{97,33},{1,65},{33,97},{66,2}... | collective-permute-start | bytes 1572872 | tf_op jit(solution)/shard_map/ppermute | solution.py:361
  6.2 1.1 collective-permute-start
  7.3 3.4 %copy-done = f32[2048,1024]{1,0:T(8,128)S(1)} copy-done((f32[2048,1024]{1,0:T(8,128)S(1)}, f32[2048,1024]{1,0:T(8,128)}, u32[]{:S(2)}) %copy-start) | copy-done | bytes 8388632
  10.7 3.2 %shard_map.29 = (bf16[2048,1024]{1,0:T(8,128)(2,1)S(1)}, f32[2048,256]{1,0:T(8,128)S(1)}) custom-call(f32[2048,1024]{1,0:T(8,128)S(1)} %copy-done, bf16[256,1024]{1,0:T(8,128)(2,1)S(1)} %shard_map.28.vectors_ref.refs_0_), custom_call_target="tpu_custom_call" | custom-call | flops 1073741824 | bytes 16777216 | tf_op jit(solution)/shard_map/pallas_call | solution.py:67
  13.9 0.7 collective-permute-done.2.refs_3_
  14.6 14.1 %collective-permute-done.1.refs_2_ = bf16[256,1024]{1,0:T(8,128)(2,1)S(1)} collective-permute-done((bf16[256,1024]{1,0:T(8,128)(2,1)S(1)}, bf16[256,1024]{1,0:T(8,128)(2,1)S(1)}, u32[]{:S(2)}, u32[]{:S(2)}) %collective-permute-start.1) | collective-permute-done | bytes 524320 | tf_op jit(solution)/shard_map/ppermute | solution.py:361
  28.8 7.9 %shard_map.30 = (f32[2048,1024]{1,0:T(8,128)S(1)}, f32[2048,1024]{1,0:T(8,128)}, bf16[1024,512]{1,0:T(8,128)(2,1)S(1)}, bf16[1024,512]{1,0:T(8,128)(2,1)S(1)}, f32[16,8,128]{2,1,0:T(8,128)S(1)}) custom-call(bf16[2048,1024]{1,0:T(8,128)(2,1)S(1)} %get-tuple-element.16.centroids_ref, f32[2048,256]{1,0:T(8,128)S(1)} %get-tuple-element.17.own_ref, ...), custom_call_target="tpu_custom_call" | custom-call | flops 4294967296 | bytes 12582912 | tf_op jit(solution)/shard_map/pallas_call | solution.py:158
  36.7 1.6 %collective-permute-start.6 = (f32[2048,1024]{1,0:T(8,128)}, f32[2048,1024]{1,0:T(8,128)S(1)}, u32[]{:S(2)}, u32[]{:S(2)}) collective-permute-start(f32[2048,1024]{1,0:T(8,128)} %get-tuple-element.23), channel_id=1, source_target_pairs={{0,128},{128,0},{1,129},{129,1},{2,130},{130,2},{3,131},{131,3},{4... | collective-permute-start | bytes 25165832 | tf_op jit(solution)/shard_map/ppermute | solution.py:366
  38.2 12.4 %all_to_all.30.received_ref = f32[16,8,128]{2,1,0:T(8,128)S(1)} all-to-all(f32[16,8,128]{2,1,0:T(8,128)S(1)} %get-tuple-element.18), channel_id=1, replica_groups=mesh['replica'=2,'dp'=4,'cx'=4,'cz'=8] {'dp','cx'}, dimensions={0} | all-to-all | bytes 131072 | tf_op jit(solution)/shard_map/all_to_all | solution.py:334
  50.7 14.9 %all_to_all.31.received_ref = f32[8,8,128]{2,1,0:T(8,128)S(1)} all-to-all(f32[8,8,128]{2,1,0:T(8,128)S(1)} %shard_map.31), channel_id=1, replica_groups=mesh['replica'=2,'dp'=4,'cx'=4,'cz'=8] {'cz'}, dimensions={0} | all-to-all | bytes 65536 | tf_op jit(solution)/shard_map/all_to_all | solution.py:334
  65.6 1.5 %shard_map.32 = f32[16,8,128]{2,1,0:T(8,128)S(1)} custom-call(f32[8,8,128]{2,1,0:T(8,128)S(1)} %all_to_all.31.received_ref, f32[2048,1024]{1,0:T(8,128)S(1)} %get-tuple-element.19.kt_ref.refs_0_.refs_1_.refs_2_.refs_3_), custom_call_target="tpu_custom_call" | custom-call | flops 8388608 | bytes 8388608 | tf_op jit(solution)/shard_map/pallas_call | solution.py:217
  67.1 9.7 %all_to_all.32.received_ref = f32[16,8,128]{2,1,0:T(8,128)S(1)} all-to-all(f32[16,8,128]{2,1,0:T(8,128)S(1)} %shard_map.32), channel_id=1, replica_groups=mesh['replica'=2,'dp'=4,'cx'=4,'cz'=8] {'dp','cx'}, dimensions={0} | all-to-all | bytes 131072 | tf_op jit(solution)/shard_map/all_to_all | solution.py:334
  76.7 9.2 %all_to_all.33.received_ref.before_ref = f32[8,8,128]{2,1,0:T(8,128)S(1)} all-to-all(f32[8,8,128]{2,1,0:T(8,128)S(1)} %shard_map.33), channel_id=1, replica_groups=mesh['replica'=2,'dp'=4,'cx'=4,'cz'=8] {'cz'}, dimensions={0} | all-to-all | bytes 65536 | tf_op jit(solution)/shard_map/all_to_all | solution.py:334
  86.0 1.5 %shard_map.34 = f32[16,8,128]{2,1,0:T(8,128)S(1)} custom-call(f32[8,8,128]{2,1,0:T(8,128)S(1)} %all_to_all.33.received_ref.before_ref, f32[2048,1024]{1,0:T(8,128)S(1)} %get-tuple-element.19.kt_ref.refs_0_.refs_1_.refs_2_.refs_3_), custom_call_target="tpu_custom_call" | custom-call | flops 8388608 | bytes 8388608 | tf_op jit(solution)/shard_map/pallas_call | solution.py:217
  87.5 9.4 %all_to_all.34.received_ref = f32[16,8,128]{2,1,0:T(8,128)S(1)} all-to-all(f32[16,8,128]{2,1,0:T(8,128)S(1)} %shard_map.34), channel_id=1, replica_groups=mesh['replica'=2,'dp'=4,'cx'=4,'cz'=8] {'dp','cx'}, dimensions={0} | all-to-all | bytes 131072 | tf_op jit(solution)/shard_map/all_to_all | solution.py:334
  96.9 9.2 %all_to_all.35.received_ref = f32[8,8,128]{2,1,0:T(8,128)S(1)} all-to-all(f32[8,8,128]{2,1,0:T(8,128)S(1)} %shard_map.35), channel_id=1, replica_groups=mesh['replica'=2,'dp'=4,'cx'=4,'cz'=8] {'cz'}, dimensions={0} | all-to-all | bytes 65536 | tf_op jit(solution)/shard_map/all_to_all | solution.py:334
  106.1 8.2 %collective-permute-start.3 = (f32[8,8,128]{2,1,0:T(8,128)S(1)}, f32[8,8,128]{2,1,0:T(8,128)S(1)}, u32[]{:S(2)}, u32[]{:S(2)}) collective-permute-start(f32[8,8,128]{2,1,0:T(8,128)S(1)} %all_to_all.33.received_ref.before_ref), channel_id=1, source_target_pairs={{0,128},{128,0},{1,129},{129,1},{2,130},{130,2},{3,131},{131,3},{4... | collective-permute-start | bytes 98312 | tf_op jit(solution)/shard_map/ppermute | solution.py:366
  114.4 4.7 %shard_map.36.refs_4_ = f32[2048,512]{1,0:T(8,128)S(1)} custom-call(f32[8,8,128]{2,1,0:T(8,128)S(1)} %all_to_all.33.received_ref.before_ref, f32[8,8,128]{2,1,0:T(8,128)S(1)} %all_to_all.35.received_ref, bf16[1024,512]{1,0:T(8,128)(2,1)S(1)} %get-tuple-element.24.slab_ref, f32[2048,1024]{1,0:T(8,128)S(1)} %get-tuple-element.19.kt_ref.refs_0_.refs_1_.refs_2_.refs_3_, ...), custom_call_target="tpu_custom_call" | custom-call | flops 2147483648 | bytes 16777216 | tf_op jit(solution)/shard_map/pallas_call | solution.py:279
  119.1 5.6 %shard_map.37 = (f32[2048,512]{1,0:T(8,128)S(1)}, f32[16,128]{1,0:T(8,128)S(1)}) custom-call(f32[8,8,128]{2,1,0:T(8,128)S(1)} %collective-permute-done.3.before_ref, f32[8,8,128]{2,1,0:T(8,128)S(1)} %collective-permute-done.4.received_ref, bf16[1024,512]{1,0:T(8,128)(2,1)S(1)} %collective-permute-done.5.slab_ref, ...), custom_call_target="tpu_custom_call" | custom-call | flops 2147483648 | bytes 16777216 | tf_op jit(solution)/shard_map/pallas_call | solution.py:279
  124.8 0.6 collective-permute-start.7
  125.4 0.8 collective-permute-done.7.theirs_ref
  126.2 3.8 %shard_map.38 = f32[2048,512]{1,0:T(8,128)} custom-call(f32[2048,512]{1,0:T(8,128)S(1)} %get-tuple-element.25.numerators_ref, f32[16,128]{1,0:T(8,128)S(1)} %get-tuple-element.26.mine_ref, f32[16,128]{1,0:T(8,128)S(1)} %collective-permute-done.7.theirs_ref), custom_call_target="tpu_custom_call" | custom-call | flops 1048576 | bytes 8388608 | tf_op jit(solution)/shard_map/pallas_call | solution.py:322
  (13 shorter events, 0.2 us)
Async XLA Ops:
  0.0 1.2 copy-start.1
  1.4 13.3 %collective-permute-start.2 = (bf16[256,1024]{1,0:T(8,128)(2,1)S(1)}, bf16[256,1024]{1,0:T(8,128)(2,1)S(1)}, u32[]{:S(2)}, u32[]{:S(2)}) collective-permute-start(bf16[256,1024]{1,0:T(8,128)(2,1)S(1)} %shard_map.28.vectors_ref.refs_0_), channel_id=1, source_target_pairs={{96,0},{0,32},{32,64},{64,96},{97,1},{1,33},{33,65},{65,97},{98,2}... | collective-permute-start | bytes 1572872 | tf_op jit(solution)/shard_map/ppermute | solution.py:361
  3.6 25.2 %collective-permute-start.1 = (bf16[256,1024]{1,0:T(8,128)(2,1)S(1)}, bf16[256,1024]{1,0:T(8,128)(2,1)S(1)}, u32[]{:S(2)}, u32[]{:S(2)}) collective-permute-start(bf16[256,1024]{1,0:T(8,128)(2,1)S(1)} %shard_map.28.vectors_ref.refs_0_), channel_id=1, source_target_pairs={{64,0},{96,32},{0,64},{32,96},{65,1},{97,33},{1,65},{33,97},{66,2}... | collective-permute-start | bytes 1572872 | tf_op jit(solution)/shard_map/ppermute | solution.py:361
  6.2 22.6 %collective-permute-start = (bf16[256,1024]{1,0:T(8,128)(2,1)S(1)}, bf16[256,1024]{1,0:T(8,128)(2,1)S(1)}, u32[]{:S(2)}, u32[]{:S(2)}) collective-permute-start(bf16[256,1024]{1,0:T(8,128)(2,1)S(1)} %shard_map.28.vectors_ref.refs_0_), channel_id=1, source_target_pairs={{32,0},{64,32},{96,64},{0,96},{33,1},{65,33},{97,65},{1,97},{34,2}... | collective-permute-start | bytes 1572872 | tf_op jit(solution)/shard_map/ppermute | solution.py:361
  7.3 3.4 %copy-start = (f32[2048,1024]{1,0:T(8,128)S(1)}, f32[2048,1024]{1,0:T(8,128)}, u32[]{:S(2)}) copy-start(f32[2048,1024]{1,0:T(8,128)} %centroids_ref.1) | copy-start | bytes 25165828
  36.7 82.4 %collective-permute-start.6 = (f32[2048,1024]{1,0:T(8,128)}, f32[2048,1024]{1,0:T(8,128)S(1)}, u32[]{:S(2)}, u32[]{:S(2)}) collective-permute-start(f32[2048,1024]{1,0:T(8,128)} %get-tuple-element.23), channel_id=1, source_target_pairs={{0,128},{128,0},{1,129},{129,1},{2,130},{130,2},{3,131},{131,3},{4... | collective-permute-start | bytes 25165832 | tf_op jit(solution)/shard_map/ppermute | solution.py:366
  38.2 80.9 %collective-permute-start.5 = (bf16[1024,512]{1,0:T(8,128)(2,1)S(1)}, bf16[1024,512]{1,0:T(8,128)(2,1)S(1)}, u32[]{:S(2)}, u32[]{:S(2)}) collective-permute-start(bf16[1024,512]{1,0:T(8,128)(2,1)S(1)} %get-tuple-element.22), channel_id=1, source_target_pairs={{0,128},{128,0},{1,129},{129,1},{2,130},{130,2},{3,131},{131,3},{4... | collective-permute-start | bytes 3145736 | tf_op jit(solution)/shard_map/ppermute | solution.py:366
  106.1 13.0 %collective-permute-start.3 = (f32[8,8,128]{2,1,0:T(8,128)S(1)}, f32[8,8,128]{2,1,0:T(8,128)S(1)}, u32[]{:S(2)}, u32[]{:S(2)}) collective-permute-start(f32[8,8,128]{2,1,0:T(8,128)S(1)} %all_to_all.33.received_ref.before_ref), channel_id=1, source_target_pairs={{0,128},{128,0},{1,129},{129,1},{2,130},{130,2},{3,131},{131,3},{4... | collective-permute-start | bytes 98312 | tf_op jit(solution)/shard_map/ppermute | solution.py:366
  114.3 4.8 %collective-permute-start.4 = (f32[8,8,128]{2,1,0:T(8,128)S(1)}, f32[8,8,128]{2,1,0:T(8,128)S(1)}, u32[]{:S(2)}, u32[]{:S(2)}) collective-permute-start(f32[8,8,128]{2,1,0:T(8,128)S(1)} %all_to_all.35.received_ref), channel_id=1, source_target_pairs={{0,128},{128,0},{1,129},{129,1},{2,130},{130,2},{3,131},{131,3},{4... | collective-permute-start | bytes 98312 | tf_op jit(solution)/shard_map/ppermute | solution.py:366
  124.8 1.4 %collective-permute-start.7 = (f32[16,128]{1,0:T(8,128)S(1)}, f32[16,128]{1,0:T(8,128)S(1)}, u32[]{:S(2)}, u32[]{:S(2)}) collective-permute-start(f32[16,128]{1,0:T(8,128)S(1)} %get-tuple-element.26.mine_ref), channel_id=1, source_target_pairs={{0,128},{128,0},{1,129},{129,1},{2,130},{130,2},{3,131},{131,3},{4... | collective-permute-start | bytes 24584 | tf_op jit(solution)/shard_map/ppermute | solution.py:366

commit v4 on v3

v4 whole, which is shorter than its diff:
```python
import functools
import math

import jax
import jax.numpy as jnp
from jax import lax
from jax.experimental import pallas as pl
from jax.experimental.pallas import tpu as pltpu
from jax.sharding import Mesh, PartitionSpec as P

VECTOR_WIDTH = 1024
ITERS = 3
SOFTMAX_HEAT = 0.05
EXPONENT = math.log2(math.e) / SOFTMAX_HEAT / VECTOR_WIDTH

LANES = 128
GROUP_ROWS = 8
CHUNK = 256
LONG = 512
TILE = 64
VMEM_LIMIT = 20 * 1024 * 1024
F32 = jnp.float32
BF16 = jnp.bfloat16

IN_VMEM = pl.BlockSpec(memory_space=pltpu.VMEM)


def params():
    return pltpu.CompilerParams(vmem_limit_bytes=VMEM_LIMIT)


def unit(values):
    scale = lax.rsqrt(jnp.mean(values * values, axis=-1, keepdims=True) + 1e-06)
    return (values * scale).astype(BF16)


def affinity(unit_centroids, unit_vectors):
    scores = lax.dot_general(
        unit_centroids, unit_vectors, (((1,), (1,)), ((), ())), preferred_element_type=F32
    )
    return jnp.exp2(scores * EXPONENT)


def share_kernel(values_ref, share_ref, rows_ref, sem):
    rows = share_ref.shape[0]
    first = pl.multiple_of(lax.axis_index("cx") * rows, rows)
    copy = pltpu.make_async_copy(values_ref.at[pl.ds(first, rows), :], rows_ref, sem)
    copy.start()
    copy.wait()
    share_ref[...] = unit(rows_ref[...])


def unit_share(values, shares):
    rows, width = values.shape[0] // shares, values.shape[1]
    return pl.pallas_call(
        share_kernel,
        out_shape=jax.ShapeDtypeStruct((rows, width), BF16),
        in_specs=[pl.BlockSpec(memory_space=pltpu.HBM)],
        out_specs=IN_VMEM,
        scratch_shapes=[pltpu.VMEM((rows, width), F32), pltpu.SemaphoreType.DMA(())],
        compiler_params=params(),
        cost_estimate=pl.CostEstimate(flops=4 * rows * width, bytes_accessed=6 * rows * width, transcendentals=0),
    )(pltpu.with_memory_space_constraint(values, pltpu.HBM))


def unit_kernel(values_ref, share_ref, unit_ref):
    unit_ref[...] = unit(values_ref[...])


def unit_rows(values, share):
    return pl.pallas_call(
        unit_kernel,
        out_shape=jax.ShapeDtypeStruct(values.shape, BF16),
        in_specs=[IN_VMEM, pl.BlockSpec(memory_space=pl.ANY)],
        out_specs=IN_VMEM,
        compiler_params=params(),
        cost_estimate=pl.CostEstimate(flops=4 * values.size, bytes_accessed=6 * values.size, transcendentals=0),
    )(values, share)


def own_scores_kernel(centroids_ref, vectors_ref, unit_ref, scores_ref):
    unit_ref[...] = unit(centroids_ref[...])
    scores_ref[...] = affinity(unit_ref[...], vectors_ref[...])


def own_scores(centroids, vectors):
    lists, width = centroids.shape
    block = vectors.shape[0]
    return pl.pallas_call(
        own_scores_kernel,
        grid=(lists // CHUNK,),
        out_shape=(
            jax.ShapeDtypeStruct((lists, width), BF16),
            jax.ShapeDtypeStruct((lists, block), F32),
        ),
        in_specs=[
            pl.BlockSpec((CHUNK, width), lambda i: (i, 0)),
            pl.BlockSpec((block, width), lambda i: (0, 0)),
        ],
        out_specs=(
            pl.BlockSpec((CHUNK, width), lambda i: (i, 0)),
            pl.BlockSpec((CHUNK, block), lambda i: (i, 0)),
        ),
        compiler_params=params(),
        cost_estimate=pl.CostEstimate(
            flops=2 * lists * width * block, bytes_accessed=8 * lists * width, transcendentals=lists * block
        ),
    )(centroids, vectors)


def scaled_lists(kt, row_scale, lists_total):
    totals = jnp.sum(kt * row_scale, axis=1, keepdims=True)
    return kt * ((1.0 / lists_total) / totals)


def place_mass(mass, hops, rows_ref, copies_ref):
    row = jnp.sum(mass, axis=0, keepdims=True)
    blocks = len(hops)
    per_block = row.shape[1] // blocks // LANES
    here = lax.axis_index("dp")
    for j, hop in enumerate(hops):
        first = lax.rem(here + hop, blocks) * per_block
        for i in range(per_block):
            at = (j * per_block + i) * LANES
            rows_ref[pl.ds(first + i, 1), :] = row[:, at : at + LANES]
    copies_ref[...] = jnp.broadcast_to(rows_ref[...][None], copies_ref.shape)


def relative_row(rows_ref, hops):
    blocks = len(hops)
    per_block = rows_ref.shape[0] // blocks
    here = lax.axis_index("dp")
    parts = []
    for hop in hops:
        first = lax.rem(here + hop, blocks) * per_block
        parts += [rows_ref[pl.ds(first + i, 1), :] for i in range(per_block)]
    return jnp.concatenate(parts, axis=1)


def sweep_lists(kt_ref, row_scale, lists, lists_total, scaled_ref=None):
    mass = jnp.zeros((GROUP_ROWS, kt_ref.shape[1]), F32)
    for t in range(lists.start, lists.stop, TILE):
        scaled = scaled_lists(kt_ref[pl.ds(t, TILE), :], row_scale, lists_total)
        mass = mass + jnp.sum(scaled.reshape(-1, GROUP_ROWS, scaled.shape[1]), axis=0)
        if scaled_ref is not None:
            scaled_ref[pl.ds(t, TILE), :] = scaled
    return mass


def chunks_of(lists, size=CHUNK):
    return [range(at, at + size) for at in range(0, lists, size)]


def near_kernel(centroids_ref, *refs):
    *vector_refs, scores_ref = refs
    block = vector_refs[0].shape[0]
    for chunk in chunks_of(scores_ref.shape[0], LONG):
        rows = pl.ds(chunk.start, LONG)
        for j, vector_ref in enumerate(vector_refs):
            scores_ref[rows, j * block : (j + 1) * block] = affinity(centroids_ref[rows, :], vector_ref[...])


def near_scores(unit_centroids, vectors):
    lists, width = unit_centroids.shape
    columns = sum(v.shape[0] for v in vectors)
    return pl.pallas_call(
        near_kernel,
        out_shape=jax.ShapeDtypeStruct((lists, columns), F32),
        in_specs=[IN_VMEM] * (1 + len(vectors)),
        out_specs=IN_VMEM,
        compiler_params=params(),
        cost_estimate=pl.CostEstimate(
            flops=2 * lists * width * columns, bytes_accessed=4 * lists * width, transcendentals=lists * columns
        ),
    )(unit_centroids, *vectors)


def first_kernel(hops, lists_total, blocks, centroids_ref, own_ref, near_ref, *refs):
    vector_refs = refs[:blocks]
    kt_ref, kt_send_ref, keep_ref, send_ref, copies_ref, slab_ref, rows_ref, sems = refs[blocks:]
    lists, slab = kt_ref.shape
    block = own_ref.shape[1]
    known = block + near_ref.shape[1]
    for j, vector_ref in enumerate(vector_refs[: len(hops) - 1]):
        slab_ref[pl.ds(j * block, block), :] = vector_ref[...]
    shares = vector_refs[len(hops) - 1 :]
    for j, share_ref in enumerate(shares):
        rows = share_ref.shape[0]
        at = lax.rem(lax.axis_index("cx") + j, len(shares)) * rows
        slab_ref[pl.ds(pl.multiple_of(known + at, rows), rows), :] = share_ref[...]
    half = keep_ref.shape[1]
    here = lax.axis_index("replica")
    keep_ref[...] = slab_ref[:, pl.ds(pl.multiple_of(here * half, half), half)]
    send_ref[...] = slab_ref[:, pl.ds(pl.multiple_of((1 - here) * half, half), half)]
    row_scale = jnp.full((1, slab), 1.0 / slab, F32)
    mass = jnp.zeros((GROUP_ROWS, slab), F32)
    sends = []
    for c, chunk in enumerate(chunks_of(lists, LONG)):
        rows = pl.ds(chunk.start, LONG)
        kt_ref[rows, :block] = own_ref[rows, :]
        kt_ref[rows, block:known] = near_ref[rows, :]
        kt_ref[rows, known:] = affinity(centroids_ref[rows, :], slab_ref[known:, :])
        sends.append(pltpu.make_async_copy(kt_ref.at[rows, :], kt_send_ref.at[rows, :], sems.at[c]))
        sends[-1].start()
        mass = mass + sweep_lists(kt_ref, row_scale, chunk, lists_total)
    place_mass(mass, hops, rows_ref, copies_ref)
    for send in sends:
        send.wait()


def first_sweep(unit_centroids, own, near, vectors, hops, lists_total, peers):
    lists, width = unit_centroids.shape
    slab = own.shape[1] * len(hops)
    rows = slab // LANES
    return pl.pallas_call(
        functools.partial(first_kernel, hops, lists_total, len(vectors)),
        out_shape=(
            jax.ShapeDtypeStruct((lists, slab), F32),
            pltpu.HBM((lists, slab), F32),
            *[jax.ShapeDtypeStruct((slab, width // 2), BF16)] * 2,
            jax.ShapeDtypeStruct((peers, rows, LANES), F32),
        ),
        in_specs=[IN_VMEM] * (3 + len(vectors)),
        out_specs=(IN_VMEM, pl.BlockSpec(memory_space=pltpu.HBM), IN_VMEM, IN_VMEM, IN_VMEM),
        scratch_shapes=[
            pltpu.VMEM((slab, width), BF16),
            pltpu.VMEM((rows, LANES), F32),
            pltpu.SemaphoreType.DMA((lists // LONG,)),
        ],
        compiler_params=params(),
        cost_estimate=pl.CostEstimate(
            flops=lists * width * slab // 2, bytes_accessed=6 * lists * slab, transcendentals=lists * slab // 4
        ),
    )(unit_centroids, own, near, *vectors)


def row_scale_of(received_ref, rows_ref, hops):
    totals = jnp.sum(received_ref[...], axis=0)
    rows_ref[...] = (1.0 / (totals.shape[0] * totals.shape[1])) / totals
    return relative_row(rows_ref, hops)


def sweep_kernel(hops, lists_total, received_ref, kt_ref, copies_ref, *refs):
    *scaled_refs, rows_ref = refs
    row_scale = row_scale_of(received_ref, rows_ref, hops)
    mass = sweep_lists(kt_ref, row_scale, range(kt_ref.shape[0]), lists_total, *scaled_refs)
    place_mass(mass, hops, rows_ref, copies_ref)


def next_sweep(received, kt, hops, lists_total, peers, last):
    lists, slab = kt.shape
    rows = slab // LANES
    outs = [jax.ShapeDtypeStruct((peers, rows, LANES), F32)] + [jax.ShapeDtypeStruct((lists, slab), F32)] * last
    return pl.pallas_call(
        functools.partial(sweep_kernel, hops, lists_total),
        out_shape=outs,
        in_specs=[IN_VMEM] * 2,
        out_specs=[IN_VMEM] * len(outs),
        scratch_shapes=[pltpu.VMEM((rows, LANES), F32)],
        compiler_params=params(),
        cost_estimate=pl.CostEstimate(flops=4 * lists * slab, bytes_accessed=4 * lists * slab, transcendentals=0),
    )(received, kt)


def to_row(column):
    return jnp.broadcast_to(column, (LANES, LANES)).T[:1, :]


def to_lanes(row):
    return jnp.broadcast_to(row, (LANES, LANES)).T


def own_update_kernel(hops, lists_total, received_ref, scaled_ref, slab_ref, out_ref, weights_ref, rows_ref):
    lists, slab = scaled_ref.shape
    scale = row_scale_of(received_ref, rows_ref, hops) * (slab * lists_total)
    for chunk in chunks_of(lists, LONG):
        rows = pl.ds(chunk.start, LONG)
        for t in range(chunk.start, chunk.stop, TILE):
            weights_ref[pl.ds(t, TILE), :] = (scaled_ref[pl.ds(t, TILE), :] * scale).astype(BF16)
        out_ref[rows, :] = jnp.dot(weights_ref[rows, :], slab_ref[...], preferred_element_type=F32)


def own_update(received, scaled, slab_vectors, hops, lists_total):
    lists, slab = scaled.shape
    width = slab_vectors.shape[1]
    return pl.pallas_call(
        functools.partial(own_update_kernel, hops, lists_total),
        out_shape=jax.ShapeDtypeStruct((lists, width), F32),
        in_specs=[IN_VMEM] * 3,
        out_specs=IN_VMEM,
        scratch_shapes=[pltpu.VMEM((lists, slab), BF16), pltpu.VMEM((slab // LANES, LANES), F32)],
        compiler_params=params(),
        cost_estimate=pl.CostEstimate(
            flops=2 * lists * width * slab, bytes_accessed=6 * lists * slab, transcendentals=0
        ),
    )(received, scaled, slab_vectors)


def other_update_kernel(
    hops, lists_total, before_ref, received_ref, slab_ref, earlier_ref, kt_ref,
    total_ref, squares_ref, incoming_ref, weights_ref, rows_ref, sems,
):
    lists, slab = kt_ref.shape
    copies = []
    for c, chunk in enumerate(chunks_of(lists)):
        rows = pl.ds(chunk.start, CHUNK)
        copies.append(pltpu.make_async_copy(kt_ref.at[rows, :], incoming_ref.at[rows, :], sems.at[c]))
        copies[-1].start()
    before_scale = row_scale_of(before_ref, rows_ref, hops)
    scale = row_scale_of(received_ref, rows_ref, hops) * (slab * lists_total)
    for chunk in chunks_of(lists, LONG):
        rows = pl.ds(chunk.start, LONG)
        for t in range(chunk.start, chunk.stop, TILE):
            if t % CHUNK == 0:
                copies[t // CHUNK].wait()
            scaled = scaled_lists(incoming_ref[pl.ds(t, TILE), :], before_scale, lists_total)
            weights_ref[pl.ds(t, TILE), :] = (scaled * scale).astype(BF16)
        total = jnp.dot(weights_ref[rows, :], slab_ref[...], preferred_element_type=F32)
        total = total + earlier_ref[rows, :]
        total_ref[rows, :] = total
        squares = jnp.sum(total * total, axis=1, keepdims=True)
        for k in range(LONG // LANES):
            at = chunk.start // LANES + k
            squares_ref[at : at + 1, :] = to_row(squares[k * LANES : (k + 1) * LANES])


def other_update(before, received, slab_vectors, earlier, kt, hops, lists_total):
    lists, slab = kt.shape
    width = slab_vectors.shape[1]
    return pl.pallas_call(
        functools.partial(other_update_kernel, hops, lists_total),
        out_shape=(
            jax.ShapeDtypeStruct((lists, width), F32),
            jax.ShapeDtypeStruct((lists // LANES, LANES), F32),
        ),
        in_specs=[IN_VMEM] * 4 + [pl.BlockSpec(memory_space=pltpu.HBM)],
        out_specs=(IN_VMEM, IN_VMEM),
        scratch_shapes=[
            pltpu.VMEM((lists, slab), F32),
            pltpu.VMEM((lists, slab), BF16),
            pltpu.VMEM((slab // LANES, LANES), F32),
            pltpu.SemaphoreType.DMA((lists // CHUNK,)),
        ],
        compiler_params=params(),
        cost_estimate=pl.CostEstimate(
            flops=2 * lists * width * slab, bytes_accessed=8 * lists * slab, transcendentals=0
        ),
    )(before, received, slab_vectors, earlier, kt)


def finish_kernel(numerators_ref, mine_ref, theirs_ref, out_ref, scaled_ref, sems):
    lists, width = numerators_ref.shape
    scales = lax.rsqrt((mine_ref[...] + theirs_ref[...]) / VECTOR_WIDTH + 1e-06)
    copies = []
    for c, chunk in enumerate(chunks_of(lists)):
        for k in range(CHUNK // LANES):
            at = chunk.start + k * LANES
            scale = to_lanes(scales[at // LANES : at // LANES + 1, :])
            for f in range(0, width, LANES):
                scaled_ref[at : at + LANES, f : f + LANES] = numerators_ref[at : at + LANES, f : f + LANES] * scale
        rows = pl.ds(chunk.start, CHUNK)
        copies.append(pltpu.make_async_copy(scaled_ref.at[rows, :], out_ref.at[rows, :], sems.at[c]))
        copies[-1].start()
    for copy in copies:
        copy.wait()


def finish(numerators, mine, theirs):
    lists, width = numerators.shape
    return pl.pallas_call(
        finish_kernel,
        out_shape=jax.ShapeDtypeStruct((lists, width), F32),
        in_specs=[IN_VMEM] * 3,
        out_specs=pl.BlockSpec(memory_space=pltpu.HBM),
        scratch_shapes=[
            pltpu.VMEM((lists, width), F32),
            pltpu.SemaphoreType.DMA((lists // CHUNK,)),
        ],
        compiler_params=params(),
        cost_estimate=pl.CostEstimate(flops=lists * width, bytes_accessed=8 * lists * width, transcendentals=0),
    )(numerators, mine, theirs)


def exchange(copies, axes):
    return lax.all_to_all(copies, axes, 0, 0, tiled=True)


def join_kernel(received_ref, copies_ref):
    copies_ref[...] = jnp.broadcast_to(jnp.sum(received_ref[...], axis=0)[None], copies_ref.shape)


def join(received, peers):
    return pl.pallas_call(
        join_kernel,
        out_shape=jax.ShapeDtypeStruct((peers,) + received.shape[1:], F32),
        in_specs=[IN_VMEM],
        out_specs=IN_VMEM,
        compiler_params=pltpu.CompilerParams(vmem_limit_bytes=1024 * 1024),
    )(received)


def sum_over_lists(copies):
    return exchange(join(exchange(copies, ("dp", "cx")), lax.axis_size("cz")), "cz")


def body(vectors, centroids):
    dp = lax.axis_size("dp")
    peers = dp * lax.axis_size("cx")
    lists_total = centroids.shape[0] * peers * lax.axis_size("cz")
    hops = (0, 1, dp - 1, 2)
    cx = lax.axis_size("cx")
    share = unit_share(vectors, cx)
    mine = unit_rows(vectors, share)
    from_hop = lambda x, axis, hop, size: lax.ppermute(x, axis, [((i + hop) % size, i) for i in range(size)])
    far = from_hop(share, "dp", hops[3], dp)
    far, ready = lax.optimization_barrier((far, mine))
    near = [from_hop(ready, "dp", hop, dp) for hop in hops[1:3]]
    far = [far] + [from_hop(far, "cx", hop, cx) for hop in range(1, cx)]
    unit_centroids, own = own_scores(centroids, mine)
    near_kt = near_scores(unit_centroids, near)
    kt, kt_sent, kept, sent, copies = first_sweep(
        unit_centroids, own, near_kt, [mine, *near, *far], hops, lists_total, peers
    )
    swapped = lambda x: lax.ppermute(x, "replica", [(0, 1), (1, 0)])
    other_kt, other_vectors = swapped(kt_sent), swapped(sent)
    received = sum_over_lists(copies)
    for sweep in range(1, ITERS):
        before = received
        copies, *scaled = next_sweep(before, kt, hops, lists_total, peers, sweep == ITERS - 1)
        received = sum_over_lists(copies)
    before, received = lax.optimization_barrier((before, received))
    other_before, other_received = swapped(before), swapped(received)
    own_numerators = own_update(received, scaled[0], kept, hops, lists_total)
    numerators, squares = other_update(
        other_before, other_received, other_vectors, own_numerators, other_kt, hops, lists_total
    )
    return finish(numerators, squares, swapped(squares))


def solution(mesh):
    cent = mesh.shape["cent"]
    split = Mesh(
        mesh.devices.reshape(mesh.shape["replica"], mesh.shape["dp"], 4, cent // 4),
        ("replica", "dp", "cx", "cz"),
    )
    placed = (P(("replica", "dp"), None), P(("dp", "cx", "cz"), None))
    return jax.shard_map(
        body, mesh=split, in_specs=placed, out_specs=P(("dp", "cx", "cz"), "replica"), check_vma=False
    )
```

time: 130 us -> 120 us (0.923)
  waiting for transfers between devices: 15.7 us -> 2.25 us
  starting transfers between devices: 16.3 us -> 25.3 us
  Pallas kernels: 28.5 us -> 23.4 us
  blocking collectives: 64.8 us -> 63.3 us
    ppermute x3 -> x6, waiting for transfers between devices: 14.9 us -> 1.41 us  [body(): lax.ppermute(x, axis, [((i + hop) % size, i) for i in range(size)])]
    ppermute x3 -> x6, starting transfers between devices: 5.89 us -> 12.1 us  [body(): lax.ppermute(x, axis, [((i + hop) % size, i) for i in range(size)])]
    pallas_call x6 -> x8, Pallas kernels: 25 us -> 19.9 us  [the longest x1 5.06 us: other_update(): pl.pallas_call(functools.partial(other_update_kernel, hops, lists_total),...]
    ppermute x5, starting transfers between devices: 10.4 us -> 13.2 us  [body(): swapped = lambda x: lax.ppermute(x, 'replica', [(0, 1), (1, 0)])]
    all_to_all x6, blocking collectives: 64.8 us -> 63.3 us  [exchange(): return lax.all_to_all(copies, axes, 0, 0, tiled=True)]
  transfers between devices with their start and end apart: 8 -> 11, of which waited for: 3 -> 3; matrix products, arithmetic and copies ran while one was open for 0% -> 0% of each run, Pallas kernels for 8% -> 9%
where the time goes in v4:
time: 120 us; the launch traced here: 119 us
  blocking collectives  63.3 us (53%)
  starting transfers between devices  25.3 us (21%)
  Pallas kernels  23.4 us (20%)
  local copies, waits for them, and re-layouts  4.61 us (4%)
  waiting for transfers between devices  2.25 us (2%)
    all_to_all x6, blocking collectives, exchange(): return lax.all_to_all(copies, axes, 0, 0, tiled=True)  63.3 us
    ppermute x5, starting transfers between devices, body(): swapped = lambda x: lax.ppermute(x, 'replica', [(0, 1), (1, 0)])  13.2 us
    ppermute x6, starting transfers between devices, body(): lax.ppermute(x, axis, [((i + hop) % size, i) for i in range(size)])  12.1 us
    pallas_call x1, Pallas kernels, other_update(): pl.pallas_call(functools.partial(other_update_kernel, hops, lists_total),...  5.06 us
    unnamed x4, local copies, waits for them, and re-layouts  4.61 us
    pallas_call x1, Pallas kernels, first_sweep(): pl.pallas_call(functools.partial(first_kernel, hops, lists_total, len(vec...  4.49 us
    pallas_call x1, Pallas kernels, own_scores(): pl.pallas_call(own_scores_kernel, grid=(lists // CHUNK,), out_shape=(jax....  3.24 us
    pallas_call x2, Pallas kernels, next_sweep(): pl.pallas_call(functools.partial(sweep_kernel, hops, lists_total), out_sh...  2.43 us
  transfers between devices with their start and end apart: 11, of which 3 were waited for; matrix products, arithmetic and copies ran while one was open for 0% of the time, Pallas kernels for 9%

profile of v4, /device:TPU:1, one launch (start us, length us, event | category | flops | bytes accessed | tf_op | source)
XLA Modules:
  0.0 119.1 jit_solution(18352663673323117940)
XLA Ops:
  1.1 3.8 %collective-permute-start = (bf16[64,1024]{1,0:T(8,128)(2,1)S(1)}, bf16[64,1024]{1,0:T(8,128)(2,1)S(1)}, u32[]{:S(2)}, u32[]{:S(2)}) collective-permute-start(bf16[64,1024]{1,0:T(8,128)(2,1)S(1)} %shard_map.28.share_ref), channel_id=1, source_target_pairs={{64,0},{96,32},{0,64},{32,96},{65,1},{97,33},{1,65},{33,97},{66,2}... | collective-permute-start | bytes 393224 | tf_op jit(solution)/shard_map/ppermute | solution.py:414
  4.9 1.2 %copy-done.1 = f32[256,1024]{1,0:T(8,128)S(1)} copy-done((f32[256,1024]{1,0:T(8,128)S(1)}, f32[256,1024]{1,0:T(8,128)}, u32[]{:S(2)}) %copy-start.1) | copy-done | bytes 1048600
  7.3 1.9 %collective-permute-start.2 = (bf16[256,1024]{1,0:T(8,128)(2,1)S(1)}, bf16[256,1024]{1,0:T(8,128)(2,1)S(1)}, u32[]{:S(2)}, u32[]{:S(2)}) collective-permute-start(bf16[256,1024]{1,0:T(8,128)(2,1)S(1)} %shard_map.29.vectors_ref.refs_0_), channel_id=1, source_target_pairs={{96,0},{0,32},{32,64},{64,96},{97,1},{1,33},{33,65},{65,97},{98,2}... | collective-permute-start | bytes 1572872 | tf_op jit(solution)/shard_map/ppermute | solution.py:414
  9.2 1.4 %collective-permute-start.1 = (bf16[256,1024]{1,0:T(8,128)(2,1)S(1)}, bf16[256,1024]{1,0:T(8,128)(2,1)S(1)}, u32[]{:S(2)}, u32[]{:S(2)}) collective-permute-start(bf16[256,1024]{1,0:T(8,128)(2,1)S(1)} %shard_map.29.vectors_ref.refs_0_), channel_id=1, source_target_pairs={{32,0},{64,32},{96,64},{0,96},{33,1},{65,33},{97,65},{1,97},{34,2}... | collective-permute-start | bytes 1572872 | tf_op jit(solution)/shard_map/ppermute | solution.py:414
  10.6 3.4 %copy-done = f32[2048,1024]{1,0:T(8,128)S(1)} copy-done((f32[2048,1024]{1,0:T(8,128)S(1)}, f32[2048,1024]{1,0:T(8,128)}, u32[]{:S(2)}) %copy-start) | copy-done | bytes 8388632
  14.0 3.2 %shard_map.30 = (bf16[2048,1024]{1,0:T(8,128)(2,1)S(1)}, f32[2048,256]{1,0:T(8,128)S(1)}) custom-call(f32[2048,1024]{1,0:T(8,128)S(1)} %copy-done, bf16[256,1024]{1,0:T(8,128)(2,1)S(1)} %shard_map.29.vectors_ref.refs_0_), custom_call_target="tpu_custom_call" | custom-call | flops 1073741824 | bytes 16777216 | tf_op jit(solution)/shard_map/pallas_call | solution.py:89
  17.2 1.3 %collective-permute-start.5 = (bf16[64,1024]{1,0:T(8,128)(2,1)S(1)}, bf16[64,1024]{1,0:T(8,128)(2,1)S(1)}, u32[]{:S(2)}, u32[]{:S(2)}) collective-permute-start(bf16[64,1024]{1,0:T(8,128)(2,1)S(1)} %collective-permute-done.refs_3_), channel_id=1, source_target_pairs={{24,0},{0,8},{8,16},{16,24},{25,1},{1,9},{9,17},{17,25},{26,2},{2,... | collective-permute-start | bytes 393224 | tf_op jit(solution)/shard_map/ppermute | solution.py:414
  18.5 2.5 %collective-permute-start.4 = (bf16[64,1024]{1,0:T(8,128)(2,1)S(1)}, bf16[64,1024]{1,0:T(8,128)(2,1)S(1)}, u32[]{:S(2)}, u32[]{:S(2)}) collective-permute-start(bf16[64,1024]{1,0:T(8,128)(2,1)S(1)} %collective-permute-done.refs_3_), channel_id=1, source_target_pairs={{16,0},{24,8},{0,16},{8,24},{17,1},{25,9},{1,17},{9,25},{18,2},{26... | collective-permute-start | bytes 393224 | tf_op jit(solution)/shard_map/ppermute | solution.py:414
  21.0 1.2 collective-permute-start.3
  22.1 2.4 %shard_map.31.near_ref = f32[2048,512]{1,0:T(8,128)S(1)} custom-call(bf16[2048,1024]{1,0:T(8,128)(2,1)S(1)} %get-tuple-element.20.centroids_ref, bf16[256,1024]{1,0:T(8,128)(2,1)S(1)} %collective-permute-done.1.refs_0_.refs_1_, bf16[256,1024]{1,0:T(8,128)(2,1)S(1)} %collective-permute-done.2.refs_1_.refs_2_), custom_call_target="tpu_custom_call" | custom-call | flops 2147483648 | bytes 8388608 | tf_op jit(solution)/shard_map/pallas_call | solution.py:166
  25.0 4.5 %shard_map.32 = (f32[2048,1024]{1,0:T(8,128)S(1)}, f32[2048,1024]{1,0:T(8,128)}, bf16[1024,512]{1,0:T(8,128)(2,1)S(1)}, bf16[1024,512]{1,0:T(8,128)(2,1)S(1)}, f32[16,8,128]{2,1,0:T(8,128)S(1)}) custom-call(bf16[2048,1024]{1,0:T(8,128)(2,1)S(1)} %get-tuple-element.20.centroids_ref, f32[2048,256]{1,0:T(8,128)S(1)} %get-tuple-element.21.own_ref, ...), custom_call_target="tpu_custom_call" | custom-call | flops 1073741824 | bytes 12582912 | tf_op jit(solution)/shard_map/pallas_call | solution.py:215
  29.5 4.4 %collective-permute-start.9 = (f32[2048,1024]{1,0:T(8,128)}, f32[2048,1024]{1,0:T(8,128)S(1)}, u32[]{:S(2)}, u32[]{:S(2)}) collective-permute-start(f32[2048,1024]{1,0:T(8,128)} %get-tuple-element.32), channel_id=1, source_target_pairs={{0,128},{128,0},{1,129},{129,1},{2,130},{130,2},{3,131},{131,3},{4... | collective-permute-start | bytes 25165832 | tf_op jit(solution)/shard_map/ppermute | solution.py:424
  33.9 10.8 %all_to_all.30.received_ref = f32[16,8,128]{2,1,0:T(8,128)S(1)} all-to-all(f32[16,8,128]{2,1,0:T(8,128)S(1)} %get-tuple-element.24), channel_id=1, replica_groups=mesh['replica'=2,'dp'=4,'cx'=4,'cz'=8] {'dp','cx'}, dimensions={0} | all-to-all | bytes 131072 | tf_op jit(solution)/shard_map/all_to_all | solution.py:385
  44.7 14.9 %all_to_all.31.received_ref = f32[8,8,128]{2,1,0:T(8,128)S(1)} all-to-all(f32[8,8,128]{2,1,0:T(8,128)S(1)} %shard_map.33), channel_id=1, replica_groups=mesh['replica'=2,'dp'=4,'cx'=4,'cz'=8] {'cz'}, dimensions={0} | all-to-all | bytes 65536 | tf_op jit(solution)/shard_map/all_to_all | solution.py:385
  59.6 1.2 shard_map.34
  60.7 9.8 %all_to_all.32.received_ref = f32[16,8,128]{2,1,0:T(8,128)S(1)} all-to-all(f32[16,8,128]{2,1,0:T(8,128)S(1)} %shard_map.34), channel_id=1, replica_groups=mesh['replica'=2,'dp'=4,'cx'=4,'cz'=8] {'dp','cx'}, dimensions={0} | all-to-all | bytes 131072 | tf_op jit(solution)/shard_map/all_to_all | solution.py:385
  70.6 9.2 %all_to_all.33.received_ref = f32[8,8,128]{2,1,0:T(8,128)S(1)} all-to-all(f32[8,8,128]{2,1,0:T(8,128)S(1)} %shard_map.35), channel_id=1, replica_groups=mesh['replica'=2,'dp'=4,'cx'=4,'cz'=8] {'cz'}, dimensions={0} | all-to-all | bytes 65536 | tf_op jit(solution)/shard_map/all_to_all | solution.py:385
  79.9 1.3 %shard_map.36 = (f32[16,8,128]{2,1,0:T(8,128)S(1)}, f32[2048,1024]{1,0:T(8,128)S(1)}) custom-call(f32[8,8,128]{2,1,0:T(8,128)S(1)} %all_to_all.33.received_ref, f32[2048,1024]{1,0:T(8,128)S(1)} %get-tuple-element.25.kt_ref), custom_call_target="tpu_custom_call" | custom-call | flops 8388608 | bytes 8388608 | tf_op jit(solution)/shard_map/pallas_call | solution.py:254
  81.1 9.4 %all_to_all.34.received_ref = f32[16,8,128]{2,1,0:T(8,128)S(1)} all-to-all(f32[16,8,128]{2,1,0:T(8,128)S(1)} %get-tuple-element.26), channel_id=1, replica_groups=mesh['replica'=2,'dp'=4,'cx'=4,'cz'=8] {'dp','cx'}, dimensions={0} | all-to-all | bytes 131072 | tf_op jit(solution)/shard_map/all_to_all | solution.py:385
  90.5 9.2 %all_to_all.35.received_ref = f32[8,8,128]{2,1,0:T(8,128)S(1)} all-to-all(f32[8,8,128]{2,1,0:T(8,128)S(1)} %shard_map.37), channel_id=1, replica_groups=mesh['replica'=2,'dp'=4,'cx'=4,'cz'=8] {'cz'}, dimensions={0} | all-to-all | bytes 65536 | tf_op jit(solution)/shard_map/all_to_all | solution.py:385
  99.8 8.1 %collective-permute-start.6 = (f32[8,8,128]{2,1,0:T(8,128)S(1)}, f32[8,8,128]{2,1,0:T(8,128)S(1)}, u32[]{:S(2)}, u32[]{:S(2)}) collective-permute-start(f32[8,8,128]{2,1,0:T(8,128)S(1)} %all_to_all.33.received_ref), channel_id=1, source_target_pairs={{0,128},{128,0},{1,129},{129,1},{2,130},{130,2},{3,131},{131,3},{4... | collective-permute-start | bytes 98312 | tf_op jit(solution)/shard_map/ppermute | solution.py:424
  107.9 2.3 %shard_map.38.earlier_ref = f32[2048,512]{1,0:T(8,128)S(1)} custom-call(f32[8,8,128]{2,1,0:T(8,128)S(1)} %all_to_all.35.received_ref, f32[2048,1024]{1,0:T(8,128)S(1)} %get-tuple-element.30.scaled_ref, bf16[1024,512]{1,0:T(8,128)(2,1)S(1)} %get-tuple-element.31.slab_ref), custom_call_target="tpu_custom_call" | custom-call | flops 2147483648 | bytes 12582912 | tf_op jit(solution)/shard_map/pallas_call | solution.py:286
  110.3 5.1 %shard_map.39 = (f32[2048,512]{1,0:T(8,128)S(1)}, f32[16,128]{1,0:T(8,128)S(1)}) custom-call(f32[8,8,128]{2,1,0:T(8,128)S(1)} %collective-permute-done.6.before_ref, f32[8,8,128]{2,1,0:T(8,128)S(1)} %collective-permute-done.7.received_ref, bf16[1024,512]{1,0:T(8,128)(2,1)S(1)} %collective-permute-done.8.slab_ref, f32[2048,512]{1,0:T(8,128)S(1)} %shard_map.38.earlier_ref, ...), custom_call_target="tpu_custom_call" | custom-call | flops 2147483648 | bytes 16777216 | tf_op jit(solution)/shard_map/pallas_call | solution.py:330
  116.8 2.2 %shard_map.40 = f32[2048,512]{1,0:T(8,128)} custom-call(f32[2048,512]{1,0:T(8,128)S(1)} %get-tuple-element.33.numerators_ref, f32[16,128]{1,0:T(8,128)S(1)} %get-tuple-element.34.mine_ref, f32[16,128]{1,0:T(8,128)S(1)} %collective-permute-done.10.theirs_ref), custom_call_target="tpu_custom_call" | custom-call | flops 1048576 | bytes 8388608 | tf_op jit(solution)/shard_map/pallas_call | solution.py:370
  (21 shorter events, 4.2 us)
Async XLA Ops:
  1.1 6.2 %collective-permute-start = (bf16[64,1024]{1,0:T(8,128)(2,1)S(1)}, bf16[64,1024]{1,0:T(8,128)(2,1)S(1)}, u32[]{:S(2)}, u32[]{:S(2)}) collective-permute-start(bf16[64,1024]{1,0:T(8,128)(2,1)S(1)} %shard_map.28.share_ref), channel_id=1, source_target_pairs={{64,0},{96,32},{0,64},{32,96},{65,1},{97,33},{1,65},{33,97},{66,2}... | collective-permute-start | bytes 393224 | tf_op jit(solution)/shard_map/ppermute | solution.py:414
  4.9 1.2 %copy-start.1 = (f32[256,1024]{1,0:T(8,128)S(1)}, f32[256,1024]{1,0:T(8,128)}, u32[]{:S(2)}) copy-start(f32[256,1024]{1,0:T(8,128)} %values_ref.3) | copy-start | bytes 3145732
  7.3 14.9 %collective-permute-start.2 = (bf16[256,1024]{1,0:T(8,128)(2,1)S(1)}, bf16[256,1024]{1,0:T(8,128)(2,1)S(1)}, u32[]{:S(2)}, u32[]{:S(2)}) collective-permute-start(bf16[256,1024]{1,0:T(8,128)(2,1)S(1)} %shard_map.29.vectors_ref.refs_0_), channel_id=1, source_target_pairs={{96,0},{0,32},{32,64},{64,96},{97,1},{1,33},{33,65},{65,97},{98,2}... | collective-permute-start | bytes 1572872 | tf_op jit(solution)/shard_map/ppermute | solution.py:414
  9.2 13.0 %collective-permute-start.1 = (bf16[256,1024]{1,0:T(8,128)(2,1)S(1)}, bf16[256,1024]{1,0:T(8,128)(2,1)S(1)}, u32[]{:S(2)}, u32[]{:S(2)}) collective-permute-start(bf16[256,1024]{1,0:T(8,128)(2,1)S(1)} %shard_map.29.vectors_ref.refs_0_), channel_id=1, source_target_pairs={{32,0},{64,32},{96,64},{0,96},{33,1},{65,33},{97,65},{1,97},{34,2}... | collective-permute-start | bytes 1572872 | tf_op jit(solution)/shard_map/ppermute | solution.py:414
  10.6 3.4 %copy-start = (f32[2048,1024]{1,0:T(8,128)S(1)}, f32[2048,1024]{1,0:T(8,128)}, u32[]{:S(2)}) copy-start(f32[2048,1024]{1,0:T(8,128)} %centroids_ref.1) | copy-start | bytes 25165828
  17.2 7.3 %collective-permute-start.5 = (bf16[64,1024]{1,0:T(8,128)(2,1)S(1)}, bf16[64,1024]{1,0:T(8,128)(2,1)S(1)}, u32[]{:S(2)}, u32[]{:S(2)}) collective-permute-start(bf16[64,1024]{1,0:T(8,128)(2,1)S(1)} %collective-permute-done.refs_3_), channel_id=1, source_target_pairs={{24,0},{0,8},{8,16},{16,24},{25,1},{1,9},{9,17},{17,25},{26,2},{2,... | collective-permute-start | bytes 393224 | tf_op jit(solution)/shard_map/ppermute | solution.py:414
  18.5 6.4 %collective-permute-start.4 = (bf16[64,1024]{1,0:T(8,128)(2,1)S(1)}, bf16[64,1024]{1,0:T(8,128)(2,1)S(1)}, u32[]{:S(2)}, u32[]{:S(2)}) collective-permute-start(bf16[64,1024]{1,0:T(8,128)(2,1)S(1)} %collective-permute-done.refs_3_), channel_id=1, source_target_pairs={{16,0},{24,8},{0,16},{8,24},{17,1},{25,9},{1,17},{9,25},{18,2},{26... | collective-permute-start | bytes 393224 | tf_op jit(solution)/shard_map/ppermute | solution.py:414
  21.0 4.0 %collective-permute-start.3 = (bf16[64,1024]{1,0:T(8,128)(2,1)S(1)}, bf16[64,1024]{1,0:T(8,128)(2,1)S(1)}, u32[]{:S(2)}, u32[]{:S(2)}) collective-permute-start(bf16[64,1024]{1,0:T(8,128)(2,1)S(1)} %collective-permute-done.refs_3_), channel_id=1, source_target_pairs={{8,0},{16,8},{24,16},{0,24},{9,1},{17,9},{25,17},{1,25},{10,2},{18... | collective-permute-start | bytes 393224 | tf_op jit(solution)/shard_map/ppermute | solution.py:414
  29.5 80.8 %collective-permute-start.9 = (f32[2048,1024]{1,0:T(8,128)}, f32[2048,1024]{1,0:T(8,128)S(1)}, u32[]{:S(2)}, u32[]{:S(2)}) collective-permute-start(f32[2048,1024]{1,0:T(8,128)} %get-tuple-element.32), channel_id=1, source_target_pairs={{0,128},{128,0},{1,129},{129,1},{2,130},{130,2},{3,131},{131,3},{4... | collective-permute-start | bytes 25165832 | tf_op jit(solution)/shard_map/ppermute | solution.py:424
  33.8 76.4 %collective-permute-start.8 = (bf16[1024,512]{1,0:T(8,128)(2,1)S(1)}, bf16[1024,512]{1,0:T(8,128)(2,1)S(1)}, u32[]{:S(2)}, u32[]{:S(2)}) collective-permute-start(bf16[1024,512]{1,0:T(8,128)(2,1)S(1)} %get-tuple-element.29), channel_id=1, source_target_pairs={{0,128},{128,0},{1,129},{129,1},{2,130},{130,2},{3,131},{131,3},{4... | collective-permute-start | bytes 3145736 | tf_op jit(solution)/shard_map/ppermute | solution.py:424
  99.8 10.5 %collective-permute-start.6 = (f32[8,8,128]{2,1,0:T(8,128)S(1)}, f32[8,8,128]{2,1,0:T(8,128)S(1)}, u32[]{:S(2)}, u32[]{:S(2)}) collective-permute-start(f32[8,8,128]{2,1,0:T(8,128)S(1)} %all_to_all.33.received_ref), channel_id=1, source_target_pairs={{0,128},{128,0},{1,129},{129,1},{2,130},{130,2},{3,131},{131,3},{4... | collective-permute-start | bytes 98312 | tf_op jit(solution)/shard_map/ppermute | solution.py:424
  107.9 2.4 %collective-permute-start.7 = (f32[8,8,128]{2,1,0:T(8,128)S(1)}, f32[8,8,128]{2,1,0:T(8,128)S(1)}, u32[]{:S(2)}, u32[]{:S(2)}) collective-permute-start(f32[8,8,128]{2,1,0:T(8,128)S(1)} %all_to_all.35.received_ref), channel_id=1, source_target_pairs={{0,128},{128,0},{1,129},{129,1},{2,130},{130,2},{3,131},{131,3},{4... | collective-permute-start | bytes 98312 | tf_op jit(solution)/shard_map/ppermute | solution.py:424
  115.3 1.4 %collective-permute-start.10 = (f32[16,128]{1,0:T(8,128)S(1)}, f32[16,128]{1,0:T(8,128)S(1)}, u32[]{:S(2)}, u32[]{:S(2)}) collective-permute-start(f32[16,128]{1,0:T(8,128)S(1)} %get-tuple-element.34.mine_ref), channel_id=1, source_target_pairs={{0,128},{128,0},{1,129},{129,1},{2,130},{130,2},{3,131},{131,3},{4... | collective-permute-start | bytes 24584 | tf_op jit(solution)/shard_map/ppermute | solution.py:424

commit v5 on v4

--- a/solution.py
+++ b/solution.py
@@ -78,34 +78,34 @@
     )(values, share)
 
 
-def own_scores_kernel(centroids_ref, vectors_ref, unit_ref, scores_ref):
-    unit_ref[...] = unit(centroids_ref[...])
-    scores_ref[...] = affinity(unit_ref[...], vectors_ref[...])
-
-
-def own_scores(centroids, vectors):
+def stream_in(source_ref, held_ref, sems):
+    copies = []
+    for c, chunk in enumerate(chunks_of(source_ref.shape[0])):
+        rows = pl.ds(chunk.start, CHUNK)
+        copies.append(pltpu.make_async_copy(source_ref.at[rows, :], held_ref.at[rows, :], sems.at[c]))
+        copies[-1].start()
+    return copies
+
+
+def centroids_kernel(centroids_ref, unit_ref, held_ref, sems):
+    copies = stream_in(centroids_ref, held_ref, sems)
+    for c, chunk in enumerate(chunks_of(centroids_ref.shape[0])):
+        copies[c].wait()
+        for t in range(chunk.start, chunk.stop, TILE):
+            unit_ref[pl.ds(t, TILE), :] = unit(held_ref[pl.ds(t, TILE), :])
+
+
+def unit_lists(centroids):
     lists, width = centroids.shape
-    block = vectors.shape[0]
-    return pl.pallas_call(
-        own_scores_kernel,
-        grid=(lists // CHUNK,),
-        out_shape=(
-            jax.ShapeDtypeStruct((lists, width), BF16),
-            jax.ShapeDtypeStruct((lists, block), F32),
-        ),
-        in_specs=[
-            pl.BlockSpec((CHUNK, width), lambda i: (i, 0)),
-            pl.BlockSpec((block, width), lambda i: (0, 0)),
-        ],
-        out_specs=(
-            pl.BlockSpec((CHUNK, width), lambda i: (i, 0)),
-            pl.BlockSpec((CHUNK, block), lambda i: (i, 0)),
-        ),
-        compiler_params=params(),
-        cost_estimate=pl.CostEstimate(
-            flops=2 * lists * width * block, bytes_accessed=8 * lists * width, transcendentals=lists * block
-        ),
-    )(centroids, vectors)
+    return pl.pallas_call(
+        centroids_kernel,
+        out_shape=jax.ShapeDtypeStruct((lists, width), BF16),
+        in_specs=[pl.BlockSpec(memory_space=pltpu.HBM)],
+        out_specs=IN_VMEM,
+        scratch_shapes=[pltpu.VMEM((lists, width), F32), pltpu.SemaphoreType.DMA((lists // CHUNK,))],
+        compiler_params=params(),
+        cost_estimate=pl.CostEstimate(flops=4 * lists * width, bytes_accessed=6 * lists * width, transcendentals=0),
+    )(pltpu.with_memory_space_constraint(centroids, pltpu.HBM))
 
 
 def scaled_lists(kt, row_scale, lists_total):
@@ -151,43 +151,62 @@
     return [range(at, at + size) for at in range(0, lists, size)]
 
 
-def near_kernel(centroids_ref, *refs):
-    *vector_refs, scores_ref = refs
-    block = vector_refs[0].shape[0]
+def score_lists(centroids_ref, vectors_ref, scores_ref):
     for chunk in chunks_of(scores_ref.shape[0], LONG):
         rows = pl.ds(chunk.start, LONG)
-        for j, vector_ref in enumerate(vector_refs):
-            scores_ref[rows, j * block : (j + 1) * block] = affinity(centroids_ref[rows, :], vector_ref[...])
-
-
-def near_scores(unit_centroids, vectors):
+        scores_ref[rows, :] = affinity(centroids_ref[rows, :], vectors_ref[...])
+
+
+def far_kernel(centroids_ref, *refs):
+    *share_refs, vectors_ref, scores_ref = refs
+    for j, share_ref in enumerate(share_refs):
+        rows = share_ref.shape[0]
+        at = lax.rem(lax.axis_index("cx") + j, len(share_refs)) * rows
+        vectors_ref[pl.ds(pl.multiple_of(at, rows), rows), :] = share_ref[...]
+    score_lists(centroids_ref, vectors_ref, scores_ref)
+
+
+def score_cost(lists, width, columns):
+    return pl.CostEstimate(
+        flops=2 * lists * width * columns, bytes_accessed=4 * lists * width, transcendentals=lists * columns
+    )
+
+
+def block_scores(unit_centroids, vectors):
     lists, width = unit_centroids.shape
-    columns = sum(v.shape[0] for v in vectors)
-    return pl.pallas_call(
-        near_kernel,
-        out_shape=jax.ShapeDtypeStruct((lists, columns), F32),
-        in_specs=[IN_VMEM] * (1 + len(vectors)),
+    block = vectors.shape[0]
+    return pl.pallas_call(
+        score_lists,
+        out_shape=jax.ShapeDtypeStruct((lists, block), F32),
+        in_specs=[IN_VMEM] * 2,
         out_specs=IN_VMEM,
         compiler_params=params(),
-        cost_estimate=pl.CostEstimate(
-            flops=2 * lists * width * columns, bytes_accessed=4 * lists * width, transcendentals=lists * columns
-        ),
-    )(unit_centroids, *vectors)
-
-
-def first_kernel(hops, lists_total, blocks, centroids_ref, own_ref, near_ref, *refs):
+        cost_estimate=score_cost(lists, width, block),
+    )(unit_centroids, vectors)
+
+
+def far_scores(unit_centroids, shares):
+    lists, width = unit_centroids.shape
+    block = shares[0].shape[0] * len(shares)
+    return pl.pallas_call(
+        far_kernel,
+        out_shape=(jax.ShapeDtypeStruct((block, width), BF16), jax.ShapeDtypeStruct((lists, block), F32)),
+        in_specs=[IN_VMEM] * (1 + len(shares)),
+        out_specs=(IN_VMEM, IN_VMEM),
+        compiler_params=params(),
+        cost_estimate=score_cost(lists, width, block),
+    )(unit_centroids, *shares)
+
+
+def first_kernel(hops, lists_total, centroids_ref, own_ref, far_ref, *refs):
+    blocks = len(hops)
     vector_refs = refs[:blocks]
     kt_ref, kt_send_ref, keep_ref, send_ref, copies_ref, slab_ref, rows_ref, sems = refs[blocks:]
     lists, slab = kt_ref.shape
     block = own_ref.shape[1]
-    known = block + near_ref.shape[1]
-    for j, vector_ref in enumerate(vector_refs[: len(hops) - 1]):
+    known = block + far_ref.shape[1]
+    for j, vector_ref in enumerate(vector_refs):
         slab_ref[pl.ds(j * block, block), :] = vector_ref[...]
-    shares = vector_refs[len(hops) - 1 :]
-    for j, share_ref in enumerate(shares):
-        rows = share_ref.shape[0]
-        at = lax.rem(lax.axis_index("cx") + j, len(shares)) * rows
-        slab_ref[pl.ds(pl.multiple_of(known + at, rows), rows), :] = share_ref[...]
     half = keep_ref.shape[1]
     here = lax.axis_index("replica")
     keep_ref[...] = slab_ref[:, pl.ds(pl.multiple_of(here * half, half), half)]
@@ -198,7 +217,7 @@
     for c, chunk in enumerate(chunks_of(lists, LONG)):
         rows = pl.ds(chunk.start, LONG)
         kt_ref[rows, :block] = own_ref[rows, :]
-        kt_ref[rows, block:known] = near_ref[rows, :]
+        kt_ref[rows, block:known] = far_ref[rows, :]
         kt_ref[rows, known:] = affinity(centroids_ref[rows, :], slab_ref[known:, :])
         sends.append(pltpu.make_async_copy(kt_ref.at[rows, :], kt_send_ref.at[rows, :], sems.at[c]))
         sends[-1].start()
@@ -208,12 +227,12 @@
         send.wait()
 
 
-def first_sweep(unit_centroids, own, near, vectors, hops, lists_total, peers):
+def first_sweep(unit_centroids, own, far, vectors, hops, lists_total, peers):
     lists, width = unit_centroids.shape
     slab = own.shape[1] * len(hops)
     rows = slab // LANES
     return pl.pallas_call(
-        functools.partial(first_kernel, hops, lists_total, len(vectors)),
+        functools.partial(first_kernel, hops, lists_total),
         out_shape=(
             jax.ShapeDtypeStruct((lists, slab), F32),
             pltpu.HBM((lists, slab), F32),
@@ -229,9 +248,9 @@
         ],
         compiler_params=params(),
         cost_estimate=pl.CostEstimate(
-            flops=lists * width * slab // 2, bytes_accessed=6 * lists * slab, transcendentals=lists * slab // 4
+            flops=lists * width * slab, bytes_accessed=6 * lists * slab, transcendentals=lists * slab // 2
         ),
-    )(unit_centroids, own, near, *vectors)
+    )(unit_centroids, own, far, *vectors)
 
 
 def row_scale_of(received_ref, rows_ref, hops):
@@ -270,51 +289,59 @@
     return jnp.broadcast_to(row, (LANES, LANES)).T
 
 
-def own_update_kernel(hops, lists_total, received_ref, scaled_ref, slab_ref, out_ref, weights_ref, rows_ref):
+def write_weights(scaled_ref, scale, weights_ref, lists):
+    for t in range(lists.start, lists.stop, TILE):
+        weights_ref[pl.ds(t, TILE), :] = (scaled_ref[pl.ds(t, TILE), :] * scale).astype(BF16)
+
+
+def own_update_kernel(
+    hops, lists_total, received_ref, scaled_ref, slab_ref, other_before_ref, other_kt_ref,
+    out_ref, other_scaled_ref, weights_ref, rows_ref, sems,
+):
+    lists, slab = scaled_ref.shape
+    copies = stream_in(other_kt_ref, other_scaled_ref, sems)
+    scale = row_scale_of(received_ref, rows_ref, hops) * (slab * lists_total)
+    other_before_scale = row_scale_of(other_before_ref, rows_ref, hops)
+    for chunk in chunks_of(lists, LONG):
+        rows = pl.ds(chunk.start, LONG)
+        write_weights(scaled_ref, scale, weights_ref, chunk)
+        out_ref[rows, :] = jnp.dot(weights_ref[rows, :], slab_ref[...], preferred_element_type=F32)
+    for c, chunk in enumerate(chunks_of(lists)):
+        copies[c].wait()
+        for t in range(chunk.start, chunk.stop, TILE):
+            rows = pl.ds(t, TILE)
+            other_scaled_ref[rows, :] = scaled_lists(other_scaled_ref[rows, :], other_before_scale, lists_total)
+
+
+def own_update(received, scaled, slab_vectors, other_before, other_kt, hops, lists_total):
+    lists, slab = scaled.shape
+    width = slab_vectors.shape[1]
+    return pl.pallas_call(
+        functools.partial(own_update_kernel, hops, lists_total),
+        out_shape=(jax.ShapeDtypeStruct((lists, width), F32), jax.ShapeDtypeStruct((lists, slab), F32)),
+        in_specs=[IN_VMEM] * 4 + [pl.BlockSpec(memory_space=pltpu.HBM)],
+        out_specs=(IN_VMEM, IN_VMEM),
+        scratch_shapes=[
+            pltpu.VMEM((lists, slab), BF16),
+            pltpu.VMEM((slab // LANES, LANES), F32),
+            pltpu.SemaphoreType.DMA((lists // CHUNK,)),
+        ],
+        compiler_params=params(),
+        cost_estimate=pl.CostEstimate(
+            flops=2 * lists * width * slab, bytes_accessed=6 * lists * slab, transcendentals=0
+        ),
+    )(received, scaled, slab_vectors, other_before, other_kt)
+
+
+def other_update_kernel(
+    hops, lists_total, received_ref, scaled_ref, slab_ref, earlier_ref,
+    total_ref, squares_ref, weights_ref, rows_ref,
+):
     lists, slab = scaled_ref.shape
     scale = row_scale_of(received_ref, rows_ref, hops) * (slab * lists_total)
     for chunk in chunks_of(lists, LONG):
         rows = pl.ds(chunk.start, LONG)
-        for t in range(chunk.start, chunk.stop, TILE):
-            weights_ref[pl.ds(t, TILE), :] = (scaled_ref[pl.ds(t, TILE), :] * scale).astype(BF16)
-        out_ref[rows, :] = jnp.dot(weights_ref[rows, :], slab_ref[...], preferred_element_type=F32)
-
-
-def own_update(received, scaled, slab_vectors, hops, lists_total):
-    lists, slab = scaled.shape
-    width = slab_vectors.shape[1]
-    return pl.pallas_call(
-        functools.partial(own_update_kernel, hops, lists_total),
-        out_shape=jax.ShapeDtypeStruct((lists, width), F32),
-        in_specs=[IN_VMEM] * 3,
-        out_specs=IN_VMEM,
-        scratch_shapes=[pltpu.VMEM((lists, slab), BF16), pltpu.VMEM((slab // LANES, LANES), F32)],
-        compiler_params=params(),
-        cost_estimate=pl.CostEstimate(
-            flops=2 * lists * width * slab, bytes_accessed=6 * lists * slab, transcendentals=0
-        ),
-    )(received, scaled, slab_vectors)
-
-
-def other_update_kernel(
-    hops, lists_total, before_ref, received_ref, slab_ref, earlier_ref, kt_ref,
-    total_ref, squares_ref, incoming_ref, weights_ref, rows_ref, sems,
-):
-    lists, slab = kt_ref.shape
-    copies = []
-    for c, chunk in enumerate(chunks_of(lists)):
-        rows = pl.ds(chunk.start, CHUNK)
-        copies.append(pltpu.make_async_copy(kt_ref.at[rows, :], incoming_ref.at[rows, :], sems.at[c]))
-        copies[-1].start()
-    before_scale = row_scale_of(before_ref, rows_ref, hops)
-    scale = row_scale_of(received_ref, rows_ref, hops) * (slab * lists_total)
-    for chunk in chunks_of(lists, LONG):
-        rows = pl.ds(chunk.start, LONG)
-        for t in range(chunk.start, chunk.stop, TILE):
-            if t % CHUNK == 0:
-                copies[t // CHUNK].wait()
-            scaled = scaled_lists(incoming_ref[pl.ds(t, TILE), :], before_scale, lists_total)
-            weights_ref[pl.ds(t, TILE), :] = (scaled * scale).astype(BF16)
+        write_weights(scaled_ref, scale, weights_ref, chunk)
         total = jnp.dot(weights_ref[rows, :], slab_ref[...], preferred_element_type=F32)
         total = total + earlier_ref[rows, :]
         total_ref[rows, :] = total
@@ -324,8 +351,8 @@
             squares_ref[at : at + 1, :] = to_row(squares[k * LANES : (k + 1) * LANES])
 
 
-def other_update(before, received, slab_vectors, earlier, kt, hops, lists_total):
-    lists, slab = kt.shape
+def other_update(received, scaled, slab_vectors, earlier, hops, lists_total):
+    lists, slab = scaled.shape
     width = slab_vectors.shape[1]
     return pl.pallas_call(
         functools.partial(other_update_kernel, hops, lists_total),
@@ -333,19 +360,14 @@
             jax.ShapeDtypeStruct((lists, width), F32),
             jax.ShapeDtypeStruct((lists // LANES, LANES), F32),
         ),
-        in_specs=[IN_VMEM] * 4 + [pl.BlockSpec(memory_space=pltpu.HBM)],
+        in_specs=[IN_VMEM] * 4,
         out_specs=(IN_VMEM, IN_VMEM),
-        scratch_shapes=[
-            pltpu.VMEM((lists, slab), F32),
-            pltpu.VMEM((lists, slab), BF16),
-            pltpu.VMEM((slab // LANES, LANES), F32),
-            pltpu.SemaphoreType.DMA((lists // CHUNK,)),
-        ],
+        scratch_shapes=[pltpu.VMEM((lists, slab), BF16), pltpu.VMEM((slab // LANES, LANES), F32)],
         compiler_params=params(),
         cost_estimate=pl.CostEstimate(
             flops=2 * lists * width * slab, bytes_accessed=8 * lists * slab, transcendentals=0
         ),
-    )(before, received, slab_vectors, earlier, kt)
+    )(received, scaled, slab_vectors, earlier)
 
 
 def finish_kernel(numerators_ref, mine_ref, theirs_ref, out_ref, scaled_ref, sems):
@@ -407,32 +429,37 @@
     dp = lax.axis_size("dp")
     peers = dp * lax.axis_size("cx")
     lists_total = centroids.shape[0] * peers * lax.axis_size("cz")
-    hops = (0, 1, dp - 1, 2)
+    hops = (0, 2, 1, dp - 1)
     cx = lax.axis_size("cx")
+    from_hop = lambda x, axis, hop, size: lax.ppermute(x, axis, [((i + hop) % size, i) for i in range(size)])
     share = unit_share(vectors, cx)
+    far = from_hop(share, "dp", hops[1], dp)
     mine = unit_rows(vectors, share)
-    from_hop = lambda x, axis, hop, size: lax.ppermute(x, axis, [((i + hop) % size, i) for i in range(size)])
-    far = from_hop(share, "dp", hops[3], dp)
-    far, ready = lax.optimization_barrier((far, mine))
-    near = [from_hop(ready, "dp", hop, dp) for hop in hops[1:3]]
-    far = [far] + [from_hop(far, "cx", hop, cx) for hop in range(1, cx)]
-    unit_centroids, own = own_scores(centroids, mine)
-    near_kt = near_scores(unit_centroids, near)
+    unit_centroids = unit_lists(centroids)
+    far, ready, unit_centroids = lax.optimization_barrier((far, mine, unit_centroids))
+    near = [from_hop(ready, "dp", hop, dp) for hop in hops[2:]]
+    shares = [far] + [from_hop(far, "cx", hop, cx) for hop in range(1, cx)]
+    own = block_scores(unit_centroids, mine)
+    far, far_kt = far_scores(unit_centroids, shares)
     kt, kt_sent, kept, sent, copies = first_sweep(
-        unit_centroids, own, near_kt, [mine, *near, *far], hops, lists_total, peers
+        unit_centroids, own, far_kt, [mine, far, *near], hops, lists_total, peers
     )
     swapped = lambda x: lax.ppermute(x, "replica", [(0, 1), (1, 0)])
+    received = sum_over_lists(copies)
+    received, kt_sent, sent = lax.optimization_barrier((received, kt_sent, sent))
     other_kt, other_vectors = swapped(kt_sent), swapped(sent)
-    received = sum_over_lists(copies)
     for sweep in range(1, ITERS):
         before = received
         copies, *scaled = next_sweep(before, kt, hops, lists_total, peers, sweep == ITERS - 1)
+        if scaled:
+            copies, other_before = lax.optimization_barrier((copies, swapped(before)))
         received = sum_over_lists(copies)
-    before, received = lax.optimization_barrier((before, received))
-    other_before, other_received = swapped(before), swapped(received)
-    own_numerators = own_update(received, scaled[0], kept, hops, lists_total)
+    other_received = swapped(received)
+    own_numerators, other_scaled = own_update(
+        received, scaled[0], kept, other_before, other_kt, hops, lists_total
+    )
     numerators, squares = other_update(
-        other_before, other_received, other_vectors, own_numerators, other_kt, hops, lists_total
+        other_received, other_scaled, other_vectors, own_numerators, hops, lists_total
     )
     return finish(numerators, squares, swapped(squares))
 

time: 120 us -> 115 us (0.958)
  starting transfers between devices: 25.3 us -> 19.8 us
  waiting for transfers between devices: 2.25 us -> 7.37 us
  local copies, waits for them, and re-layouts: 4.61 us -> 1.22 us
    ppermute x6, waiting for transfers between devices: 1.41 us -> 6.2 us  [body(): lax.ppermute(x, axis, [((i + hop) % size, i) for i in range(size)])]
    unnamed x4 -> x2, local copies, waits for them, and re-layouts: 4.61 us -> 1.22 us
    ppermute x6, starting transfers between devices: 12.1 us -> 8.98 us  [body(): lax.ppermute(x, axis, [((i + hop) % size, i) for i in range(size)])]
    pallas_call x1, Pallas kernels: 5.06 us -> 2.53 us  [other_update(): pl.pallas_call(functools.partial(other_update_kernel, hops, lists_total),...]
    ppermute x5, starting transfers between devices: 13.2 us -> 10.8 us  [body(): swapped = lambda x: lax.ppermute(x, 'replica', [(0, 1), (1, 0)])]
    pallas_call x1, Pallas kernels: 2.33 us -> 4.25 us  [own_update(): pl.pallas_call(functools.partial(own_update_kernel, hops, lists_total), o...]
    pallas_call x3 -> x4, Pallas kernels: 10.1 us -> 10.7 us  [the longest x1 4.44 us: first_sweep(): pl.pallas_call(functools.partial(first_kernel, hops, lists_total), out_sh...]
  transfers between devices with their start and end apart: 11 -> 11, of which waited for: 3 -> 3; matrix products, arithmetic and copies ran while one was open for 0% -> 0% of each run, Pallas kernels for 9% -> 11%
where the time goes in v5:
time: 115 us
  blocking collectives  62.7 us (55%)
  Pallas kernels  23.4 us (20%)
  starting transfers between devices  19.8 us (17%)
  waiting for transfers between devices  7.37 us (6%)
  local copies, waits for them, and re-layouts  1.22 us (1%)
    all_to_all x6, blocking collectives, exchange(): return lax.all_to_all(copies, axes, 0, 0, tiled=True)  62.7 us
    ppermute x5, starting transfers between devices, body(): swapped = lambda x: lax.ppermute(x, 'replica', [(0, 1), (1, 0)])  10.8 us
    ppermute x6, starting transfers between devices, body(): lax.ppermute(x, axis, [((i + hop) % size, i) for i in range(size)])  8.98 us
    ppermute x6, waiting for transfers between devices, body(): lax.ppermute(x, axis, [((i + hop) % size, i) for i in range(size)])  6.2 us
    pallas_call x1, Pallas kernels, first_sweep(): pl.pallas_call(functools.partial(first_kernel, hops, lists_total), out_sh...  4.44 us
    pallas_call x1, Pallas kernels, own_update(): pl.pallas_call(functools.partial(own_update_kernel, hops, lists_total), o...  4.25 us
    pallas_call x1, Pallas kernels, unit_lists(): pl.pallas_call(centroids_kernel, out_shape=jax.ShapeDtypeStruct((lists, w...  3.64 us
    pallas_call x1, Pallas kernels, other_update(): pl.pallas_call(functools.partial(other_update_kernel, hops, lists_total),...  2.53 us
  transfers between devices with their start and end apart: 11, of which 3 were waited for; matrix products, arithmetic and copies ran while one was open for 0% of the time, Pallas kernels for 11%

profile of v5, /device:TPU:1, one launch (start us, length us, event | category | flops | bytes accessed | tf_op | source)
XLA Modules:
  0.0 114.7 jit_solution(13187806852789226987)
XLA Ops:
  1.1 3.8 %collective-permute-start = (bf16[64,1024]{1,0:T(8,128)(2,1)S(1)}, bf16[64,1024]{1,0:T(8,128)(2,1)S(1)}, u32[]{:S(2)}, u32[]{:S(2)}) collective-permute-start(bf16[64,1024]{1,0:T(8,128)(2,1)S(1)} %shard_map.28.share_ref), channel_id=1, source_target_pairs={{64,0},{96,32},{0,64},{32,96},{65,1},{97,33},{1,65},{33,97},{66,2}... | collective-permute-start | bytes 393224 | tf_op jit(solution)/shard_map/ppermute | solution.py:434
  4.9 1.2 %copy-done = f32[256,1024]{1,0:T(8,128)S(1)} copy-done((f32[256,1024]{1,0:T(8,128)S(1)}, f32[256,1024]{1,0:T(8,128)}, u32[]{:S(2)}) %copy-start) | copy-done | bytes 1048600
  6.3 3.6 %shard_map.30.centroids_ref = bf16[2048,1024]{1,0:T(8,128)(2,1)S(1)} custom-call(f32[2048,1024]{1,0:T(8,128)} %centroids_ref.1), custom_call_target="tpu_custom_call" | custom-call | flops 8388608 | bytes 12582912 | tf_op jit(solution)/shard_map/pallas_call | solution.py:100
  11.5 2.5 %collective-permute-start.1 = (bf16[64,1024]{1,0:T(8,128)(2,1)S(1)}, bf16[64,1024]{1,0:T(8,128)(2,1)S(1)}, u32[]{:S(2)}, u32[]{:S(2)}) collective-permute-start(bf16[64,1024]{1,0:T(8,128)(2,1)S(1)} %collective-permute-done.refs_0_), channel_id=1, source_target_pairs={{8,0},{16,8},{24,16},{0,24},{9,1},{17,9},{25,17},{1,25},{10,2},{18... | collective-permute-start | bytes 393224 | tf_op jit(solution)/shard_map/ppermute | solution.py:434
  15.1 1.3 %shard_map.31.own_ref = f32[2048,256]{1,0:T(8,128)S(1)} custom-call(bf16[2048,1024]{1,0:T(8,128)(2,1)S(1)} %shard_map.30.centroids_ref, bf16[256,1024]{1,0:T(8,128)(2,1)S(1)} %shard_map.29.vectors_ref.refs_0_), custom_call_target="tpu_custom_call" | custom-call | flops 1073741824 | bytes 8388608 | tf_op jit(solution)/shard_map/pallas_call | solution.py:178
  16.4 3.0 %collective-permute-done.2.refs_2_ = bf16[64,1024]{1,0:T(8,128)(2,1)S(1)} collective-permute-done((bf16[64,1024]{1,0:T(8,128)(2,1)S(1)}, bf16[64,1024]{1,0:T(8,128)(2,1)S(1)}, u32[]{:S(2)}, u32[]{:S(2)}) %collective-permute-start.2) | collective-permute-done | bytes 131104 | tf_op jit(solution)/shard_map/ppermute | solution.py:434
  19.4 3.2 %collective-permute-done.3.refs_3_ = bf16[64,1024]{1,0:T(8,128)(2,1)S(1)} collective-permute-done((bf16[64,1024]{1,0:T(8,128)(2,1)S(1)}, bf16[64,1024]{1,0:T(8,128)(2,1)S(1)}, u32[]{:S(2)}, u32[]{:S(2)}) %collective-permute-start.3) | collective-permute-done | bytes 131104 | tf_op jit(solution)/shard_map/ppermute | solution.py:434
  22.6 1.3 %shard_map.32 = (bf16[256,1024]{1,0:T(8,128)(2,1)S(1)}, f32[2048,256]{1,0:T(8,128)S(1)}) custom-call(bf16[2048,1024]{1,0:T(8,128)(2,1)S(1)} %shard_map.30.centroids_ref, bf16[64,1024]{1,0:T(8,128)(2,1)S(1)} %collective-permute-done.refs_0_, bf16[64,1024]{1,0:T(8,128)(2,1)S(1)} %collective-permute-done.1.refs_1_, ...), custom_call_target="tpu_custom_call" | custom-call | flops 1073741824 | bytes 8388608 | tf_op jit(solution)/shard_map/pallas_call | solution.py:191
  24.0 4.4 %shard_map.33 = (f32[2048,1024]{1,0:T(8,128)S(1)}, f32[2048,1024]{1,0:T(8,128)}, bf16[1024,512]{1,0:T(8,128)(2,1)S(1)}, bf16[1024,512]{1,0:T(8,128)(2,1)S(1)}, f32[16,8,128]{2,1,0:T(8,128)S(1)}) custom-call(bf16[2048,1024]{1,0:T(8,128)(2,1)S(1)} %shard_map.30.centroids_ref, f32[2048,256]{1,0:T(8,128)S(1)} %shard_map.31.own_ref, ...), custom_call_target="tpu_custom_call" | custom-call | flops 2147483648 | bytes 12582912 | tf_op jit(solution)/shard_map/pallas_call | solution.py:234
  28.4 10.6 %all_to_all.30.received_ref = f32[16,8,128]{2,1,0:T(8,128)S(1)} all-to-all(f32[16,8,128]{2,1,0:T(8,128)S(1)} %get-tuple-element.31), channel_id=1, replica_groups=mesh['replica'=2,'dp'=4,'cx'=4,'cz'=8] {'dp','cx'}, dimensions={0} | all-to-all | bytes 131072 | tf_op jit(solution)/shard_map/all_to_all | solution.py:407
  39.0 14.9 %all_to_all.31.received_ref = f32[8,8,128]{2,1,0:T(8,128)S(1)} all-to-all(f32[8,8,128]{2,1,0:T(8,128)S(1)} %shard_map.34), channel_id=1, replica_groups=mesh['replica'=2,'dp'=4,'cx'=4,'cz'=8] {'cz'}, dimensions={0} | all-to-all | bytes 65536 | tf_op jit(solution)/shard_map/all_to_all | solution.py:407
  53.9 5.1 %collective-permute-start.8 = (f32[2048,1024]{1,0:T(8,128)}, f32[2048,1024]{1,0:T(8,128)S(1)}, u32[]{:S(2)}, u32[]{:S(2)}) collective-permute-start(f32[2048,1024]{1,0:T(8,128)} %get-tuple-element.41), channel_id=1, source_target_pairs={{0,128},{128,0},{1,129},{129,1},{2,130},{130,2},{3,131},{131,3},{4... | collective-permute-start | bytes 25165832 | tf_op jit(solution)/shard_map/ppermute | solution.py:447
  59.0 1.2 %shard_map.35 = f32[16,8,128]{2,1,0:T(8,128)S(1)} custom-call(f32[8,8,128]{2,1,0:T(8,128)S(1)} %all_to_all.31.received_ref, f32[2048,1024]{1,0:T(8,128)S(1)} %get-tuple-element.35.kt_ref), custom_call_target="tpu_custom_call" | custom-call | flops 8388608 | bytes 8388608 | tf_op jit(solution)/shard_map/pallas_call | solution.py:273
  60.1 9.4 %all_to_all.32.received_ref = f32[16,8,128]{2,1,0:T(8,128)S(1)} all-to-all(f32[16,8,128]{2,1,0:T(8,128)S(1)} %shard_map.35), channel_id=1, replica_groups=mesh['replica'=2,'dp'=4,'cx'=4,'cz'=8] {'dp','cx'}, dimensions={0} | all-to-all | bytes 131072 | tf_op jit(solution)/shard_map/all_to_all | solution.py:407
  69.5 9.2 %all_to_all.33.received_ref = f32[8,8,128]{2,1,0:T(8,128)S(1)} all-to-all(f32[8,8,128]{2,1,0:T(8,128)S(1)} %shard_map.36), channel_id=1, replica_groups=mesh['replica'=2,'dp'=4,'cx'=4,'cz'=8] {'cz'}, dimensions={0} | all-to-all | bytes 65536 | tf_op jit(solution)/shard_map/all_to_all | solution.py:407
  78.8 3.1 %collective-permute-start.6 = (f32[8,8,128]{2,1,0:T(8,128)S(1)}, f32[8,8,128]{2,1,0:T(8,128)S(1)}, u32[]{:S(2)}, u32[]{:S(2)}) collective-permute-start(f32[8,8,128]{2,1,0:T(8,128)S(1)} %all_to_all.33.received_ref), channel_id=1, source_target_pairs={{0,128},{128,0},{1,129},{129,1},{2,130},{130,2},{3,131},{131,3},{4... | collective-permute-start | bytes 98312 | tf_op jit(solution)/shard_map/ppermute | solution.py:447
  81.9 1.3 %shard_map.37 = (f32[16,8,128]{2,1,0:T(8,128)S(1)}, f32[2048,1024]{1,0:T(8,128)S(1)}) custom-call(f32[8,8,128]{2,1,0:T(8,128)S(1)} %all_to_all.33.received_ref, f32[2048,1024]{1,0:T(8,128)S(1)} %get-tuple-element.35.kt_ref), custom_call_target="tpu_custom_call" | custom-call | flops 8388608 | bytes 8388608 | tf_op jit(solution)/shard_map/pallas_call | solution.py:273
  83.1 9.4 %all_to_all.34.received_ref = f32[16,8,128]{2,1,0:T(8,128)S(1)} all-to-all(f32[16,8,128]{2,1,0:T(8,128)S(1)} %get-tuple-element.37), channel_id=1, replica_groups=mesh['replica'=2,'dp'=4,'cx'=4,'cz'=8] {'dp','cx'}, dimensions={0} | all-to-all | bytes 131072 | tf_op jit(solution)/shard_map/all_to_all | solution.py:407
  92.5 9.2 %all_to_all.35.received_ref = f32[8,8,128]{2,1,0:T(8,128)S(1)} all-to-all(f32[8,8,128]{2,1,0:T(8,128)S(1)} %shard_map.38), channel_id=1, replica_groups=mesh['replica'=2,'dp'=4,'cx'=4,'cz'=8] {'cz'}, dimensions={0} | all-to-all | bytes 65536 | tf_op jit(solution)/shard_map/all_to_all | solution.py:407
  101.8 2.6 %collective-permute-start.7 = (f32[8,8,128]{2,1,0:T(8,128)S(1)}, f32[8,8,128]{2,1,0:T(8,128)S(1)}, u32[]{:S(2)}, u32[]{:S(2)}) collective-permute-start(f32[8,8,128]{2,1,0:T(8,128)S(1)} %all_to_all.35.received_ref), channel_id=1, source_target_pairs={{0,128},{128,0},{1,129},{129,1},{2,130},{130,2},{3,131},{131,3},{4... | collective-permute-start | bytes 98312 | tf_op jit(solution)/shard_map/ppermute | solution.py:447
  104.4 4.3 %shard_map.39 = (f32[2048,512]{1,0:T(8,128)S(1)}, f32[2048,1024]{1,0:T(8,128)S(1)}) custom-call(f32[8,8,128]{2,1,0:T(8,128)S(1)} %all_to_all.35.received_ref, f32[2048,1024]{1,0:T(8,128)S(1)} %get-tuple-element.38.scaled_ref, bf16[1024,512]{1,0:T(8,128)(2,1)S(1)} %get-tuple-element.39.slab_ref, f32[8,8,128]{2,1,0:T(8,128)S(1)} %collective-permute-done.6.other_before_ref, ...), custom_call_target="tpu_custom_call" | custom-call | flops 2147483648 | bytes 12582912 | tf_op jit(solution)/shard_map/pallas_call | solution.py:319
  108.6 2.5 %shard_map.40 = (f32[2048,512]{1,0:T(8,128)S(1)}, f32[16,128]{1,0:T(8,128)S(1)}) custom-call(f32[8,8,128]{2,1,0:T(8,128)S(1)} %collective-permute-done.7.received_ref, f32[2048,1024]{1,0:T(8,128)S(1)} %get-tuple-element.42.scaled_ref, bf16[1024,512]{1,0:T(8,128)(2,1)S(1)} %collective-permute-done.9.slab_ref, f32[2048,512]{1,0:T(8,128)S(1)} %get-tuple-element.44.earlier_ref), custom_call_target="tpu_custom_call" | custom-call | flops 2147483648 | bytes 16777216 | tf_op jit(solution)/shard_map/pallas_call | solution.py:357
  111.2 1.2 %collective-permute-done.10.theirs_ref = f32[16,128]{1,0:T(8,128)S(1)} collective-permute-done((f32[16,128]{1,0:T(8,128)S(1)}, f32[16,128]{1,0:T(8,128)S(1)}, u32[]{:S(2)}, u32[]{:S(2)}) %collective-permute-start.10) | collective-permute-done | bytes 8224 | tf_op jit(solution)/shard_map/ppermute | solution.py:447
  112.4 2.2 %shard_map.41 = f32[2048,512]{1,0:T(8,128)} custom-call(f32[2048,512]{1,0:T(8,128)S(1)} %get-tuple-element.45.numerators_ref, f32[16,128]{1,0:T(8,128)S(1)} %get-tuple-element.46.mine_ref, f32[16,128]{1,0:T(8,128)S(1)} %collective-permute-done.10.theirs_ref), custom_call_target="tpu_custom_call" | custom-call | flops 1048576 | bytes 8388608 | tf_op jit(solution)/shard_map/pallas_call | solution.py:392
  (20 shorter events, 4.1 us)
Async XLA Ops:
  1.1 8.9 %collective-permute-start = (bf16[64,1024]{1,0:T(8,128)(2,1)S(1)}, bf16[64,1024]{1,0:T(8,128)(2,1)S(1)}, u32[]{:S(2)}, u32[]{:S(2)}) collective-permute-start(bf16[64,1024]{1,0:T(8,128)(2,1)S(1)} %shard_map.28.share_ref), channel_id=1, source_target_pairs={{64,0},{96,32},{0,64},{32,96},{65,1},{97,33},{1,65},{33,97},{66,2}... | collective-permute-start | bytes 393224 | tf_op jit(solution)/shard_map/ppermute | solution.py:434
  4.9 1.2 %copy-start = (f32[256,1024]{1,0:T(8,128)S(1)}, f32[256,1024]{1,0:T(8,128)}, u32[]{:S(2)}) copy-start(f32[256,1024]{1,0:T(8,128)} %values_ref.3) | copy-start | bytes 3145732
  10.0 14.0 %collective-permute-start.4 = (bf16[256,1024]{1,0:T(8,128)(2,1)S(1)}, bf16[256,1024]{1,0:T(8,128)(2,1)S(1)}, u32[]{:S(2)}, u32[]{:S(2)}) collective-permute-start(bf16[256,1024]{1,0:T(8,128)(2,1)S(1)} %shard_map.29.vectors_ref.refs_0_), channel_id=1, source_target_pairs={{32,0},{64,32},{96,64},{0,96},{33,1},{65,33},{97,65},{1,97},{34,2}... | collective-permute-start | bytes 1572872 | tf_op jit(solution)/shard_map/ppermute | solution.py:434
  10.8 13.1 %collective-permute-start.5 = (bf16[256,1024]{1,0:T(8,128)(2,1)S(1)}, bf16[256,1024]{1,0:T(8,128)(2,1)S(1)}, u32[]{:S(2)}, u32[]{:S(2)}) collective-permute-start(bf16[256,1024]{1,0:T(8,128)(2,1)S(1)} %shard_map.29.vectors_ref.refs_0_), channel_id=1, source_target_pairs={{96,0},{0,32},{32,64},{64,96},{97,1},{1,33},{33,65},{65,97},{98,2}... | collective-permute-start | bytes 1572872 | tf_op jit(solution)/shard_map/ppermute | solution.py:434
  11.5 4.9 %collective-permute-start.1 = (bf16[64,1024]{1,0:T(8,128)(2,1)S(1)}, bf16[64,1024]{1,0:T(8,128)(2,1)S(1)}, u32[]{:S(2)}, u32[]{:S(2)}) collective-permute-start(bf16[64,1024]{1,0:T(8,128)(2,1)S(1)} %collective-permute-done.refs_0_), channel_id=1, source_target_pairs={{8,0},{16,8},{24,16},{0,24},{9,1},{17,9},{25,17},{1,25},{10,2},{18... | collective-permute-start | bytes 393224 | tf_op jit(solution)/shard_map/ppermute | solution.py:434
  14.0 5.4 %collective-permute-start.2 = (bf16[64,1024]{1,0:T(8,128)(2,1)S(1)}, bf16[64,1024]{1,0:T(8,128)(2,1)S(1)}, u32[]{:S(2)}, u32[]{:S(2)}) collective-permute-start(bf16[64,1024]{1,0:T(8,128)(2,1)S(1)} %collective-permute-done.refs_0_), channel_id=1, source_target_pairs={{16,0},{24,8},{0,16},{8,24},{17,1},{25,9},{1,17},{9,25},{18,2},{26... | collective-permute-start | bytes 393224 | tf_op jit(solution)/shard_map/ppermute | solution.py:434
  14.5 8.1 %collective-permute-start.3 = (bf16[64,1024]{1,0:T(8,128)(2,1)S(1)}, bf16[64,1024]{1,0:T(8,128)(2,1)S(1)}, u32[]{:S(2)}, u32[]{:S(2)}) collective-permute-start(bf16[64,1024]{1,0:T(8,128)(2,1)S(1)} %collective-permute-done.refs_0_), channel_id=1, source_target_pairs={{24,0},{0,8},{8,16},{16,24},{25,1},{1,9},{9,17},{17,25},{26,2},{2,... | collective-permute-start | bytes 393224 | tf_op jit(solution)/shard_map/ppermute | solution.py:434
  53.9 50.5 %collective-permute-start.8 = (f32[2048,1024]{1,0:T(8,128)}, f32[2048,1024]{1,0:T(8,128)S(1)}, u32[]{:S(2)}, u32[]{:S(2)}) collective-permute-start(f32[2048,1024]{1,0:T(8,128)} %get-tuple-element.41), channel_id=1, source_target_pairs={{0,128},{128,0},{1,129},{129,1},{2,130},{130,2},{3,131},{131,3},{4... | collective-permute-start | bytes 25165832 | tf_op jit(solution)/shard_map/ppermute | solution.py:447
  59.0 49.7 %collective-permute-start.9 = (bf16[1024,512]{1,0:T(8,128)(2,1)S(1)}, bf16[1024,512]{1,0:T(8,128)(2,1)S(1)}, u32[]{:S(2)}, u32[]{:S(2)}) collective-permute-start(bf16[1024,512]{1,0:T(8,128)(2,1)S(1)} %get-tuple-element.43), channel_id=1, source_target_pairs={{0,128},{128,0},{1,129},{129,1},{2,130},{130,2},{3,131},{131,3},{4... | collective-permute-start | bytes 3145736 | tf_op jit(solution)/shard_map/ppermute | solution.py:447
  78.8 4.4 %collective-permute-start.6 = (f32[8,8,128]{2,1,0:T(8,128)S(1)}, f32[8,8,128]{2,1,0:T(8,128)S(1)}, u32[]{:S(2)}, u32[]{:S(2)}) collective-permute-start(f32[8,8,128]{2,1,0:T(8,128)S(1)} %all_to_all.33.received_ref), channel_id=1, source_target_pairs={{0,128},{128,0},{1,129},{129,1},{2,130},{130,2},{3,131},{131,3},{4... | collective-permute-start | bytes 98312 | tf_op jit(solution)/shard_map/ppermute | solution.py:447
  101.8 6.8 %collective-permute-start.7 = (f32[8,8,128]{2,1,0:T(8,128)S(1)}, f32[8,8,128]{2,1,0:T(8,128)S(1)}, u32[]{:S(2)}, u32[]{:S(2)}) collective-permute-start(f32[8,8,128]{2,1,0:T(8,128)S(1)} %all_to_all.35.received_ref), channel_id=1, source_target_pairs={{0,128},{128,0},{1,129},{129,1},{2,130},{130,2},{3,131},{131,3},{4... | collective-permute-start | bytes 98312 | tf_op jit(solution)/shard_map/ppermute | solution.py:447
  111.2 1.2 %collective-permute-start.10 = (f32[16,128]{1,0:T(8,128)S(1)}, f32[16,128]{1,0:T(8,128)S(1)}, u32[]{:S(2)}, u32[]{:S(2)}) collective-permute-start(f32[16,128]{1,0:T(8,128)S(1)} %get-tuple-element.46.mine_ref), channel_id=1, source_target_pairs={{0,128},{128,0},{1,129},{129,1},{2,130},{130,2},{3,131},{131,3},{4... | collective-permute-start | bytes 24584 | tf_op jit(solution)/shard_map/ppermute | solution.py:447

commit v6 on v5

--- a/solution.py
+++ b/solution.py
@@ -212,16 +212,15 @@
     keep_ref[...] = slab_ref[:, pl.ds(pl.multiple_of(here * half, half), half)]
     send_ref[...] = slab_ref[:, pl.ds(pl.multiple_of((1 - here) * half, half), half)]
     row_scale = jnp.full((1, slab), 1.0 / slab, F32)
-    mass = jnp.zeros((GROUP_ROWS, slab), F32)
     sends = []
-    for c, chunk in enumerate(chunks_of(lists, LONG)):
-        rows = pl.ds(chunk.start, LONG)
+    for c, chunk in enumerate(chunks_of(lists)):
+        rows = pl.ds(chunk.start, CHUNK)
         kt_ref[rows, :block] = own_ref[rows, :]
         kt_ref[rows, block:known] = far_ref[rows, :]
         kt_ref[rows, known:] = affinity(centroids_ref[rows, :], slab_ref[known:, :])
         sends.append(pltpu.make_async_copy(kt_ref.at[rows, :], kt_send_ref.at[rows, :], sems.at[c]))
         sends[-1].start()
-        mass = mass + sweep_lists(kt_ref, row_scale, chunk, lists_total)
+    mass = sweep_lists(kt_ref, row_scale, range(lists), lists_total)
     place_mass(mass, hops, rows_ref, copies_ref)
     for send in sends:
         send.wait()
@@ -244,7 +243,7 @@
         scratch_shapes=[
             pltpu.VMEM((slab, width), BF16),
             pltpu.VMEM((rows, LANES), F32),
-            pltpu.SemaphoreType.DMA((lists // LONG,)),
+            pltpu.SemaphoreType.DMA((lists // CHUNK,)),
         ],
         compiler_params=params(),
         cost_estimate=pl.CostEstimate(

time: 115 us -> 115 us (level)
  no operation moved by 1% of the time
where the time goes in v6:
time: 115 us
  blocking collectives  62.7 us (55%)
  Pallas kernels  23.1 us (20%)
  starting transfers between devices  19.8 us (17%)
  waiting for transfers between devices  7.37 us (6%)
  local copies, waits for them, and re-layouts  1.22 us (1%)
    all_to_all x6, blocking collectives, exchange(): return lax.all_to_all(copies, axes, 0, 0, tiled=True)  62.7 us
    ppermute x5, starting transfers between devices, body(): swapped = lambda x: lax.ppermute(x, 'replica', [(0, 1), (1, 0)])  10.8 us
    ppermute x6, starting transfers between devices, body(): lax.ppermute(x, axis, [((i + hop) % size, i) for i in range(size)])  8.98 us
    ppermute x6, waiting for transfers between devices, body(): lax.ppermute(x, axis, [((i + hop) % size, i) for i in range(size)])  6.2 us
    pallas_call x1, Pallas kernels, own_update(): pl.pallas_call(functools.partial(own_update_kernel, hops, lists_total), o...  4.25 us
    pallas_call x1, Pallas kernels, first_sweep(): pl.pallas_call(functools.partial(first_kernel, hops, lists_total), out_sh...  4.2 us
    pallas_call x1, Pallas kernels, unit_lists(): pl.pallas_call(centroids_kernel, out_shape=jax.ShapeDtypeStruct((lists, w...  3.64 us
    pallas_call x1, Pallas kernels, other_update(): pl.pallas_call(functools.partial(other_update_kernel, hops, lists_total),...  2.53 us
  transfers between devices with their start and end apart: 11, of which 3 were waited for; matrix products, arithmetic and copies ran while one was open for 0% of the time, Pallas kernels for 11%

profile of v6, /device:TPU:1, one launch (start us, length us, event | category | flops | bytes accessed | tf_op | source)
XLA Modules:
  0.0 114.5 jit_solution(14586149864538434145)
XLA Ops:
  1.1 3.8 %collective-permute-start = (bf16[64,1024]{1,0:T(8,128)(2,1)S(1)}, bf16[64,1024]{1,0:T(8,128)(2,1)S(1)}, u32[]{:S(2)}, u32[]{:S(2)}) collective-permute-start(bf16[64,1024]{1,0:T(8,128)(2,1)S(1)} %shard_map.28.share_ref), channel_id=1, source_target_pairs={{64,0},{96,32},{0,64},{32,96},{65,1},{97,33},{1,65},{33,97},{66,2}... | collective-permute-start | bytes 393224 | tf_op jit(solution)/shard_map/ppermute | solution.py:433
  4.9 1.2 %copy-done = f32[256,1024]{1,0:T(8,128)S(1)} copy-done((f32[256,1024]{1,0:T(8,128)S(1)}, f32[256,1024]{1,0:T(8,128)}, u32[]{:S(2)}) %copy-start) | copy-done | bytes 1048600
  6.3 3.6 %shard_map.30.centroids_ref = bf16[2048,1024]{1,0:T(8,128)(2,1)S(1)} custom-call(f32[2048,1024]{1,0:T(8,128)} %centroids_ref.1), custom_call_target="tpu_custom_call" | custom-call | flops 8388608 | bytes 12582912 | tf_op jit(solution)/shard_map/pallas_call | solution.py:100
  11.5 2.5 %collective-permute-start.1 = (bf16[64,1024]{1,0:T(8,128)(2,1)S(1)}, bf16[64,1024]{1,0:T(8,128)(2,1)S(1)}, u32[]{:S(2)}, u32[]{:S(2)}) collective-permute-start(bf16[64,1024]{1,0:T(8,128)(2,1)S(1)} %collective-permute-done.refs_0_), channel_id=1, source_target_pairs={{8,0},{16,8},{24,16},{0,24},{9,1},{17,9},{25,17},{1,25},{10,2},{18... | collective-permute-start | bytes 393224 | tf_op jit(solution)/shard_map/ppermute | solution.py:433
  15.1 1.3 %shard_map.31.own_ref = f32[2048,256]{1,0:T(8,128)S(1)} custom-call(bf16[2048,1024]{1,0:T(8,128)(2,1)S(1)} %shard_map.30.centroids_ref, bf16[256,1024]{1,0:T(8,128)(2,1)S(1)} %shard_map.29.vectors_ref.refs_0_), custom_call_target="tpu_custom_call" | custom-call | flops 1073741824 | bytes 8388608 | tf_op jit(solution)/shard_map/pallas_call | solution.py:178
  16.4 3.0 %collective-permute-done.2.refs_2_ = bf16[64,1024]{1,0:T(8,128)(2,1)S(1)} collective-permute-done((bf16[64,1024]{1,0:T(8,128)(2,1)S(1)}, bf16[64,1024]{1,0:T(8,128)(2,1)S(1)}, u32[]{:S(2)}, u32[]{:S(2)}) %collective-permute-start.2) | collective-permute-done | bytes 131104 | tf_op jit(solution)/shard_map/ppermute | solution.py:433
  19.4 3.2 %collective-permute-done.3.refs_3_ = bf16[64,1024]{1,0:T(8,128)(2,1)S(1)} collective-permute-done((bf16[64,1024]{1,0:T(8,128)(2,1)S(1)}, bf16[64,1024]{1,0:T(8,128)(2,1)S(1)}, u32[]{:S(2)}, u32[]{:S(2)}) %collective-permute-start.3) | collective-permute-done | bytes 131104 | tf_op jit(solution)/shard_map/ppermute | solution.py:433
  22.6 1.3 %shard_map.32 = (bf16[256,1024]{1,0:T(8,128)(2,1)S(1)}, f32[2048,256]{1,0:T(8,128)S(1)}) custom-call(bf16[2048,1024]{1,0:T(8,128)(2,1)S(1)} %shard_map.30.centroids_ref, bf16[64,1024]{1,0:T(8,128)(2,1)S(1)} %collective-permute-done.refs_0_, bf16[64,1024]{1,0:T(8,128)(2,1)S(1)} %collective-permute-done.1.refs_1_, ...), custom_call_target="tpu_custom_call" | custom-call | flops 1073741824 | bytes 8388608 | tf_op jit(solution)/shard_map/pallas_call | solution.py:191
  24.0 4.2 %shard_map.33 = (f32[2048,1024]{1,0:T(8,128)S(1)}, f32[2048,1024]{1,0:T(8,128)}, bf16[1024,512]{1,0:T(8,128)(2,1)S(1)}, bf16[1024,512]{1,0:T(8,128)(2,1)S(1)}, f32[16,8,128]{2,1,0:T(8,128)S(1)}) custom-call(bf16[2048,1024]{1,0:T(8,128)(2,1)S(1)} %shard_map.30.centroids_ref, f32[2048,256]{1,0:T(8,128)S(1)} %shard_map.31.own_ref, ...), custom_call_target="tpu_custom_call" | custom-call | flops 2147483648 | bytes 12582912 | tf_op jit(solution)/shard_map/pallas_call | solution.py:233
  28.2 10.6 %all_to_all.30.received_ref = f32[16,8,128]{2,1,0:T(8,128)S(1)} all-to-all(f32[16,8,128]{2,1,0:T(8,128)S(1)} %get-tuple-element.31), channel_id=1, replica_groups=mesh['replica'=2,'dp'=4,'cx'=4,'cz'=8] {'dp','cx'}, dimensions={0} | all-to-all | bytes 131072 | tf_op jit(solution)/shard_map/all_to_all | solution.py:406
  38.8 14.9 %all_to_all.31.received_ref = f32[8,8,128]{2,1,0:T(8,128)S(1)} all-to-all(f32[8,8,128]{2,1,0:T(8,128)S(1)} %shard_map.34), channel_id=1, replica_groups=mesh['replica'=2,'dp'=4,'cx'=4,'cz'=8] {'cz'}, dimensions={0} | all-to-all | bytes 65536 | tf_op jit(solution)/shard_map/all_to_all | solution.py:406
  53.6 5.1 %collective-permute-start.8 = (f32[2048,1024]{1,0:T(8,128)}, f32[2048,1024]{1,0:T(8,128)S(1)}, u32[]{:S(2)}, u32[]{:S(2)}) collective-permute-start(f32[2048,1024]{1,0:T(8,128)} %get-tuple-element.41), channel_id=1, source_target_pairs={{0,128},{128,0},{1,129},{129,1},{2,130},{130,2},{3,131},{131,3},{4... | collective-permute-start | bytes 25165832 | tf_op jit(solution)/shard_map/ppermute | solution.py:446
  58.7 1.2 %shard_map.35 = f32[16,8,128]{2,1,0:T(8,128)S(1)} custom-call(f32[8,8,128]{2,1,0:T(8,128)S(1)} %all_to_all.31.received_ref, f32[2048,1024]{1,0:T(8,128)S(1)} %get-tuple-element.35.kt_ref), custom_call_target="tpu_custom_call" | custom-call | flops 8388608 | bytes 8388608 | tf_op jit(solution)/shard_map/pallas_call | solution.py:272
  59.9 9.4 %all_to_all.32.received_ref = f32[16,8,128]{2,1,0:T(8,128)S(1)} all-to-all(f32[16,8,128]{2,1,0:T(8,128)S(1)} %shard_map.35), channel_id=1, replica_groups=mesh['replica'=2,'dp'=4,'cx'=4,'cz'=8] {'dp','cx'}, dimensions={0} | all-to-all | bytes 131072 | tf_op jit(solution)/shard_map/all_to_all | solution.py:406
  69.3 9.2 %all_to_all.33.received_ref = f32[8,8,128]{2,1,0:T(8,128)S(1)} all-to-all(f32[8,8,128]{2,1,0:T(8,128)S(1)} %shard_map.36), channel_id=1, replica_groups=mesh['replica'=2,'dp'=4,'cx'=4,'cz'=8] {'cz'}, dimensions={0} | all-to-all | bytes 65536 | tf_op jit(solution)/shard_map/all_to_all | solution.py:406
  78.5 3.1 %collective-permute-start.6 = (f32[8,8,128]{2,1,0:T(8,128)S(1)}, f32[8,8,128]{2,1,0:T(8,128)S(1)}, u32[]{:S(2)}, u32[]{:S(2)}) collective-permute-start(f32[8,8,128]{2,1,0:T(8,128)S(1)} %all_to_all.33.received_ref), channel_id=1, source_target_pairs={{0,128},{128,0},{1,129},{129,1},{2,130},{130,2},{3,131},{131,3},{4... | collective-permute-start | bytes 98312 | tf_op jit(solution)/shard_map/ppermute | solution.py:446
  81.6 1.3 %shard_map.37 = (f32[16,8,128]{2,1,0:T(8,128)S(1)}, f32[2048,1024]{1,0:T(8,128)S(1)}) custom-call(f32[8,8,128]{2,1,0:T(8,128)S(1)} %all_to_all.33.received_ref, f32[2048,1024]{1,0:T(8,128)S(1)} %get-tuple-element.35.kt_ref), custom_call_target="tpu_custom_call" | custom-call | flops 8388608 | bytes 8388608 | tf_op jit(solution)/shard_map/pallas_call | solution.py:272
  82.9 9.4 %all_to_all.34.received_ref = f32[16,8,128]{2,1,0:T(8,128)S(1)} all-to-all(f32[16,8,128]{2,1,0:T(8,128)S(1)} %get-tuple-element.37), channel_id=1, replica_groups=mesh['replica'=2,'dp'=4,'cx'=4,'cz'=8] {'dp','cx'}, dimensions={0} | all-to-all | bytes 131072 | tf_op jit(solution)/shard_map/all_to_all | solution.py:406
  92.3 9.2 %all_to_all.35.received_ref = f32[8,8,128]{2,1,0:T(8,128)S(1)} all-to-all(f32[8,8,128]{2,1,0:T(8,128)S(1)} %shard_map.38), channel_id=1, replica_groups=mesh['replica'=2,'dp'=4,'cx'=4,'cz'=8] {'cz'}, dimensions={0} | all-to-all | bytes 65536 | tf_op jit(solution)/shard_map/all_to_all | solution.py:406
  101.5 2.6 %collective-permute-start.7 = (f32[8,8,128]{2,1,0:T(8,128)S(1)}, f32[8,8,128]{2,1,0:T(8,128)S(1)}, u32[]{:S(2)}, u32[]{:S(2)}) collective-permute-start(f32[8,8,128]{2,1,0:T(8,128)S(1)} %all_to_all.35.received_ref), channel_id=1, source_target_pairs={{0,128},{128,0},{1,129},{129,1},{2,130},{130,2},{3,131},{131,3},{4... | collective-permute-start | bytes 98312 | tf_op jit(solution)/shard_map/ppermute | solution.py:446
  104.1 4.2 %shard_map.39 = (f32[2048,512]{1,0:T(8,128)S(1)}, f32[2048,1024]{1,0:T(8,128)S(1)}) custom-call(f32[8,8,128]{2,1,0:T(8,128)S(1)} %all_to_all.35.received_ref, f32[2048,1024]{1,0:T(8,128)S(1)} %get-tuple-element.38.scaled_ref, bf16[1024,512]{1,0:T(8,128)(2,1)S(1)} %get-tuple-element.39.slab_ref, f32[8,8,128]{2,1,0:T(8,128)S(1)} %collective-permute-done.6.other_before_ref, ...), custom_call_target="tpu_custom_call" | custom-call | flops 2147483648 | bytes 12582912 | tf_op jit(solution)/shard_map/pallas_call | solution.py:318
  108.4 2.5 %shard_map.40 = (f32[2048,512]{1,0:T(8,128)S(1)}, f32[16,128]{1,0:T(8,128)S(1)}) custom-call(f32[8,8,128]{2,1,0:T(8,128)S(1)} %collective-permute-done.7.received_ref, f32[2048,1024]{1,0:T(8,128)S(1)} %get-tuple-element.42.scaled_ref, bf16[1024,512]{1,0:T(8,128)(2,1)S(1)} %collective-permute-done.9.slab_ref, f32[2048,512]{1,0:T(8,128)S(1)} %get-tuple-element.44.earlier_ref), custom_call_target="tpu_custom_call" | custom-call | flops 2147483648 | bytes 16777216 | tf_op jit(solution)/shard_map/pallas_call | solution.py:356
  111.0 1.2 %collective-permute-done.10.theirs_ref = f32[16,128]{1,0:T(8,128)S(1)} collective-permute-done((f32[16,128]{1,0:T(8,128)S(1)}, f32[16,128]{1,0:T(8,128)S(1)}, u32[]{:S(2)}, u32[]{:S(2)}) %collective-permute-start.10) | collective-permute-done | bytes 8224 | tf_op jit(solution)/shard_map/ppermute | solution.py:446
  112.2 2.2 %shard_map.41 = f32[2048,512]{1,0:T(8,128)} custom-call(f32[2048,512]{1,0:T(8,128)S(1)} %get-tuple-element.45.numerators_ref, f32[16,128]{1,0:T(8,128)S(1)} %get-tuple-element.46.mine_ref, f32[16,128]{1,0:T(8,128)S(1)} %collective-permute-done.10.theirs_ref), custom_call_target="tpu_custom_call" | custom-call | flops 1048576 | bytes 8388608 | tf_op jit(solution)/shard_map/pallas_call | solution.py:391
  (20 shorter events, 4.1 us)
Async XLA Ops:
  1.1 8.9 %collective-permute-start = (bf16[64,1024]{1,0:T(8,128)(2,1)S(1)}, bf16[64,1024]{1,0:T(8,128)(2,1)S(1)}, u32[]{:S(2)}, u32[]{:S(2)}) collective-permute-start(bf16[64,1024]{1,0:T(8,128)(2,1)S(1)} %shard_map.28.share_ref), channel_id=1, source_target_pairs={{64,0},{96,32},{0,64},{32,96},{65,1},{97,33},{1,65},{33,97},{66,2}... | collective-permute-start | bytes 393224 | tf_op jit(solution)/shard_map/ppermute | solution.py:433
  4.9 1.2 %copy-start = (f32[256,1024]{1,0:T(8,128)S(1)}, f32[256,1024]{1,0:T(8,128)}, u32[]{:S(2)}) copy-start(f32[256,1024]{1,0:T(8,128)} %values_ref.3) | copy-start | bytes 3145732
  10.0 14.0 %collective-permute-start.4 = (bf16[256,1024]{1,0:T(8,128)(2,1)S(1)}, bf16[256,1024]{1,0:T(8,128)(2,1)S(1)}, u32[]{:S(2)}, u32[]{:S(2)}) collective-permute-start(bf16[256,1024]{1,0:T(8,128)(2,1)S(1)} %shard_map.29.vectors_ref.refs_0_), channel_id=1, source_target_pairs={{32,0},{64,32},{96,64},{0,96},{33,1},{65,33},{97,65},{1,97},{34,2}... | collective-permute-start | bytes 1572872 | tf_op jit(solution)/shard_map/ppermute | solution.py:433
  10.8 13.1 %collective-permute-start.5 = (bf16[256,1024]{1,0:T(8,128)(2,1)S(1)}, bf16[256,1024]{1,0:T(8,128)(2,1)S(1)}, u32[]{:S(2)}, u32[]{:S(2)}) collective-permute-start(bf16[256,1024]{1,0:T(8,128)(2,1)S(1)} %shard_map.29.vectors_ref.refs_0_), channel_id=1, source_target_pairs={{96,0},{0,32},{32,64},{64,96},{97,1},{1,33},{33,65},{65,97},{98,2}... | collective-permute-start | bytes 1572872 | tf_op jit(solution)/shard_map/ppermute | solution.py:433
  11.5 4.9 %collective-permute-start.1 = (bf16[64,1024]{1,0:T(8,128)(2,1)S(1)}, bf16[64,1024]{1,0:T(8,128)(2,1)S(1)}, u32[]{:S(2)}, u32[]{:S(2)}) collective-permute-start(bf16[64,1024]{1,0:T(8,128)(2,1)S(1)} %collective-permute-done.refs_0_), channel_id=1, source_target_pairs={{8,0},{16,8},{24,16},{0,24},{9,1},{17,9},{25,17},{1,25},{10,2},{18... | collective-permute-start | bytes 393224 | tf_op jit(solution)/shard_map/ppermute | solution.py:433
  14.0 5.4 %collective-permute-start.2 = (bf16[64,1024]{1,0:T(8,128)(2,1)S(1)}, bf16[64,1024]{1,0:T(8,128)(2,1)S(1)}, u32[]{:S(2)}, u32[]{:S(2)}) collective-permute-start(bf16[64,1024]{1,0:T(8,128)(2,1)S(1)} %collective-permute-done.refs_0_), channel_id=1, source_target_pairs={{16,0},{24,8},{0,16},{8,24},{17,1},{25,9},{1,17},{9,25},{18,2},{26... | collective-permute-start | bytes 393224 | tf_op jit(solution)/shard_map/ppermute | solution.py:433
  14.5 8.1 %collective-permute-start.3 = (bf16[64,1024]{1,0:T(8,128)(2,1)S(1)}, bf16[64,1024]{1,0:T(8,128)(2,1)S(1)}, u32[]{:S(2)}, u32[]{:S(2)}) collective-permute-start(bf16[64,1024]{1,0:T(8,128)(2,1)S(1)} %collective-permute-done.refs_0_), channel_id=1, source_target_pairs={{24,0},{0,8},{8,16},{16,24},{25,1},{1,9},{9,17},{17,25},{26,2},{2,... | collective-permute-start | bytes 393224 | tf_op jit(solution)/shard_map/ppermute | solution.py:433
  53.6 50.5 %collective-permute-start.8 = (f32[2048,1024]{1,0:T(8,128)}, f32[2048,1024]{1,0:T(8,128)S(1)}, u32[]{:S(2)}, u32[]{:S(2)}) collective-permute-start(f32[2048,1024]{1,0:T(8,128)} %get-tuple-element.41), channel_id=1, source_target_pairs={{0,128},{128,0},{1,129},{129,1},{2,130},{130,2},{3,131},{131,3},{4... | collective-permute-start | bytes 25165832 | tf_op jit(solution)/shard_map/ppermute | solution.py:446
  58.7 49.7 %collective-permute-start.9 = (bf16[1024,512]{1,0:T(8,128)(2,1)S(1)}, bf16[1024,512]{1,0:T(8,128)(2,1)S(1)}, u32[]{:S(2)}, u32[]{:S(2)}) collective-permute-start(bf16[1024,512]{1,0:T(8,128)(2,1)S(1)} %get-tuple-element.43), channel_id=1, source_target_pairs={{0,128},{128,0},{1,129},{129,1},{2,130},{130,2},{3,131},{131,3},{4... | collective-permute-start | bytes 3145736 | tf_op jit(solution)/shard_map/ppermute | solution.py:446
  78.5 4.4 %collective-permute-start.6 = (f32[8,8,128]{2,1,0:T(8,128)S(1)}, f32[8,8,128]{2,1,0:T(8,128)S(1)}, u32[]{:S(2)}, u32[]{:S(2)}) collective-permute-start(f32[8,8,128]{2,1,0:T(8,128)S(1)} %all_to_all.33.received_ref), channel_id=1, source_target_pairs={{0,128},{128,0},{1,129},{129,1},{2,130},{130,2},{3,131},{131,3},{4... | collective-permute-start | bytes 98312 | tf_op jit(solution)/shard_map/ppermute | solution.py:446
  101.5 6.8 %collective-permute-start.7 = (f32[8,8,128]{2,1,0:T(8,128)S(1)}, f32[8,8,128]{2,1,0:T(8,128)S(1)}, u32[]{:S(2)}, u32[]{:S(2)}) collective-permute-start(f32[8,8,128]{2,1,0:T(8,128)S(1)} %all_to_all.35.received_ref), channel_id=1, source_target_pairs={{0,128},{128,0},{1,129},{129,1},{2,130},{130,2},{3,131},{131,3},{4... | collective-permute-start | bytes 98312 | tf_op jit(solution)/shard_map/ppermute | solution.py:446
  110.9 1.2 %collective-permute-start.10 = (f32[16,128]{1,0:T(8,128)S(1)}, f32[16,128]{1,0:T(8,128)S(1)}, u32[]{:S(2)}, u32[]{:S(2)}) collective-permute-start(f32[16,128]{1,0:T(8,128)S(1)} %get-tuple-element.46.mine_ref), channel_id=1, source_target_pairs={{0,128},{128,0},{1,129},{129,1},{2,130},{130,2},{3,131},{131,3},{4... | collective-permute-start | bytes 24584 | tf_op jit(solution)/shard_map/ppermute | solution.py:446

commit v7 on v5

--- a/solution.py
+++ b/solution.py
@@ -17,7 +17,7 @@
 GROUP_ROWS = 8
 CHUNK = 256
 LONG = 512
-TILE = 64
+TILE = 32
 VMEM_LIMIT = 20 * 1024 * 1024
 F32 = jnp.float32
 BF16 = jnp.bfloat16

time: 115 us -> 115 us (level)
  no operation moved by 1% of the time
where the time goes in v7:
time: 115 us
  blocking collectives  62.7 us (55%)
  Pallas kernels  23.3 us (20%)
  starting transfers between devices  19.8 us (17%)
  waiting for transfers between devices  7.37 us (6%)
  local copies, waits for them, and re-layouts  1.22 us (1%)
    all_to_all x6, blocking collectives, exchange(): return lax.all_to_all(copies, axes, 0, 0, tiled=True)  62.7 us
    ppermute x5, starting transfers between devices, body(): swapped = lambda x: lax.ppermute(x, 'replica', [(0, 1), (1, 0)])  10.8 us
    ppermute x6, starting transfers between devices, body(): lax.ppermute(x, axis, [((i + hop) % size, i) for i in range(size)])  8.98 us
    ppermute x6, waiting for transfers between devices, body(): lax.ppermute(x, axis, [((i + hop) % size, i) for i in range(size)])  6.2 us
    pallas_call x1, Pallas kernels, first_sweep(): pl.pallas_call(functools.partial(first_kernel, hops, lists_total), out_sh...  4.42 us
    pallas_call x1, Pallas kernels, own_update(): pl.pallas_call(functools.partial(own_update_kernel, hops, lists_total), o...  4.25 us
    pallas_call x1, Pallas kernels, unit_lists(): pl.pallas_call(centroids_kernel, out_shape=jax.ShapeDtypeStruct((lists, w...  3.64 us
    pallas_call x1, Pallas kernels, other_update(): pl.pallas_call(functools.partial(other_update_kernel, hops, lists_total),...  2.53 us
  transfers between devices with their start and end apart: 11, of which 3 were waited for; matrix products, arithmetic and copies ran while one was open for 0% of the time, Pallas kernels for 11%

profile of v7, /device:TPU:1, one launch (start us, length us, event | category | flops | bytes accessed | tf_op | source)
XLA Modules:
  0.0 114.7 jit_solution(14909037702557241702)
XLA Ops:
  1.1 3.8 %collective-permute-start = (bf16[64,1024]{1,0:T(8,128)(2,1)S(1)}, bf16[64,1024]{1,0:T(8,128)(2,1)S(1)}, u32[]{:S(2)}, u32[]{:S(2)}) collective-permute-start(bf16[64,1024]{1,0:T(8,128)(2,1)S(1)} %shard_map.28.share_ref), channel_id=1, source_target_pairs={{64,0},{96,32},{0,64},{32,96},{65,1},{97,33},{1,65},{33,97},{66,2}... | collective-permute-start | bytes 393224 | tf_op jit(solution)/shard_map/ppermute | solution.py:434
  4.9 1.2 %copy-done = f32[256,1024]{1,0:T(8,128)S(1)} copy-done((f32[256,1024]{1,0:T(8,128)S(1)}, f32[256,1024]{1,0:T(8,128)}, u32[]{:S(2)}) %copy-start) | copy-done | bytes 1048600
  6.3 3.6 %shard_map.30.centroids_ref = bf16[2048,1024]{1,0:T(8,128)(2,1)S(1)} custom-call(f32[2048,1024]{1,0:T(8,128)} %centroids_ref.1), custom_call_target="tpu_custom_call" | custom-call | flops 8388608 | bytes 12582912 | tf_op jit(solution)/shard_map/pallas_call | solution.py:100
  11.5 2.5 %collective-permute-start.1 = (bf16[64,1024]{1,0:T(8,128)(2,1)S(1)}, bf16[64,1024]{1,0:T(8,128)(2,1)S(1)}, u32[]{:S(2)}, u32[]{:S(2)}) collective-permute-start(bf16[64,1024]{1,0:T(8,128)(2,1)S(1)} %collective-permute-done.refs_0_), channel_id=1, source_target_pairs={{8,0},{16,8},{24,16},{0,24},{9,1},{17,9},{25,17},{1,25},{10,2},{18... | collective-permute-start | bytes 393224 | tf_op jit(solution)/shard_map/ppermute | solution.py:434
  15.1 1.3 %shard_map.31.own_ref = f32[2048,256]{1,0:T(8,128)S(1)} custom-call(bf16[2048,1024]{1,0:T(8,128)(2,1)S(1)} %shard_map.30.centroids_ref, bf16[256,1024]{1,0:T(8,128)(2,1)S(1)} %shard_map.29.vectors_ref.refs_0_), custom_call_target="tpu_custom_call" | custom-call | flops 1073741824 | bytes 8388608 | tf_op jit(solution)/shard_map/pallas_call | solution.py:178
  16.4 3.0 %collective-permute-done.2.refs_2_ = bf16[64,1024]{1,0:T(8,128)(2,1)S(1)} collective-permute-done((bf16[64,1024]{1,0:T(8,128)(2,1)S(1)}, bf16[64,1024]{1,0:T(8,128)(2,1)S(1)}, u32[]{:S(2)}, u32[]{:S(2)}) %collective-permute-start.2) | collective-permute-done | bytes 131104 | tf_op jit(solution)/shard_map/ppermute | solution.py:434
  19.4 3.2 %collective-permute-done.3.refs_3_ = bf16[64,1024]{1,0:T(8,128)(2,1)S(1)} collective-permute-done((bf16[64,1024]{1,0:T(8,128)(2,1)S(1)}, bf16[64,1024]{1,0:T(8,128)(2,1)S(1)}, u32[]{:S(2)}, u32[]{:S(2)}) %collective-permute-start.3) | collective-permute-done | bytes 131104 | tf_op jit(solution)/shard_map/ppermute | solution.py:434
  22.6 1.3 %shard_map.32 = (bf16[256,1024]{1,0:T(8,128)(2,1)S(1)}, f32[2048,256]{1,0:T(8,128)S(1)}) custom-call(bf16[2048,1024]{1,0:T(8,128)(2,1)S(1)} %shard_map.30.centroids_ref, bf16[64,1024]{1,0:T(8,128)(2,1)S(1)} %collective-permute-done.refs_0_, bf16[64,1024]{1,0:T(8,128)(2,1)S(1)} %collective-permute-done.1.refs_1_, ...), custom_call_target="tpu_custom_call" | custom-call | flops 1073741824 | bytes 8388608 | tf_op jit(solution)/shard_map/pallas_call | solution.py:191
  24.0 4.4 %shard_map.33 = (f32[2048,1024]{1,0:T(8,128)S(1)}, f32[2048,1024]{1,0:T(8,128)}, bf16[1024,512]{1,0:T(8,128)(2,1)S(1)}, bf16[1024,512]{1,0:T(8,128)(2,1)S(1)}, f32[16,8,128]{2,1,0:T(8,128)S(1)}) custom-call(bf16[2048,1024]{1,0:T(8,128)(2,1)S(1)} %shard_map.30.centroids_ref, f32[2048,256]{1,0:T(8,128)S(1)} %shard_map.31.own_ref, ...), custom_call_target="tpu_custom_call" | custom-call | flops 2147483648 | bytes 12582912 | tf_op jit(solution)/shard_map/pallas_call | solution.py:234
  28.4 10.6 %all_to_all.30.received_ref = f32[16,8,128]{2,1,0:T(8,128)S(1)} all-to-all(f32[16,8,128]{2,1,0:T(8,128)S(1)} %get-tuple-element.31), channel_id=1, replica_groups=mesh['replica'=2,'dp'=4,'cx'=4,'cz'=8] {'dp','cx'}, dimensions={0} | all-to-all | bytes 131072 | tf_op jit(solution)/shard_map/all_to_all | solution.py:407
  39.0 14.9 %all_to_all.31.received_ref = f32[8,8,128]{2,1,0:T(8,128)S(1)} all-to-all(f32[8,8,128]{2,1,0:T(8,128)S(1)} %shard_map.34), channel_id=1, replica_groups=mesh['replica'=2,'dp'=4,'cx'=4,'cz'=8] {'cz'}, dimensions={0} | all-to-all | bytes 65536 | tf_op jit(solution)/shard_map/all_to_all | solution.py:407
  53.9 5.1 %collective-permute-start.8 = (f32[2048,1024]{1,0:T(8,128)}, f32[2048,1024]{1,0:T(8,128)S(1)}, u32[]{:S(2)}, u32[]{:S(2)}) collective-permute-start(f32[2048,1024]{1,0:T(8,128)} %get-tuple-element.41), channel_id=1, source_target_pairs={{0,128},{128,0},{1,129},{129,1},{2,130},{130,2},{3,131},{131,3},{4... | collective-permute-start | bytes 25165832 | tf_op jit(solution)/shard_map/ppermute | solution.py:447
  58.9 1.2 %shard_map.35 = f32[16,8,128]{2,1,0:T(8,128)S(1)} custom-call(f32[8,8,128]{2,1,0:T(8,128)S(1)} %all_to_all.31.received_ref, f32[2048,1024]{1,0:T(8,128)S(1)} %get-tuple-element.35.kt_ref), custom_call_target="tpu_custom_call" | custom-call | flops 8388608 | bytes 8388608 | tf_op jit(solution)/shard_map/pallas_call | solution.py:273
  60.1 9.4 %all_to_all.32.received_ref = f32[16,8,128]{2,1,0:T(8,128)S(1)} all-to-all(f32[16,8,128]{2,1,0:T(8,128)S(1)} %shard_map.35), channel_id=1, replica_groups=mesh['replica'=2,'dp'=4,'cx'=4,'cz'=8] {'dp','cx'}, dimensions={0} | all-to-all | bytes 131072 | tf_op jit(solution)/shard_map/all_to_all | solution.py:407
  69.5 9.2 %all_to_all.33.received_ref = f32[8,8,128]{2,1,0:T(8,128)S(1)} all-to-all(f32[8,8,128]{2,1,0:T(8,128)S(1)} %shard_map.36), channel_id=1, replica_groups=mesh['replica'=2,'dp'=4,'cx'=4,'cz'=8] {'cz'}, dimensions={0} | all-to-all | bytes 65536 | tf_op jit(solution)/shard_map/all_to_all | solution.py:407
  78.7 3.1 %collective-permute-start.6 = (f32[8,8,128]{2,1,0:T(8,128)S(1)}, f32[8,8,128]{2,1,0:T(8,128)S(1)}, u32[]{:S(2)}, u32[]{:S(2)}) collective-permute-start(f32[8,8,128]{2,1,0:T(8,128)S(1)} %all_to_all.33.received_ref), channel_id=1, source_target_pairs={{0,128},{128,0},{1,129},{129,1},{2,130},{130,2},{3,131},{131,3},{4... | collective-permute-start | bytes 98312 | tf_op jit(solution)/shard_map/ppermute | solution.py:447
  81.8 1.2 %shard_map.37 = (f32[16,8,128]{2,1,0:T(8,128)S(1)}, f32[2048,1024]{1,0:T(8,128)S(1)}) custom-call(f32[8,8,128]{2,1,0:T(8,128)S(1)} %all_to_all.33.received_ref, f32[2048,1024]{1,0:T(8,128)S(1)} %get-tuple-element.35.kt_ref), custom_call_target="tpu_custom_call" | custom-call | flops 8388608 | bytes 8388608 | tf_op jit(solution)/shard_map/pallas_call | solution.py:273
  83.1 9.4 %all_to_all.34.received_ref = f32[16,8,128]{2,1,0:T(8,128)S(1)} all-to-all(f32[16,8,128]{2,1,0:T(8,128)S(1)} %get-tuple-element.37), channel_id=1, replica_groups=mesh['replica'=2,'dp'=4,'cx'=4,'cz'=8] {'dp','cx'}, dimensions={0} | all-to-all | bytes 131072 | tf_op jit(solution)/shard_map/all_to_all | solution.py:407
  92.5 9.2 %all_to_all.35.received_ref = f32[8,8,128]{2,1,0:T(8,128)S(1)} all-to-all(f32[8,8,128]{2,1,0:T(8,128)S(1)} %shard_map.38), channel_id=1, replica_groups=mesh['replica'=2,'dp'=4,'cx'=4,'cz'=8] {'cz'}, dimensions={0} | all-to-all | bytes 65536 | tf_op jit(solution)/shard_map/all_to_all | solution.py:407
  101.7 2.6 %collective-permute-start.7 = (f32[8,8,128]{2,1,0:T(8,128)S(1)}, f32[8,8,128]{2,1,0:T(8,128)S(1)}, u32[]{:S(2)}, u32[]{:S(2)}) collective-permute-start(f32[8,8,128]{2,1,0:T(8,128)S(1)} %all_to_all.35.received_ref), channel_id=1, source_target_pairs={{0,128},{128,0},{1,129},{129,1},{2,130},{130,2},{3,131},{131,3},{4... | collective-permute-start | bytes 98312 | tf_op jit(solution)/shard_map/ppermute | solution.py:447
  104.3 4.2 %shard_map.39 = (f32[2048,512]{1,0:T(8,128)S(1)}, f32[2048,1024]{1,0:T(8,128)S(1)}) custom-call(f32[8,8,128]{2,1,0:T(8,128)S(1)} %all_to_all.35.received_ref, f32[2048,1024]{1,0:T(8,128)S(1)} %get-tuple-element.38.scaled_ref, bf16[1024,512]{1,0:T(8,128)(2,1)S(1)} %get-tuple-element.39.slab_ref, f32[8,8,128]{2,1,0:T(8,128)S(1)} %collective-permute-done.6.other_before_ref, ...), custom_call_target="tpu_custom_call" | custom-call | flops 2147483648 | bytes 12582912 | tf_op jit(solution)/shard_map/pallas_call | solution.py:319
  108.6 2.5 %shard_map.40 = (f32[2048,512]{1,0:T(8,128)S(1)}, f32[16,128]{1,0:T(8,128)S(1)}) custom-call(f32[8,8,128]{2,1,0:T(8,128)S(1)} %collective-permute-done.7.received_ref, f32[2048,1024]{1,0:T(8,128)S(1)} %get-tuple-element.42.scaled_ref, bf16[1024,512]{1,0:T(8,128)(2,1)S(1)} %collective-permute-done.9.slab_ref, f32[2048,512]{1,0:T(8,128)S(1)} %get-tuple-element.44.earlier_ref), custom_call_target="tpu_custom_call" | custom-call | flops 2147483648 | bytes 16777216 | tf_op jit(solution)/shard_map/pallas_call | solution.py:357
  111.2 1.2 %collective-permute-done.10.theirs_ref = f32[16,128]{1,0:T(8,128)S(1)} collective-permute-done((f32[16,128]{1,0:T(8,128)S(1)}, f32[16,128]{1,0:T(8,128)S(1)}, u32[]{:S(2)}, u32[]{:S(2)}) %collective-permute-start.10) | collective-permute-done | bytes 8224 | tf_op jit(solution)/shard_map/ppermute | solution.py:447
  112.3 2.2 %shard_map.41 = f32[2048,512]{1,0:T(8,128)} custom-call(f32[2048,512]{1,0:T(8,128)S(1)} %get-tuple-element.45.numerators_ref, f32[16,128]{1,0:T(8,128)S(1)} %get-tuple-element.46.mine_ref, f32[16,128]{1,0:T(8,128)S(1)} %collective-permute-done.10.theirs_ref), custom_call_target="tpu_custom_call" | custom-call | flops 1048576 | bytes 8388608 | tf_op jit(solution)/shard_map/pallas_call | solution.py:392
  (20 shorter events, 4.1 us)
Async XLA Ops:
  1.1 8.9 %collective-permute-start = (bf16[64,1024]{1,0:T(8,128)(2,1)S(1)}, bf16[64,1024]{1,0:T(8,128)(2,1)S(1)}, u32[]{:S(2)}, u32[]{:S(2)}) collective-permute-start(bf16[64,1024]{1,0:T(8,128)(2,1)S(1)} %shard_map.28.share_ref), channel_id=1, source_target_pairs={{64,0},{96,32},{0,64},{32,96},{65,1},{97,33},{1,65},{33,97},{66,2}... | collective-permute-start | bytes 393224 | tf_op jit(solution)/shard_map/ppermute | solution.py:434
  4.9 1.2 %copy-start = (f32[256,1024]{1,0:T(8,128)S(1)}, f32[256,1024]{1,0:T(8,128)}, u32[]{:S(2)}) copy-start(f32[256,1024]{1,0:T(8,128)} %values_ref.3) | copy-start | bytes 3145732
  10.0 14.0 %collective-permute-start.4 = (bf16[256,1024]{1,0:T(8,128)(2,1)S(1)}, bf16[256,1024]{1,0:T(8,128)(2,1)S(1)}, u32[]{:S(2)}, u32[]{:S(2)}) collective-permute-start(bf16[256,1024]{1,0:T(8,128)(2,1)S(1)} %shard_map.29.vectors_ref.refs_0_), channel_id=1, source_target_pairs={{32,0},{64,32},{96,64},{0,96},{33,1},{65,33},{97,65},{1,97},{34,2}... | collective-permute-start | bytes 1572872 | tf_op jit(solution)/shard_map/ppermute | solution.py:434
  10.8 13.1 %collective-permute-start.5 = (bf16[256,1024]{1,0:T(8,128)(2,1)S(1)}, bf16[256,1024]{1,0:T(8,128)(2,1)S(1)}, u32[]{:S(2)}, u32[]{:S(2)}) collective-permute-start(bf16[256,1024]{1,0:T(8,128)(2,1)S(1)} %shard_map.29.vectors_ref.refs_0_), channel_id=1, source_target_pairs={{96,0},{0,32},{32,64},{64,96},{97,1},{1,33},{33,65},{65,97},{98,2}... | collective-permute-start | bytes 1572872 | tf_op jit(solution)/shard_map/ppermute | solution.py:434
  11.5 4.9 %collective-permute-start.1 = (bf16[64,1024]{1,0:T(8,128)(2,1)S(1)}, bf16[64,1024]{1,0:T(8,128)(2,1)S(1)}, u32[]{:S(2)}, u32[]{:S(2)}) collective-permute-start(bf16[64,1024]{1,0:T(8,128)(2,1)S(1)} %collective-permute-done.refs_0_), channel_id=1, source_target_pairs={{8,0},{16,8},{24,16},{0,24},{9,1},{17,9},{25,17},{1,25},{10,2},{18... | collective-permute-start | bytes 393224 | tf_op jit(solution)/shard_map/ppermute | solution.py:434
  14.0 5.4 %collective-permute-start.2 = (bf16[64,1024]{1,0:T(8,128)(2,1)S(1)}, bf16[64,1024]{1,0:T(8,128)(2,1)S(1)}, u32[]{:S(2)}, u32[]{:S(2)}) collective-permute-start(bf16[64,1024]{1,0:T(8,128)(2,1)S(1)} %collective-permute-done.refs_0_), channel_id=1, source_target_pairs={{16,0},{24,8},{0,16},{8,24},{17,1},{25,9},{1,17},{9,25},{18,2},{26... | collective-permute-start | bytes 393224 | tf_op jit(solution)/shard_map/ppermute | solution.py:434
  14.5 8.1 %collective-permute-start.3 = (bf16[64,1024]{1,0:T(8,128)(2,1)S(1)}, bf16[64,1024]{1,0:T(8,128)(2,1)S(1)}, u32[]{:S(2)}, u32[]{:S(2)}) collective-permute-start(bf16[64,1024]{1,0:T(8,128)(2,1)S(1)} %collective-permute-done.refs_0_), channel_id=1, source_target_pairs={{24,0},{0,8},{8,16},{16,24},{25,1},{1,9},{9,17},{17,25},{26,2},{2,... | collective-permute-start | bytes 393224 | tf_op jit(solution)/shard_map/ppermute | solution.py:434
  53.9 50.4 %collective-permute-start.8 = (f32[2048,1024]{1,0:T(8,128)}, f32[2048,1024]{1,0:T(8,128)S(1)}, u32[]{:S(2)}, u32[]{:S(2)}) collective-permute-start(f32[2048,1024]{1,0:T(8,128)} %get-tuple-element.41), channel_id=1, source_target_pairs={{0,128},{128,0},{1,129},{129,1},{2,130},{130,2},{3,131},{131,3},{4... | collective-permute-start | bytes 25165832 | tf_op jit(solution)/shard_map/ppermute | solution.py:447
  58.9 49.6 %collective-permute-start.9 = (bf16[1024,512]{1,0:T(8,128)(2,1)S(1)}, bf16[1024,512]{1,0:T(8,128)(2,1)S(1)}, u32[]{:S(2)}, u32[]{:S(2)}) collective-permute-start(bf16[1024,512]{1,0:T(8,128)(2,1)S(1)} %get-tuple-element.43), channel_id=1, source_target_pairs={{0,128},{128,0},{1,129},{129,1},{2,130},{130,2},{3,131},{131,3},{4... | collective-permute-start | bytes 3145736 | tf_op jit(solution)/shard_map/ppermute | solution.py:447
  78.7 4.3 %collective-permute-start.6 = (f32[8,8,128]{2,1,0:T(8,128)S(1)}, f32[8,8,128]{2,1,0:T(8,128)S(1)}, u32[]{:S(2)}, u32[]{:S(2)}) collective-permute-start(f32[8,8,128]{2,1,0:T(8,128)S(1)} %all_to_all.33.received_ref), channel_id=1, source_target_pairs={{0,128},{128,0},{1,129},{129,1},{2,130},{130,2},{3,131},{131,3},{4... | collective-permute-start | bytes 98312 | tf_op jit(solution)/shard_map/ppermute | solution.py:447
  101.7 6.8 %collective-permute-start.7 = (f32[8,8,128]{2,1,0:T(8,128)S(1)}, f32[8,8,128]{2,1,0:T(8,128)S(1)}, u32[]{:S(2)}, u32[]{:S(2)}) collective-permute-start(f32[8,8,128]{2,1,0:T(8,128)S(1)} %all_to_all.35.received_ref), channel_id=1, source_target_pairs={{0,128},{128,0},{1,129},{129,1},{2,130},{130,2},{3,131},{131,3},{4... | collective-permute-start | bytes 98312 | tf_op jit(solution)/shard_map/ppermute | solution.py:447
  111.1 1.2 %collective-permute-start.10 = (f32[16,128]{1,0:T(8,128)S(1)}, f32[16,128]{1,0:T(8,128)S(1)}, u32[]{:S(2)}, u32[]{:S(2)}) collective-permute-start(f32[16,128]{1,0:T(8,128)S(1)} %get-tuple-element.46.mine_ref), channel_id=1, source_target_pairs={{0,128},{128,0},{1,129},{129,1},{2,130},{130,2},{3,131},{131,3},{4... | collective-permute-start | bytes 24584 | tf_op jit(solution)/shard_map/ppermute | solution.py:447
